TPU v7x, 256 devices: a whole 4x4x8 slice. The times are simulated.
256 devices in a mesh: fsdp: 16 (over y_lo, z), ctx: 16 (over x, y_hi, core).
Axes of the slice: x: 4, y: 4 (y_hi: 2, y_lo: 2; y = y_hi * 2 + y_lo), z: 8, core: 2. Of those that a mesh axis runs over, the one named last changes fastest.
Arguments:
- tokens: bfloat16 [32768, 8192], P('ctx', 'fsdp'), may hold values from -6 to 6
- in_proj: bfloat16 [3, 8192, 1024], P(None, 'fsdp', 'ctx'), may hold values from -0.09375 to 0.09375
- filter_taps: float32 [1024, 32768], P('fsdp', 'ctx'), may hold values from -0.7 to 0.7
- skip_gain: float32 [1024], P('fsdp'), may hold values from -4 to 4
- out_proj: bfloat16 [1024, 8192], P('ctx', 'fsdp'), may hold values from -0.1875 to 0.1875
Outputs:
- projected: bfloat16 [32768, 8192], P('ctx', 'fsdp')
All inputs are finite; a program needn't handle non-finite values.
Results may differ from a plain program's by a relative error of at most 0.038.
Values may be sent and summed in bfloat16 or wider, within the bound.
No kernel may reach another device: no remote copies, remote signals or barrier semaphores. Data moves between devices by JAX's collectives and lax.ppermute only.
A program may use at most 128 MiB of HBM per device.

v0:
```python
import math

import jax
import jax.numpy as jnp
import numpy as np
from jax import lax
from jax.experimental import pallas as pl
from jax.experimental.pallas import tpu as pltpu
from jax.sharding import PartitionSpec as P

AXES = ("fsdp", "ctx")
RINGS = 8
SEQ = 32768
ROWS = 128
COLS = 256
F32 = jnp.float32
BF16 = jnp.bfloat16


def flip(array, mask):
    return lax.ppermute(array, AXES, [(i, i ^ mask) for i in range(256)])


FLIP_CORE = 1
FLIP_Y_HI = 2
FLIP_X = 4
FLIP_Y_LO = 128


def along_z(array, step):
    pairs = []
    for i in range(256):
        z = (i // 16) % RINGS
        pairs.append((i, i + 16 * ((z + step) % RINGS - z)))
    return lax.ppermute(array, AXES, pairs)


def plane_groups():
    return [
        [(y_lo * RINGS + z) * 16 + ctx for ctx in range(16) for y_lo in range(2)]
        for z in range(RINGS)
    ]


def transform_tables():
    freq = np.arange(ROWS)[:, None] + 0.25
    row_angle = 2.0 * np.pi * freq * np.arange(ROWS)[None, :] / ROWS
    twiddle_angle = 2.0 * np.pi * freq * np.arange(COLS)[None, :] / SEQ
    col_angle = 2.0 * np.pi * (np.arange(COLS)[:, None] * np.arange(COLS)[None, :] % COLS) / COLS
    cos_col, sin_col = np.cos(col_angle), np.sin(col_angle)
    row_forward = np.concatenate([np.cos(row_angle), -np.sin(row_angle)], axis=0)
    row_inverse = np.concatenate([np.cos(row_angle), -np.sin(row_angle)], axis=0).T / SEQ
    col_forward = np.block([[cos_col, -sin_col], [sin_col, cos_col]])
    col_inverse = np.block([[cos_col, sin_col], [-sin_col, cos_col]])
    twiddle = np.stack([np.cos(twiddle_angle), -np.sin(twiddle_angle)])
    return row_forward, row_inverse, col_forward, col_inverse, twiddle


def row_order(sources):
    per_source = ROWS // sources
    return (np.arange(sources)[None, :] * per_source + np.arange(per_source)[:, None]).reshape(-1)


def dot32(left, right):
    return jnp.dot(left, right, preferred_element_type=F32)


def forward(signal_ref, row_table, col_table, twiddle_ref):
    channels, sources, _ = signal_ref.shape
    per_source = ROWS // sources
    cos_part, sin_part = twiddle_ref[0], twiddle_ref[1]
    turned = []
    for channel in range(channels):
        signal = jnp.concatenate(
            [signal_ref[channel, :, pl.ds(j * COLS, COLS)] for j in range(per_source)], axis=0
        )
        both = dot32(row_table[...], signal)
        real, imag = both[:ROWS], both[ROWS:]
        turned.append(
            jnp.concatenate(
                [
                    (real * cos_part - imag * sin_part).astype(BF16),
                    (real * sin_part + imag * cos_part).astype(BF16),
                ],
                axis=1,
            )
        )
    return dot32(jnp.concatenate(turned, axis=0), col_table[...])


def filter_kernel(taps_ref, row_table, col_table, twiddle_ref, out_ref):
    out_ref[...] = forward(taps_ref, row_table, col_table, twiddle_ref)


def conv_kernel(
    signal_ref, spectrum_ref, row_table, col_table, col_back, row_back, twiddle_ref, out_ref
):
    channels, sources, _ = signal_ref.shape
    per_source = ROWS // sources
    spectrum = forward(signal_ref, row_table, col_table, twiddle_ref)
    real, imag = spectrum[:, :COLS], spectrum[:, COLS:]
    filter_real, filter_imag = spectrum_ref[:, :COLS], spectrum_ref[:, COLS:]
    product = jnp.concatenate(
        [
            (real * filter_real - imag * filter_imag).astype(BF16),
            (real * filter_imag + imag * filter_real).astype(BF16),
        ],
        axis=1,
    )
    back = dot32(product, col_back[...])
    cos_part, sin_part = twiddle_ref[0], twiddle_ref[1]
    for channel in range(channels):
        part = back[channel * ROWS : (channel + 1) * ROWS]
        real, imag = part[:, :COLS], part[:, COLS:]
        turned = jnp.concatenate(
            [
                (real * cos_part + imag * sin_part).astype(BF16),
                (imag * cos_part - real * sin_part).astype(BF16),
            ],
            axis=0,
        )
        result = dot32(row_back[...], turned).astype(BF16)
        for j in range(per_source):
            out_ref[channel, :, pl.ds(j * COLS, COLS)] = result[j * sources : (j + 1) * sources]


def call_local(kernel, out_shape, *operands):
    vmem = pl.BlockSpec(memory_space=pltpu.VMEM)
    return pl.pallas_call(
        kernel,
        out_shape=out_shape,
        in_specs=[vmem] * len(operands),
        out_specs=vmem,
        compiler_params=pltpu.CompilerParams(vmem_limit_bytes=24 * 1024 * 1024),
    )(*operands)


def x_groups():
    return [
        [fsdp * 16 + x * 4 + rest for x in range(4)] for fsdp in range(16) for rest in range(4)
    ]


def z_groups():
    return [list(range(first, first + RINGS)) for first in (0, RINGS)]


def after(array, *others):
    return lax.optimization_barrier((array,) + others)[0]


def gather_y(shard, y_hi):
    own = jnp.concatenate([shard, flip(shard, FLIP_Y_LO)], axis=-1)
    other = jnp.concatenate(
        [flip(shard, FLIP_Y_HI), flip(shard, FLIP_Y_HI | FLIP_Y_LO)], axis=-1
    )
    return jnp.where(y_hi == 0, jnp.stack([own, other]), jnp.stack([other, own]))


def gather_x(column):
    copies = jnp.broadcast_to(column[None], (4,) + column.shape)
    return lax.all_to_all(
        copies, AXES, split_axis=0, concat_axis=0, tiled=True, axis_index_groups=x_groups()
    )


def gather_core(plane, core):
    other = flip(plane, FLIP_CORE)
    both = jnp.where(core == 0, jnp.stack([plane, other], 2), jnp.stack([other, plane], 2))
    both = both.reshape((2, 2) + both.shape[1:])
    both = both.transpose((1, 2, 3, 0) + tuple(range(4, both.ndim)))
    return both.reshape((RINGS, 2) + both.shape[4:])


def reduce_over_z(parts):
    return lax.psum_scatter(
        parts, "fsdp", scatter_dimension=0, tiled=True, axis_index_groups=z_groups()
    )


def times_tokens(weights, wide_tokens):
    return lax.dot_general(
        weights.reshape(-1, 1024),
        wide_tokens,
        (((1,), (1,)), ((), ())),
        preferred_element_type=F32,
    ).astype(BF16)


def local(tokens, in_proj, filter_taps, skip_gain, out_proj):
    fsdp = lax.axis_index("fsdp")
    ctx = lax.axis_index("ctx")
    y_lo, z, y_hi, core = fsdp // RINGS, fsdp % RINGS, ctx // 2 % 2, ctx % 2
    groups = plane_groups()
    row_forward, row_inverse, col_forward, col_inverse, twiddle = transform_tables()
    as_bf16 = lambda table: jnp.asarray(table.astype(np.float32)).astype(BF16)
    twiddle = jnp.asarray(twiddle.astype(np.float32))
    half = tokens.shape[0] // 2

    shards = in_proj.transpose(0, 2, 1)
    given = lax.dynamic_slice_in_dim(tokens, (1 - y_lo) * half, half, 0)
    column = after(gather_y(shards[1:3], y_hi), given)

    plane = gather_x(column)
    got = flip(given, FLIP_Y_LO)
    other_gain = flip(skip_gain, FLIP_Y_LO)
    plane, got, other_gain, query_shard, out_proj = lax.optimization_barrier(
        (plane, got, other_gain, shards[0], out_proj)
    )
    gain = jnp.where(
        y_lo == 0, jnp.stack([skip_gain, other_gain]), jnp.stack([other_gain, skip_gain])
    )
    query_column = gather_y(query_shard, y_hi)
    out_other = flip(out_proj, FLIP_Y_HI)
    out_column = jnp.where(
        y_hi == 0, jnp.stack([out_proj, out_other]), jnp.stack([out_other, out_proj])
    )
    late = jnp.concatenate([query_column, out_column.reshape(2, 32, 1024)], axis=1)

    weights = gather_core(plane, core)
    kept = lax.dynamic_slice_in_dim(tokens, y_lo * half, half, 0)
    wide_tokens = jnp.concatenate([kept, got], axis=1)
    parts = times_tokens(weights, wide_tokens)
    sums = reduce_over_z(parts)

    late = gather_x(after(late, parts))
    late = gather_core(late, core)
    query_parts = times_tokens(late[:, :, :64], wide_tokens)
    query = reduce_over_z(query_parts)

    taps = after(filter_taps.astype(BF16), parts)
    taps = lax.all_to_all(
        taps.reshape(16, 4, 2048), "ctx", split_axis=0, concat_axis=0, tiled=True
    ).transpose(1, 0, 2)
    spectrum = call_local(
        filter_kernel,
        jax.ShapeDtypeStruct((4 * ROWS, 2 * COLS), F32),
        taps,
        as_bf16(row_forward[:, row_order(16)]),
        as_bf16(col_forward),
        twiddle,
    )
    sums, query_parts, spectrum = lax.optimization_barrier((sums, query_parts, spectrum))
    sums = sums.reshape(2, 2, 64, half).astype(F32)
    mixed = sums[:, 0] * sums[:, 1]

    def to_plane(array):
        return lax.all_to_all(
            array, AXES, split_axis=0, concat_axis=0, tiled=True, axis_index_groups=groups
        )

    spread = mixed.astype(BF16).reshape(2, 16, 4, half).transpose(1, 0, 2, 3).reshape(32, 4, half)
    spread = to_plane(spread).transpose(1, 0, 2)
    convolved = call_local(
        conv_kernel,
        jax.ShapeDtypeStruct(spread.shape, BF16),
        spread,
        spectrum,
        as_bf16(row_forward[:, row_order(32)]),
        as_bf16(col_forward),
        as_bf16(col_inverse),
        as_bf16(row_inverse[row_order(32)]),
        twiddle,
    )
    convolved = to_plane(convolved.transpose(1, 0, 2))
    convolved = convolved.reshape(16, 2, 4, half).transpose(1, 0, 2, 3).reshape(2, 64, half)

    query = query.reshape(2, 64, half).astype(F32)
    gated = (query * (convolved.astype(F32) + gain[:, :, None] * mixed)).astype(BF16)

    gated = gated.reshape(128, half)
    out_rows = late[:, :, 64:].reshape(1024, 512)

    def project(values):
        return lax.dot_general(
            values, out_rows, (((0,), (0,)), ((), ())), preferred_element_type=F32
        ).astype(BF16)

    gathered = lax.all_gather(
        gated, "fsdp", axis=0, tiled=True, axis_index_groups=z_groups()
    )
    up = down = flip(gated, FLIP_Y_LO)
    other_rows = jnp.zeros((1024, half), BF16)

    def put(array, piece, offset, row=0):
        return lax.dynamic_update_slice_in_dim(
            array, piece, (z + offset) % RINGS * 128 + row, 0
        )

    other_rows = put(other_rows, up, 0)
    for distance in (1, 2, 3):
        up, down = along_z(up, 1), along_z(down, -1)
        other_rows = put(put(other_rows, up, -distance), down, distance)
    up, down = along_z(up[:64], 1), along_z(down[64:], -1)
    other_rows = put(put(other_rows, up, -4), down, 4, 64)
    both = jnp.stack([project(gathered), project(other_rows)])
    return jnp.where(y_lo == 0, both, both[::-1]).reshape(2 * half, 512)


def solution(mesh):
    placed = (
        P("ctx", "fsdp"),
        P(None, "fsdp", "ctx"),
        P("fsdp", "ctx"),
        P("fsdp"),
        P("ctx", "fsdp"),
    )
    return jax.shard_map(
        local, mesh=mesh, in_specs=placed, out_specs=P("ctx", "fsdp"), check_vma=False
    )
```

profile of v0, /device:TPU:2, one launch (start us, length us, event | category | flops | bytes accessed | tf_op | source)
XLA Modules:
  0.0 235.0 jit_solution(14203742068820596643)
XLA Ops:
  7.5 3.1 %collective-permute-start.2 = (bf16[2,64,512]{2,1,0:T(8,128)(2,1)S(1)}, bf16[2,64,512]{2,1,0:T(8,128)(2,1)S(1)}, u32[]{:S(2)}, u32[]{:S(2)}) collective-permute-start(bf16[2,64,512]{2,1,0:T(8,128)(2,1)S(1)} %slice.32), channel_id=1, source_target_pairs={{0,130},{1,131},{2,128},{3,129},{4,134},{5,135},{6,132},{7,133},{8... | collective-permute-start | bytes 393224 | tf_op jit(solution)/shard_map/ppermute | solution.py:21
  14.3 3.3 %collective-permute-done = bf16[2,64,512]{2,1,0:T(8,128)(2,1)S(1)} collective-permute-done((bf16[2,64,512]{2,1,0:T(8,128)(2,1)S(1)}, bf16[2,64,512]{2,1,0:T(8,128)(2,1)S(1)}, u32[]{:S(2)}, u32[]{:S(2)}) %collective-permute-start) | collective-permute-done | bytes 131104 | tf_op jit(solution)/shard_map/ppermute | solution.py:21
  20.1 5.0 %all-to-all-start = ((bf16[4,2,2,64,1024]{4,3,2,1,0:T(8,128)(2,1)}), bf16[4,2,2,64,1024]{4,3,2,1,0:T(8,128)(2,1)S(1)}, u32[]{:S(2)}, u32[]{:S(2)}) async-start(bf16[4,2,2,64,1024]{4,3,2,1,0:T(8,128)(2,1)} %broadcast_in_dim.6), calls=%async_computation | async-start | bytes 4194304 | tf_op jit(solution)/shard_map/all_to_all | solution.py:162
  28.0 20.0 %collective-permute-done.4 = f32[64]{0:T(128)S(1)} collective-permute-done((f32[64]{0:T(128)S(1)}, f32[64]{0:T(128)S(1)}, u32[]{:S(2)}, u32[]{:S(2)}) %collective-permute-start.4) | collective-permute-done | bytes 288 | tf_op jit(solution)/shard_map/ppermute | solution.py:21
  48.2 4.3 %collective-permute-done.9 = bf16[4,2,2,64,1024]{4,3,2,1,0:T(8,128)(2,1)} collective-permute-done((bf16[4,2,2,64,1024]{4,3,2,1,0:T(8,128)(2,1)S(1)}, bf16[4,2,2,64,1024]{4,3,2,1,0:T(8,128)(2,1)}, u32[]{:S(2)}, u32[]{:S(2)}) %collective-permute-start.9) | collective-permute-done | bytes 2097184 | tf_op jit(solution)/shard_map/ppermute | solution.py:21
  52.5 2.9 %fusion = bf16[2,2,2,2,2,64,1024]{6,5,4,1,0,3,2:T(8,128)(2,1)S(1)} fusion(bf16[2,2,2,1,2,64,1024]{6,5,4,2,1,0,3:T(8,128)(2,1)} %bitcast.7, bf16[2,2,2,1,2,64,1024]{6,5,4,2,1,0,3:T(8,128)(2,1)S(1)} %bitcast.67, pred[]{:T(512)S(6)} %eq.27), kind=kLoop, calls=%fused_computation.1 | loop fusion | flops 6291456 | bytes 8388609 | tf_op jit(solution)/shard_map/transpose | solution.py:171
  56.1 7.3 %convolution_convert_fusion = bf16[2048,1024]{1,0:T(8,128)(2,1)} fusion(bf16[2048,1024]{1,0:T(8,128)(2,1)S(1)} %bitcast.69, bf16[1024,512]{1,0:T(8,128)(2,1)} %collective-permute-done.3, bf16[1024,512]{1,0:T(8,128)(2,1)S(1)} %get-tuple-element.27), kind=kOutput, calls=%fused_computation.2 | convolution fusion | flops 4301258752 | bytes 10485760 | tf_op jit(solution)/shard_map/dot_general | solution.py:182
  71.4 3.2 %collective-permute-done.5 = bf16[64,512]{1,0:T(8,128)(2,1)S(1)} collective-permute-done((bf16[64,512]{1,0:T(8,128)(2,1)S(1)}, bf16[64,512]{1,0:T(8,128)(2,1)S(1)}, u32[]{:S(2)}, u32[]{:S(2)}) %collective-permute-start.5) | collective-permute-done | bytes 65568 | tf_op jit(solution)/shard_map/ppermute | solution.py:21
  74.9 22.4 %all_to_all.25 = bf16[4,2,96,1024]{3,2,1,0:T(8,128)(2,1)S(1)} all-to-all(bf16[4,2,96,1024]{3,2,1,0:T(8,128)(2,1)S(1)} %broadcast_in_dim.7), channel_id=1, replica_groups={{0,4,8,12},{1,5,9,13},{2,6,10,14},{3,7,11,15},{16,20,24,28},{17,21,25,2..., dimensions={0} | all-to-all | bytes 3145728 | tf_op jit(solution)/shard_map/all_to_all | solution.py:162
  97.2 3.4 %collective-permute-done.10 = bf16[4,2,96,1024]{3,2,1,0:T(8,128)(2,1)S(1)} collective-permute-done((bf16[4,2,96,1024]{3,2,1,0:T(8,128)(2,1)S(1)}, bf16[4,2,96,1024]{3,2,1,0:T(8,128)(2,1)S(1)}, u32[]{:S(2)}, u32[]{:S(2)}) %collective-permute-start.10) | collective-permute-done | bytes 1572896 | tf_op jit(solution)/shard_map/ppermute | solution.py:21
  103.2 4.9 %convolution_convert_fusion.1 = bf16[1024,1024]{1,0:T(8,128)(2,1)} fusion(bf16[1024,1024]{1,0:T(8,128)(2,1)S(1)} %bitcast.70, bf16[1024,512]{1,0:T(8,128)(2,1)} %collective-permute-done.3, bf16[1024,512]{1,0:T(8,128)(2,1)S(1)} %get-tuple-element.27), kind=kOutput, calls=%fused_computation.8 | convolution fusion | flops 2152726528 | bytes 6291456 | tf_op jit(solution)/shard_map/dot_general | solution.py:182
  109.4 11.9 %all_to_all.26 = bf16[16,4,2048]{2,1,0:T(4,128)(2,1)S(1)} all-to-all(bf16[16,4,2048]{2,1,0:T(4,128)(2,1)S(1)} %reshape.100), channel_id=1, replica_groups=mesh['fsdp'=16,'ctx'=16] {'ctx'}, dimensions={0} | all-to-all | bytes 524288 | tf_op jit(solution)/shard_map/all_to_all | solution.py:232
  124.3 13.8 %all_to_all.27 = bf16[32,4,1024]{2,1,0:T(4,128)(2,1)S(1)} all-to-all(bf16[32,4,1024]{2,1,0:T(4,128)(2,1)S(1)} %bitcast.75), channel_id=1, replica_groups={{0,128,1,129,2,130,3,131,4,132,5,133,6,134,7,135,8,136,9,137,10,138,11,..., dimensions={0} | all-to-all | bytes 524288 | tf_op jit(solution)/shard_map/all_to_all | solution.py:248
  140.2 5.3 %all-to-all-start.4 = ((bf16[32,4,1024]{2,1,0:T(4,128)(2,1)}), bf16[32,4,1024]{2,1,0:T(4,128)(2,1)S(1)}, u32[]{:S(2)}, u32[]{:S(2)}) async-start(bf16[32,4,1024]{2,1,0:T(4,128)(2,1)} %copy.51), calls=%async_computation.6 | async-start | bytes 524288 | tf_op jit(solution)/shard_map/all_to_all | solution.py:248
  145.9 7.0 %all-to-all-done.4 = bf16[32,4,1024]{2,1,0:T(4,128)(2,1)S(1)} async-done(((bf16[32,4,1024]{2,1,0:T(4,128)(2,1)}), bf16[32,4,1024]{2,1,0:T(4,128)(2,1)S(1)}, u32[]{:S(2)}, u32[]{:S(2)}) %all-to-all-start.4) | async-done | bytes 262176 | tf_op jit(solution)/shard_map/all_to_all | solution.py:248
  153.2 11.4 %reduce-scatter.3.cloned.1.call-done = bf16[128,1024]{1,0:T(8,128)(2,1)} async-done(((bf16[1024,1024]{1,0:T(8,128)(2,1)}), bf16[128,1024]{1,0:T(8,128)(2,1)}) %reduce-scatter.3.cloned.1.call-update) | async-done | bytes 262160 | tf_op jit(solution)/shard_map/reduce_scatter | solution.py:176
  168.1 5.0 %collective-permute-done.11 = bf16[128,1024]{1,0:T(8,128)(2,1)S(1)} collective-permute-done((bf16[128,1024]{1,0:T(8,128)(2,1)}, bf16[128,1024]{1,0:T(8,128)(2,1)S(1)}, u32[]{:S(2)}, u32[]{:S(2)}) %collective-permute-start.11) | collective-permute-done | bytes 262176 | tf_op jit(solution)/shard_map/ppermute | solution.py:21
  175.1 9.8 %collective-permute-done.13 = bf16[128,1024]{1,0:T(8,128)(2,1)S(1)} collective-permute-done((bf16[128,1024]{1,0:T(8,128)(2,1)S(1)}, bf16[128,1024]{1,0:T(8,128)(2,1)S(1)}, u32[]{:S(2)}, u32[]{:S(2)}) %collective-permute-start.13) | collective-permute-done | bytes 262176 | tf_op jit(solution)/shard_map/ppermute | solution.py:35
  184.9 3.1 %collective-permute-start.15 = (bf16[128,1024]{1,0:T(8,128)(2,1)S(1)}, bf16[128,1024]{1,0:T(8,128)(2,1)S(1)}, u32[]{:S(2)}, u32[]{:S(2)}) collective-permute-start(bf16[128,1024]{1,0:T(8,128)(2,1)S(1)} %collective-permute-done.13), channel_id=1, source_target_pairs={{0,112},{1,113},{2,114},{3,115},{4,116},{5,117},{6,118},{7,119},{8... | collective-permute-start | bytes 786440 | tf_op jit(solution)/shard_map/ppermute | solution.py:35
  191.0 8.3 %collective-permute-done.15 = bf16[128,1024]{1,0:T(8,128)(2,1)S(1)} collective-permute-done((bf16[128,1024]{1,0:T(8,128)(2,1)S(1)}, bf16[128,1024]{1,0:T(8,128)(2,1)S(1)}, u32[]{:S(2)}, u32[]{:S(2)}) %collective-permute-start.15) | collective-permute-done | bytes 262176 | tf_op jit(solution)/shard_map/ppermute | solution.py:35
  199.3 3.7 %collective-permute-start.17 = (bf16[128,1024]{1,0:T(8,128)(2,1)S(1)}, bf16[128,1024]{1,0:T(8,128)(2,1)S(1)}, u32[]{:S(2)}, u32[]{:S(2)}) collective-permute-start(bf16[128,1024]{1,0:T(8,128)(2,1)S(1)} %collective-permute-done.15), channel_id=1, source_target_pairs={{0,112},{1,113},{2,114},{3,115},{4,116},{5,117},{6,118},{7,119},{8... | collective-permute-start | bytes 786440 | tf_op jit(solution)/shard_map/ppermute | solution.py:35
  204.4 8.3 %collective-permute-done.17 = bf16[128,1024]{1,0:T(8,128)(2,1)S(1)} collective-permute-done((bf16[128,1024]{1,0:T(8,128)(2,1)S(1)}, bf16[128,1024]{1,0:T(8,128)(2,1)S(1)}, u32[]{:S(2)}, u32[]{:S(2)}) %collective-permute-start.17) | collective-permute-done | bytes 262176 | tf_op jit(solution)/shard_map/ppermute | solution.py:35
  212.7 3.3 %collective-permute-start.19 = (bf16[64,1024]{1,0:T(8,128)(2,1)S(1)}, bf16[64,1024]{1,0:T(8,128)(2,1)S(1)}, u32[]{:S(2)}, u32[]{:S(2)}) collective-permute-start(bf16[64,1024]{1,0:T(8,128)(2,1)S(1)} %slice.39), channel_id=1, source_target_pairs={{0,112},{1,113},{2,114},{3,115},{4,116},{5,117},{6,118},{7,119},{8... | collective-permute-start | bytes 393224 | tf_op jit(solution)/shard_map/ppermute | solution.py:35
  216.2 6.1 %collective-permute-done.18 = bf16[64,1024]{1,0:T(8,128)(2,1)S(1)} collective-permute-done((bf16[64,1024]{1,0:T(8,128)(2,1)S(1)}, bf16[64,1024]{1,0:T(8,128)(2,1)S(1)}, u32[]{:S(2)}, u32[]{:S(2)}) %collective-permute-start.18) | collective-permute-done | bytes 131104 | tf_op jit(solution)/shard_map/ppermute | solution.py:35
  (108 shorter events, 44.6 us)
Async XLA Ops:
  7.5 10.2 %collective-permute-start.2 = (bf16[2,64,512]{2,1,0:T(8,128)(2,1)S(1)}, bf16[2,64,512]{2,1,0:T(8,128)(2,1)S(1)}, u32[]{:S(2)}, u32[]{:S(2)}) collective-permute-start(bf16[2,64,512]{2,1,0:T(8,128)(2,1)S(1)} %slice.32), channel_id=1, source_target_pairs={{0,130},{1,131},{2,128},{3,129},{4,134},{5,135},{6,132},{7,133},{8... | collective-permute-start | bytes 393224 | tf_op jit(solution)/shard_map/ppermute | solution.py:21
  10.6 7.9 %collective-permute-start.1 = (bf16[2,64,512]{2,1,0:T(8,128)(2,1)S(1)}, bf16[2,64,512]{2,1,0:T(8,128)(2,1)S(1)}, u32[]{:S(2)}, u32[]{:S(2)}) collective-permute-start(bf16[2,64,512]{2,1,0:T(8,128)(2,1)S(1)} %slice.32), channel_id=1, source_target_pairs={{0,2},{1,3},{2,0},{3,1},{4,6},{5,7},{6,4},{7,5},{8,10},{9,11},{10,... | collective-permute-start | bytes 393224 | tf_op jit(solution)/shard_map/ppermute | solution.py:21
  11.2 6.4 %collective-permute-start = (bf16[2,64,512]{2,1,0:T(8,128)(2,1)S(1)}, bf16[2,64,512]{2,1,0:T(8,128)(2,1)S(1)}, u32[]{:S(2)}, u32[]{:S(2)}) collective-permute-start(bf16[2,64,512]{2,1,0:T(8,128)(2,1)S(1)} %slice.32), channel_id=1, source_target_pairs={{0,128},{1,129},{2,130},{3,131},{4,132},{5,133},{6,134},{7,135},{8... | collective-permute-start | bytes 393224 | tf_op jit(solution)/shard_map/ppermute | solution.py:21
  20.1 28.1 %all-to-all-start = ((bf16[4,2,2,64,1024]{4,3,2,1,0:T(8,128)(2,1)}), bf16[4,2,2,64,1024]{4,3,2,1,0:T(8,128)(2,1)S(1)}, u32[]{:S(2)}, u32[]{:S(2)}) async-start(bf16[4,2,2,64,1024]{4,3,2,1,0:T(8,128)(2,1)} %broadcast_in_dim.6), calls=%async_computation | async-start | bytes 4194304 | tf_op jit(solution)/shard_map/all_to_all | solution.py:162
  25.1 97.1 %reduce-scatter.5.cloned.1.call-start = ((), (), s32[]{:S(2)}) async-start(), calls=%async_computation.8 | async-start | bytes 4718592 | tf_op jit(solution)/shard_map/reduce_scatter | solution.py:176
  25.1 22.9 %collective-permute-start.3 = (bf16[1024,512]{1,0:T(8,128)(2,1)}, bf16[1024,512]{1,0:T(8,128)(2,1)}, u32[]{:S(2)}, u32[]{:S(2)}) collective-permute-start(bf16[1024,512]{1,0:T(8,128)(2,1)} %get-tuple-element.28), channel_id=1, source_target_pairs={{0,128},{1,129},{2,130},{3,131},{4,132},{5,133},{6,134},{7,135},{8... | collective-permute-start | bytes 3145736 | tf_op jit(solution)/shard_map/ppermute | solution.py:21
  25.7 22.3 %collective-permute-start.4 = (f32[64]{0:T(128)S(1)}, f32[64]{0:T(128)S(1)}, u32[]{:S(2)}, u32[]{:S(2)}) collective-permute-start(f32[64]{0:T(128)S(1)} %copy-done.9), channel_id=1, source_target_pairs={{0,128},{1,129},{2,130},{3,131},{4,132},{5,133},{6,134},{7,135},{8... | collective-permute-start | bytes 776 | tf_op jit(solution)/shard_map/ppermute | solution.py:21
  48.2 4.3 %collective-permute-start.9 = (bf16[4,2,2,64,1024]{4,3,2,1,0:T(8,128)(2,1)S(1)}, bf16[4,2,2,64,1024]{4,3,2,1,0:T(8,128)(2,1)}, u32[]{:S(2)}, u32[]{:S(2)}) collective-permute-start(bf16[4,2,2,64,1024]{4,3,2,1,0:T(8,128)(2,1)S(1)} %all-to-all-done), channel_id=1, source_target_pairs={{0,1},{1,0},{2,3},{3,2},{4,5},{5,4},{6,7},{7,6},{8,9},{9,8},{10,11... | collective-permute-start | bytes 6291464 | tf_op jit(solution)/shard_map/ppermute | solution.py:21
  63.5 101.1 %reduce-scatter.3.cloned.1.call-start = ((), (), s32[]{:S(2)}) async-start(), calls=%async_computation.7 | async-start | bytes 2359296 | tf_op jit(solution)/shard_map/reduce_scatter | solution.py:176
  64.3 7.0 %collective-permute-start.8 = (bf16[64,512]{1,0:T(8,128)(2,1)S(1)}, bf16[64,512]{1,0:T(8,128)(2,1)S(1)}, u32[]{:S(2)}, u32[]{:S(2)}) collective-permute-start(bf16[64,512]{1,0:T(8,128)(2,1)S(1)} %copy-done.8), channel_id=1, source_target_pairs={{0,2},{1,3},{2,0},{3,1},{4,6},{5,7},{6,4},{7,5},{8,10},{9,11},{10,... | collective-permute-start | bytes 196616 | tf_op jit(solution)/shard_map/ppermute | solution.py:21
  67.1 7.5 %collective-permute-start.7 = (bf16[64,512]{1,0:T(8,128)(2,1)S(1)}, bf16[64,512]{1,0:T(8,128)(2,1)S(1)}, u32[]{:S(2)}, u32[]{:S(2)}) collective-permute-start(bf16[64,512]{1,0:T(8,128)(2,1)S(1)} %slice_bitcast_fusion), channel_id=1, source_target_pairs={{0,130},{1,131},{2,128},{3,129},{4,134},{5,135},{6,132},{7,133},{8... | collective-permute-start | bytes 196616 | tf_op jit(solution)/shard_map/ppermute | solution.py:21
  68.3 6.2 %collective-permute-start.6 = (bf16[64,512]{1,0:T(8,128)(2,1)S(1)}, bf16[64,512]{1,0:T(8,128)(2,1)S(1)}, u32[]{:S(2)}, u32[]{:S(2)}) collective-permute-start(bf16[64,512]{1,0:T(8,128)(2,1)S(1)} %slice_bitcast_fusion), channel_id=1, source_target_pairs={{0,2},{1,3},{2,0},{3,1},{4,6},{5,7},{6,4},{7,5},{8,10},{9,11},{10,... | collective-permute-start | bytes 196616 | tf_op jit(solution)/shard_map/ppermute | solution.py:21
  70.3 4.3 %collective-permute-start.5 = (bf16[64,512]{1,0:T(8,128)(2,1)S(1)}, bf16[64,512]{1,0:T(8,128)(2,1)S(1)}, u32[]{:S(2)}, u32[]{:S(2)}) collective-permute-start(bf16[64,512]{1,0:T(8,128)(2,1)S(1)} %slice_bitcast_fusion), channel_id=1, source_target_pairs={{0,128},{1,129},{2,130},{3,131},{4,132},{5,133},{6,134},{7,135},{8... | collective-permute-start | bytes 196616 | tf_op jit(solution)/shard_map/ppermute | solution.py:21
  140.2 12.7 %all-to-all-start.4 = ((bf16[32,4,1024]{2,1,0:T(4,128)(2,1)}), bf16[32,4,1024]{2,1,0:T(4,128)(2,1)S(1)}, u32[]{:S(2)}, u32[]{:S(2)}) async-start(bf16[32,4,1024]{2,1,0:T(4,128)(2,1)} %copy.51), calls=%async_computation.6 | async-start | bytes 524288 | tf_op jit(solution)/shard_map/all_to_all | solution.py:248
  145.6 78.1 %all-gather.2.cloned.1.call-start = ((), (), s32[]{:S(2)}) async-start(), calls=%async_computation.9 | async-start | bytes 2359296 | tf_op jit(solution)/shard_map/all_gather | solution.py:279
  166.4 6.7 %collective-permute-start.11 = (bf16[128,1024]{1,0:T(8,128)(2,1)}, bf16[128,1024]{1,0:T(8,128)(2,1)S(1)}, u32[]{:S(2)}, u32[]{:S(2)}) collective-permute-start(bf16[128,1024]{1,0:T(8,128)(2,1)} %fusion.6), channel_id=1, source_target_pairs={{0,128},{1,129},{2,130},{3,131},{4,132},{5,133},{6,134},{7,135},{8... | collective-permute-start | bytes 786440 | tf_op jit(solution)/shard_map/ppermute | solution.py:21
  173.1 11.8 %collective-permute-start.13 = (bf16[128,1024]{1,0:T(8,128)(2,1)S(1)}, bf16[128,1024]{1,0:T(8,128)(2,1)S(1)}, u32[]{:S(2)}, u32[]{:S(2)}) collective-permute-start(bf16[128,1024]{1,0:T(8,128)(2,1)S(1)} %collective-permute-done.11), channel_id=1, source_target_pairs={{0,112},{1,113},{2,114},{3,115},{4,116},{5,117},{6,118},{7,119},{8... | collective-permute-start | bytes 786440 | tf_op jit(solution)/shard_map/ppermute | solution.py:35
  174.5 14.4 %collective-permute-start.12 = (bf16[128,1024]{1,0:T(8,128)(2,1)S(1)}, bf16[128,1024]{1,0:T(8,128)(2,1)S(1)}, u32[]{:S(2)}, u32[]{:S(2)}) collective-permute-start(bf16[128,1024]{1,0:T(8,128)(2,1)S(1)} %collective-permute-done.11), channel_id=1, source_target_pairs={{0,16},{1,17},{2,18},{3,19},{4,20},{5,21},{6,22},{7,23},{8,24},{9,... | collective-permute-start | bytes 786440 | tf_op jit(solution)/shard_map/ppermute | solution.py:35
  184.9 14.4 %collective-permute-start.15 = (bf16[128,1024]{1,0:T(8,128)(2,1)S(1)}, bf16[128,1024]{1,0:T(8,128)(2,1)S(1)}, u32[]{:S(2)}, u32[]{:S(2)}) collective-permute-start(bf16[128,1024]{1,0:T(8,128)(2,1)S(1)} %collective-permute-done.13), channel_id=1, source_target_pairs={{0,112},{1,113},{2,114},{3,115},{4,116},{5,117},{6,118},{7,119},{8... | collective-permute-start | bytes 786440 | tf_op jit(solution)/shard_map/ppermute | solution.py:35
  188.9 15.4 %collective-permute-start.14 = (bf16[128,1024]{1,0:T(8,128)(2,1)S(1)}, bf16[128,1024]{1,0:T(8,128)(2,1)S(1)}, u32[]{:S(2)}, u32[]{:S(2)}) collective-permute-start(bf16[128,1024]{1,0:T(8,128)(2,1)S(1)} %collective-permute-done.12), channel_id=1, source_target_pairs={{0,16},{1,17},{2,18},{3,19},{4,20},{5,21},{6,22},{7,23},{8,24},{9,... | collective-permute-start | bytes 786440 | tf_op jit(solution)/shard_map/ppermute | solution.py:35
  199.3 13.4 %collective-permute-start.17 = (bf16[128,1024]{1,0:T(8,128)(2,1)S(1)}, bf16[128,1024]{1,0:T(8,128)(2,1)S(1)}, u32[]{:S(2)}, u32[]{:S(2)}) collective-permute-start(bf16[128,1024]{1,0:T(8,128)(2,1)S(1)} %collective-permute-done.15), channel_id=1, source_target_pairs={{0,112},{1,113},{2,114},{3,115},{4,116},{5,117},{6,118},{7,119},{8... | collective-permute-start | bytes 786440 | tf_op jit(solution)/shard_map/ppermute | solution.py:35
  204.3 11.7 %collective-permute-start.16 = (bf16[128,1024]{1,0:T(8,128)(2,1)S(1)}, bf16[128,1024]{1,0:T(8,128)(2,1)S(1)}, u32[]{:S(2)}, u32[]{:S(2)}) collective-permute-start(bf16[128,1024]{1,0:T(8,128)(2,1)S(1)} %collective-permute-done.14), channel_id=1, source_target_pairs={{0,16},{1,17},{2,18},{3,19},{4,20},{5,21},{6,22},{7,23},{8,24},{9,... | collective-permute-start | bytes 786440 | tf_op jit(solution)/shard_map/ppermute | solution.py:35
  212.7 9.6 %collective-permute-start.19 = (bf16[64,1024]{1,0:T(8,128)(2,1)S(1)}, bf16[64,1024]{1,0:T(8,128)(2,1)S(1)}, u32[]{:S(2)}, u32[]{:S(2)}) collective-permute-start(bf16[64,1024]{1,0:T(8,128)(2,1)S(1)} %slice.39), channel_id=1, source_target_pairs={{0,112},{1,113},{2,114},{3,115},{4,116},{5,117},{6,118},{7,119},{8... | collective-permute-start | bytes 393224 | tf_op jit(solution)/shard_map/ppermute | solution.py:35
  216.0 6.3 %collective-permute-start.18 = (bf16[64,1024]{1,0:T(8,128)(2,1)S(1)}, bf16[64,1024]{1,0:T(8,128)(2,1)S(1)}, u32[]{:S(2)}, u32[]{:S(2)}) collective-permute-start(bf16[64,1024]{1,0:T(8,128)(2,1)S(1)} %slice.38), channel_id=1, source_target_pairs={{0,16},{1,17},{2,18},{3,19},{4,20},{5,21},{6,22},{7,23},{8,24},{9,... | collective-permute-start | bytes 393224 | tf_op jit(solution)/shard_map/ppermute | solution.py:35
  (11 other events, 96.8 us)
Sparse Core Ops, SparseCore 0:
  63.6 57.7 reduce-scatter.4
  123.9 40.5 reduce-scatter.2
  166.6 47.5 all-gather.1
where the time goes:
time: 236 us; the launch traced here: 235 us
  waiting for transfers between devices  93.5 us (40%)
  blocking collectives  48 us (20%)
  starting transfers between devices  37.4 us (16%)
  matrix products  16.4 us (7%)
  local copies, waits for them, and re-layouts  15.9 us (7%)
  between operations  13.6 us (6%)
  other arithmetic  8.31 us (4%)
    ppermute x12, waiting for transfers between devices, flip(): return lax.ppermute(array, AXES, [(i, i ^ mask) for i in range(256)])  40 us
    ppermute x8, waiting for transfers between devices, along_z(): return lax.ppermute(array, AXES, pairs)  34.7 us
    all_to_all x1, blocking collectives, gather_x(): lax.all_to_all(copies, AXES, split_axis=0, concat_axis=0, tiled=True, axi...  22.4 us
    ppermute x12, starting transfers between devices, flip(): return lax.ppermute(array, AXES, [(i, i ^ mask) for i in range(256)])  14.8 us
    all_to_all x1, blocking collectives, to_plane(): lax.all_to_all(array, AXES, split_axis=0, concat_axis=0, tiled=True, axis...  13.8 us
    dot_general x2, matrix products, times_tokens(): lax.dot_general(weights.reshape(-1, 1024), wide_tokens, (((1,), (1,)), ((...  12.3 us
    ppermute x8, starting transfers between devices, along_z(): return lax.ppermute(array, AXES, pairs)  12.2 us
    all_to_all x1, blocking collectives, local(): lax.all_to_all(taps.reshape(16, 4, 2048), 'ctx', split_axis=0, concat_axi...  11.9 us
  transfers between devices with their start and end apart: 25, of which 16 were waited for; matrix products, arithmetic and copies ran while one was open for 7% of the time, Pallas kernels for 1%

commit v1 on v0

--- a/solution.py
+++ b/solution.py
@@ -164,27 +164,102 @@
     )
 
 
-def gather_core(plane, core):
+def product_kernel(core_ref, weights_ref, kept_ref, got_ref, *rest):
+    del core_ref
+    out_ref = rest[-1]
+    width = kept_ref.shape[1]
+    rows = weights_ref.shape[3]
+    left = weights_ref[:, 0].reshape(4 * rows, 2 * width)
+    over = (((1,), (1,)), ((), ()))
+    sums = lax.dot_general(left[:, :width], kept_ref[...], over, preferred_element_type=F32)
+    sums += lax.dot_general(left[:, width:], got_ref[...], over, preferred_element_type=F32)
+    sums = sums.astype(BF16)
+    for x_high in range(2):
+        for y_high in range(2):
+            first = (x_high * 2 + y_high) * rows
+            out_ref[0, y_high, 0, x_high] = sums[first : first + rows]
+
+
+def product(plane, rows, kept, got, core, *started):
+    plane = plane.reshape(2, 2, 2, -1, 1024)
+    count, width = kept.shape
+    whole = pl.BlockSpec((count, width), lambda i, core: (0, 0))
+    shape = (2, 2, 2, 2, rows, count)
+    return pl.pallas_call(
+        product_kernel,
+        grid_spec=pltpu.PrefetchScalarGridSpec(
+            num_scalar_prefetch=1,
+            grid=(2,),
+            in_specs=[
+                pl.BlockSpec((2, 1, 2, rows, 1024), lambda i, core: (0, i, 0, 0, 0)),
+                whole,
+                whole,
+            ]
+            + [pl.BlockSpec(memory_space=pl.ANY)] * len(started),
+            out_specs=pl.BlockSpec(
+                (1, 2, 1, 2, rows, count), lambda i, core: (i, 0, core[0], 0, 0, 0)
+            ),
+        ),
+        out_shape=pltpu.HBM(shape, BF16),
+        input_output_aliases={4: 0} if started else {},
+        compiler_params=pltpu.CompilerParams(vmem_limit_bytes=56 * 1024 * 1024),
+        cost_estimate=pl.CostEstimate(
+            flops=16 * rows * count * 1024, bytes_accessed=8 * 2**20, transcendentals=0
+        ),
+    )(jnp.reshape(core, (1,)).astype(jnp.int32), plane, kept, got, *started)
+
+
+def products(plane, rows, kept, got, core):
     other = flip(plane, FLIP_CORE)
-    both = jnp.where(core == 0, jnp.stack([plane, other], 2), jnp.stack([other, plane], 2))
-    both = both.reshape((2, 2) + both.shape[1:])
-    both = both.transpose((1, 2, 3, 0) + tuple(range(4, both.ndim)))
-    return both.reshape((RINGS, 2) + both.shape[4:])
+    own = product(plane, rows, kept, got, core)
+    both = product(other, rows, kept, got, 1 - core, own)
+    return both.reshape(-1, kept.shape[0]), other
+
+
+def project_kernel(y_lo_ref, own_ref, other_ref, weights_ref, out_ref):
+    del y_lo_ref
+    over = (((0,), (0,)), ((), ()))
+
+    def write(values_ref):
+        out_ref[...] = lax.dot_general(
+            values_ref[...], weights_ref[...], over, preferred_element_type=F32
+        ).astype(BF16)
+
+    first = pl.program_id(0) == 0
+    pl.when(first)(lambda: write(own_ref))
+    pl.when(jnp.logical_not(first))(lambda: write(other_ref))
+
+
+def project(own, other, weights, y_lo):
+    channels, count = own.shape
+    features = weights.shape[1]
+    block = count // 2
+    return pl.pallas_call(
+        project_kernel,
+        grid_spec=pltpu.PrefetchScalarGridSpec(
+            num_scalar_prefetch=1,
+            grid=(2, 2),
+            in_specs=[
+                pl.BlockSpec((channels, block), lambda i, j, y: (0, jnp.where(i == 0, j, 1))),
+                pl.BlockSpec((channels, block), lambda i, j, y: (0, jnp.where(i == 0, 0, j))),
+                pl.BlockSpec((channels, features), lambda i, j, y: (0, 0)),
+            ],
+            out_specs=pl.BlockSpec(
+                (block, features), lambda i, j, y: (jnp.where(i == 0, y[0], 1 - y[0]) * 2 + j, 0)
+            ),
+        ),
+        out_shape=jax.ShapeDtypeStruct((2 * count, features), BF16),
+        compiler_params=pltpu.CompilerParams(vmem_limit_bytes=56 * 1024 * 1024),
+        cost_estimate=pl.CostEstimate(
+            flops=4 * channels * count * features, bytes_accessed=7 * 2**20, transcendentals=0
+        ),
+    )(jnp.reshape(y_lo, (1,)).astype(jnp.int32), own, other, weights)
 
 
 def reduce_over_z(parts):
     return lax.psum_scatter(
         parts, "fsdp", scatter_dimension=0, tiled=True, axis_index_groups=z_groups()
     )
-
-
-def times_tokens(weights, wide_tokens):
-    return lax.dot_general(
-        weights.reshape(-1, 1024),
-        wide_tokens,
-        (((1,), (1,)), ((), ())),
-        preferred_element_type=F32,
-    ).astype(BF16)
 
 
 def local(tokens, in_proj, filter_taps, skip_gain, out_proj):
@@ -217,16 +292,18 @@
     )
     late = jnp.concatenate([query_column, out_column.reshape(2, 32, 1024)], axis=1)
 
-    weights = gather_core(plane, core)
     kept = lax.dynamic_slice_in_dim(tokens, y_lo * half, half, 0)
-    wide_tokens = jnp.concatenate([kept, got], axis=1)
-    parts = times_tokens(weights, wide_tokens)
+    parts, _ = products(plane, 128, kept, got, core)
     sums = reduce_over_z(parts)
 
     late = gather_x(after(late, parts))
-    late = gather_core(late, core)
-    query_parts = times_tokens(late[:, :, :64], wide_tokens)
+    query_parts, other = products(late, 64, kept, got, core)
     query = reduce_over_z(query_parts)
+    out_own, out_other = late[:, :, 64:], other[:, :, 64:]
+    out_rows = jnp.where(
+        core == 0, jnp.stack([out_own, out_other], 2), jnp.stack([out_other, out_own], 2)
+    )
+    out_rows = out_rows.reshape(2, 2, 2, 2, 64, 512).transpose(1, 2, 3, 0, 4, 5).reshape(1024, 512)
 
     taps = after(filter_taps.astype(BF16), parts)
     taps = lax.all_to_all(
@@ -269,12 +346,6 @@
     gated = (query * (convolved.astype(F32) + gain[:, :, None] * mixed)).astype(BF16)
 
     gated = gated.reshape(128, half)
-    out_rows = late[:, :, 64:].reshape(1024, 512)
-
-    def project(values):
-        return lax.dot_general(
-            values, out_rows, (((0,), (0,)), ((), ())), preferred_element_type=F32
-        ).astype(BF16)
 
     gathered = lax.all_gather(
         gated, "fsdp", axis=0, tiled=True, axis_index_groups=z_groups()
@@ -293,8 +364,7 @@
         other_rows = put(put(other_rows, up, -distance), down, distance)
     up, down = along_z(up[:64], 1), along_z(down[64:], -1)
     other_rows = put(put(other_rows, up, -4), down, 4, 64)
-    both = jnp.stack([project(gathered), project(other_rows)])
-    return jnp.where(y_lo == 0, both, both[::-1]).reshape(2 * half, 512)
+    return project(gathered, other_rows, out_rows, y_lo)
 
 
 def solution(mesh):

time: 236 us -> 233 us (0.987)
  Pallas kernels: 1.83 us -> 27.1 us
  matrix products: 16.4 us -> 0 us
  waiting for transfers between devices: 93.5 us -> 83 us
  other arithmetic: 8.31 us -> 3.55 us
  local copies, waits for them, and re-layouts: 15.9 us -> 19.3 us
    pallas_call x0 -> x5, Pallas kernels: none -> 25.3 us  [the longest x4 18.9 us: product(): pl.pallas_call(product_kernel, grid_spec=pltpu.PrefetchScalarGridSpec(num...]
    dot_general x4 -> x0, matrix products: 16.4 us -> none  [the longest x2 12.3 us: times_tokens(): lax.dot_general(weights.reshape(-1, 1024), wide_tokens, (((1,), (1,)), ((...]
    ppermute x12, waiting for transfers between devices: 40 us -> 33.8 us  [flip(): return lax.ppermute(array, AXES, [(i, i ^ mask) for i in range(256)])]
    ppermute x8, waiting for transfers between devices: 34.7 us -> 28.7 us  [along_z(): return lax.ppermute(array, AXES, pairs)]
    unnamed x20 -> x28, local copies, waits for them, and re-layouts: 3.23 us -> 6.82 us
    transpose x2 -> x1, other arithmetic: 3.43 us -> 0.17 us  [local(): out_rows.reshape(2, 2, 2, 2, 64, 512).transpose(1, 2, 3, 0, 4, 5)]
  transfers between devices with their start and end apart: 25 -> 25, of which waited for: 16 -> 15; matrix products, arithmetic and copies ran while one was open for 7% -> 5% of each run, Pallas kernels for 1% -> 7%
where the time goes in v1:
time: 233 us; the launch traced here: 232 us
  waiting for transfers between devices  83 us (36%)
  blocking collectives  47.5 us (20%)
  starting transfers between devices  37.8 us (16%)
  Pallas kernels  27.1 us (12%)
  local copies, waits for them, and re-layouts  19.3 us (8%)
  between operations  13.6 us (6%)
  other arithmetic  3.55 us (2%)
    ppermute x12, waiting for transfers between devices, flip(): return lax.ppermute(array, AXES, [(i, i ^ mask) for i in range(256)])  33.8 us
    ppermute x8, waiting for transfers between devices, along_z(): return lax.ppermute(array, AXES, pairs)  28.7 us
    all_to_all x1, blocking collectives, gather_x(): lax.all_to_all(copies, AXES, split_axis=0, concat_axis=0, tiled=True, axi...  21.4 us
    pallas_call x4, Pallas kernels, product(): pl.pallas_call(product_kernel, grid_spec=pltpu.PrefetchScalarGridSpec(num...  18.9 us
    all_to_all x1, blocking collectives, to_plane(): lax.all_to_all(array, AXES, split_axis=0, concat_axis=0, tiled=True, axis...  14.6 us
    ppermute x12, starting transfers between devices, flip(): return lax.ppermute(array, AXES, [(i, i ^ mask) for i in range(256)])  13.9 us
    ppermute x8, starting transfers between devices, along_z(): return lax.ppermute(array, AXES, pairs)  13.4 us
    reduce_scatter x2, waiting for transfers between devices, reduce_over_z(): lax.psum_scatter(parts, 'fsdp', scatter_dimension=0, tiled=True, axis_ind...  13 us
  transfers between devices with their start and end apart: 25, of which 15 were waited for; matrix products, arithmetic and copies ran while one was open for 5% of the time, Pallas kernels for 7%

profile of v1, /device:TPU:2, one launch (start us, length us, event | category | flops | bytes accessed | tf_op | source)
XLA Modules:
  0.0 231.8 jit_solution(10145283910352810583)
XLA Ops:
  7.5 3.3 %collective-permute-start.1 = (bf16[2,64,512]{2,1,0:T(8,128)(2,1)S(1)}, bf16[2,64,512]{2,1,0:T(8,128)(2,1)S(1)}, u32[]{:S(2)}, u32[]{:S(2)}) collective-permute-start(bf16[2,64,512]{2,1,0:T(8,128)(2,1)S(1)} %slice.32), channel_id=1, source_target_pairs={{0,2},{1,3},{2,0},{3,1},{4,6},{5,7},{6,4},{7,5},{8,10},{9,11},{10,... | collective-permute-start | bytes 393224 | tf_op jit(solution)/shard_map/ppermute | solution.py:21
  11.8 3.1 %constant_dynamic-slice_fusion = (bf16[1024,512]{1,0:T(8,128)(2,1)}, bf16[1024,512]{1,0:T(8,128)(2,1)}) fusion(bf16[2048,512]{1,0:T(8,128)(2,1)} %param.12, s32[]{:T(128)S(6)} %select_n.151, s32[]{:T(128)S(6)} %select_n.147), kind=kLoop, calls=%fused_computation.28 | loop fusion | bytes 4194312 | tf_op jit(solution)/shard_map/dynamic_slice | solution.py:295
  19.2 5.1 %all-to-all-start = ((bf16[4,2,2,64,1024]{4,3,2,1,0:T(8,128)(2,1)}), bf16[4,2,2,64,1024]{4,3,2,1,0:T(8,128)(2,1)S(1)}, u32[]{:S(2)}, u32[]{:S(2)}) async-start(bf16[4,2,2,64,1024]{4,3,2,1,0:T(8,128)(2,1)} %broadcast_in_dim.6), calls=%async_computation | async-start | bytes 4194304 | tf_op jit(solution)/shard_map/all_to_all | solution.py:162
  27.1 21.9 %collective-permute-done.4 = f32[64]{0:T(128)S(1)} collective-permute-done((f32[64]{0:T(128)S(1)}, f32[64]{0:T(128)S(1)}, u32[]{:S(2)}, u32[]{:S(2)}) %collective-permute-start.4) | collective-permute-done | bytes 288 | tf_op jit(solution)/shard_map/ppermute | solution.py:21
  50.7 5.4 %shard_map.118.rest_0_ = bf16[2,2,2,2,128,1024]{5,4,3,2,1,0:T(8,128)(2,1)} custom-call(s32[1]{0:T(128)} %bitcast.9.core_ref, bf16[2,2,2,128,1024]{4,3,2,1,0:T(8,128)(2,1)} %bitcast.60, bf16[1024,512]{1,0:T(8,128)(2,1)} %get-tuple-element.27.kept_ref, bf16[1024,512]{1,0:T(8,128)(2,1)} %copy-done.6), custom_call_target="tpu_custom_call" | custom-call | flops 2147483648 | bytes 8388608 | tf_op jit(solution)/shard_map/pallas_call | solution.py:188
  56.1 5.5 %shard_map.119 = bf16[2,2,2,2,128,1024]{5,4,3,2,1,0:T(8,128)(2,1)} custom-call(s32[1]{0:T(128)} %bitcast.1.core_ref, bf16[2,2,2,128,1024]{4,3,2,1,0:T(8,128)(2,1)} %bitcast.8.weights_ref, bf16[1024,512]{1,0:T(8,128)(2,1)} %get-tuple-element.27.kept_ref, bf16[1024,512]{1,0:T(8,128)(2,1)} %copy-done.6, ...), custom_call_target="tpu_custom_call", output_to_operand_aliasing={{}: (4, {})} | custom-call | flops 2147483648 | bytes 8388608 | tf_op jit(solution)/shard_map/pallas_call | solution.py:188
  69.0 3.8 %collective-permute-done.5 = bf16[64,512]{1,0:T(8,128)(2,1)S(1)} collective-permute-done((bf16[64,512]{1,0:T(8,128)(2,1)S(1)}, bf16[64,512]{1,0:T(8,128)(2,1)S(1)}, u32[]{:S(2)}, u32[]{:S(2)}) %collective-permute-start.5) | collective-permute-done | bytes 65568 | tf_op jit(solution)/shard_map/ppermute | solution.py:21
  73.0 21.4 %all_to_all.25 = bf16[4,2,96,1024]{3,2,1,0:T(8,128)(2,1)S(1)} all-to-all(bf16[4,2,96,1024]{3,2,1,0:T(8,128)(2,1)S(1)} %broadcast_in_dim.7), channel_id=1, replica_groups={{0,4,8,12},{1,5,9,13},{2,6,10,14},{3,7,11,15},{16,20,24,28},{17,21,25,2..., dimensions={0} | all-to-all | bytes 3145728 | tf_op jit(solution)/shard_map/all_to_all | solution.py:162
  95.6 4.0 %shard_map.120.rest_0_ = bf16[2,2,2,2,64,1024]{5,4,3,2,1,0:T(8,128)(2,1)} custom-call(s32[1]{0:T(128)} %bitcast.9.core_ref, bf16[2,2,2,96,1024]{4,3,2,1,0:T(8,128)(2,1)} %bitcast.59, bf16[1024,512]{1,0:T(8,128)(2,1)} %get-tuple-element.27.kept_ref, bf16[1024,512]{1,0:T(8,128)(2,1)} %copy-done.6), custom_call_target="tpu_custom_call" | custom-call | flops 1073741824 | bytes 8388608 | tf_op jit(solution)/shard_map/pallas_call | solution.py:188
  100.8 4.0 %shard_map.121 = bf16[2,2,2,2,64,1024]{5,4,3,2,1,0:T(8,128)(2,1)} custom-call(s32[1]{0:T(128)} %bitcast.1.core_ref, bf16[2,2,2,96,1024]{4,3,2,1,0:T(8,128)(2,1)} %bitcast.61, bf16[1024,512]{1,0:T(8,128)(2,1)} %get-tuple-element.27.kept_ref, bf16[1024,512]{1,0:T(8,128)(2,1)} %copy-done.6, ...), custom_call_target="tpu_custom_call", output_to_operand_aliasing={{}: (4, {})} | custom-call | flops 1073741824 | bytes 8388608 | tf_op jit(solution)/shard_map/pallas_call | solution.py:188
  106.0 11.6 %all_to_all.26 = bf16[16,4,2048]{2,1,0:T(4,128)(2,1)S(1)} all-to-all(bf16[16,4,2048]{2,1,0:T(4,128)(2,1)S(1)} %reshape.118), channel_id=1, replica_groups=mesh['fsdp'=16,'ctx'=16] {'ctx'}, dimensions={0} | all-to-all | bytes 524288 | tf_op jit(solution)/shard_map/all_to_all | solution.py:309
  120.8 14.6 %all_to_all.27 = bf16[32,4,1024]{2,1,0:T(4,128)(2,1)S(1)} all-to-all(bf16[32,4,1024]{2,1,0:T(4,128)(2,1)S(1)} %bitcast.65), channel_id=1, replica_groups={{0,128,1,129,2,130,3,131,4,132,5,133,6,134,7,135,8,136,9,137,10,138,11,..., dimensions={0} | all-to-all | bytes 524288 | tf_op jit(solution)/shard_map/all_to_all | solution.py:325
  137.5 5.3 %all-to-all-start.4 = ((bf16[32,4,1024]{2,1,0:T(4,128)(2,1)}), bf16[32,4,1024]{2,1,0:T(4,128)(2,1)S(1)}, u32[]{:S(2)}, u32[]{:S(2)}) async-start(bf16[32,4,1024]{2,1,0:T(4,128)(2,1)} %copy.24), calls=%async_computation.6 | async-start | bytes 524288 | tf_op jit(solution)/shard_map/all_to_all | solution.py:325
  143.0 7.2 %all-to-all-done.4 = bf16[32,4,1024]{2,1,0:T(4,128)(2,1)S(1)} async-done(((bf16[32,4,1024]{2,1,0:T(4,128)(2,1)}), bf16[32,4,1024]{2,1,0:T(4,128)(2,1)S(1)}, u32[]{:S(2)}, u32[]{:S(2)}) %all-to-all-start.4) | async-done | bytes 262176 | tf_op jit(solution)/shard_map/all_to_all | solution.py:325
  150.4 12.1 %reduce-scatter.3.cloned.1.call-done = bf16[128,1024]{1,0:T(8,128)(2,1)} async-done(((bf16[1024,1024]{1,0:T(8,128)(2,1)}), bf16[128,1024]{1,0:T(8,128)(2,1)}) %reduce-scatter.3.cloned.1.call-update) | async-done | bytes 262160 | tf_op jit(solution)/shard_map/reduce_scatter | solution.py:260
  165.9 5.2 %collective-permute-done.11 = bf16[128,1024]{1,0:T(8,128)(2,1)S(1)} collective-permute-done((bf16[128,1024]{1,0:T(8,128)(2,1)}, bf16[128,1024]{1,0:T(8,128)(2,1)S(1)}, u32[]{:S(2)}, u32[]{:S(2)}) %collective-permute-start.11) | collective-permute-done | bytes 262176 | tf_op jit(solution)/shard_map/ppermute | solution.py:21
  176.9 7.4 %collective-permute-done.12 = bf16[128,1024]{1,0:T(8,128)(2,1)S(1)} collective-permute-done((bf16[128,1024]{1,0:T(8,128)(2,1)S(1)}, bf16[128,1024]{1,0:T(8,128)(2,1)S(1)}, u32[]{:S(2)}, u32[]{:S(2)}) %collective-permute-start.12) | collective-permute-done | bytes 262176 | tf_op jit(solution)/shard_map/ppermute | solution.py:35
  185.5 3.1 %collective-permute-start.15 = (bf16[128,1024]{1,0:T(8,128)(2,1)S(1)}, bf16[128,1024]{1,0:T(8,128)(2,1)S(1)}, u32[]{:S(2)}, u32[]{:S(2)}) collective-permute-start(bf16[128,1024]{1,0:T(8,128)(2,1)S(1)} %collective-permute-done.13), channel_id=1, source_target_pairs={{0,112},{1,113},{2,114},{3,115},{4,116},{5,117},{6,118},{7,119},{8... | collective-permute-start | bytes 786440 | tf_op jit(solution)/shard_map/ppermute | solution.py:35
  190.2 9.3 %collective-permute-done.14 = bf16[128,1024]{1,0:T(8,128)(2,1)S(1)} collective-permute-done((bf16[128,1024]{1,0:T(8,128)(2,1)S(1)}, bf16[128,1024]{1,0:T(8,128)(2,1)S(1)}, u32[]{:S(2)}, u32[]{:S(2)}) %collective-permute-start.14) | collective-permute-done | bytes 262176 | tf_op jit(solution)/shard_map/ppermute | solution.py:35
  200.3 3.7 %collective-permute-start.17 = (bf16[128,1024]{1,0:T(8,128)(2,1)S(1)}, bf16[128,1024]{1,0:T(8,128)(2,1)S(1)}, u32[]{:S(2)}, u32[]{:S(2)}) collective-permute-start(bf16[128,1024]{1,0:T(8,128)(2,1)S(1)} %collective-permute-done.15), channel_id=1, source_target_pairs={{0,112},{1,113},{2,114},{3,115},{4,116},{5,117},{6,118},{7,119},{8... | collective-permute-start | bytes 786440 | tf_op jit(solution)/shard_map/ppermute | solution.py:35
  204.1 7.2 %collective-permute-done.16 = bf16[128,1024]{1,0:T(8,128)(2,1)S(1)} collective-permute-done((bf16[128,1024]{1,0:T(8,128)(2,1)S(1)}, bf16[128,1024]{1,0:T(8,128)(2,1)S(1)}, u32[]{:S(2)}, u32[]{:S(2)}) %collective-permute-start.16) | collective-permute-done | bytes 262176 | tf_op jit(solution)/shard_map/ppermute | solution.py:35
  212.1 2.6 %collective-permute-start.19 = (bf16[64,1024]{1,0:T(8,128)(2,1)S(1)}, bf16[64,1024]{1,0:T(8,128)(2,1)S(1)}, u32[]{:S(2)}, u32[]{:S(2)}) collective-permute-start(bf16[64,1024]{1,0:T(8,128)(2,1)S(1)} %slice.37), channel_id=1, source_target_pairs={{0,112},{1,113},{2,114},{3,115},{4,116},{5,117},{6,118},{7,119},{8... | collective-permute-start | bytes 393224 | tf_op jit(solution)/shard_map/ppermute | solution.py:35
  214.7 2.8 %collective-permute-done.18 = bf16[64,1024]{1,0:T(8,128)(2,1)S(1)} collective-permute-done((bf16[64,1024]{1,0:T(8,128)(2,1)S(1)}, bf16[64,1024]{1,0:T(8,128)(2,1)S(1)}, u32[]{:S(2)}, u32[]{:S(2)}) %collective-permute-start.18) | collective-permute-done | bytes 131104 | tf_op jit(solution)/shard_map/ppermute | solution.py:35
  218.9 6.3 %shard_map.124 = bf16[2048,512]{1,0:T(8,128)(2,1)} custom-call(s32[1]{0:T(128)} %bitcast.y_lo_ref, bf16[1024,1024]{1,0:T(8,128)(2,1)} %all-gather.2.cloned.1.call-done.own_ref, bf16[1024,1024]{1,0:T(8,128)(2,1)} %copy-done.10, bf16[1024,512]{1,0:T(8,128)(2,1)} %bitcast.63), custom_call_target="tpu_custom_call" | custom-call | flops 2147483648 | bytes 7340032 | tf_op jit(solution)/shard_map/pallas_call | solution.py:237
  (114 shorter events, 42.4 us)
Async XLA Ops:
  7.5 10.0 %collective-permute-start.1 = (bf16[2,64,512]{2,1,0:T(8,128)(2,1)S(1)}, bf16[2,64,512]{2,1,0:T(8,128)(2,1)S(1)}, u32[]{:S(2)}, u32[]{:S(2)}) collective-permute-start(bf16[2,64,512]{2,1,0:T(8,128)(2,1)S(1)} %slice.32), channel_id=1, source_target_pairs={{0,2},{1,3},{2,0},{3,1},{4,6},{5,7},{6,4},{7,5},{8,10},{9,11},{10,... | collective-permute-start | bytes 393224 | tf_op jit(solution)/shard_map/ppermute | solution.py:21
  10.7 6.7 %collective-permute-start.2 = (bf16[2,64,512]{2,1,0:T(8,128)(2,1)S(1)}, bf16[2,64,512]{2,1,0:T(8,128)(2,1)S(1)}, u32[]{:S(2)}, u32[]{:S(2)}) collective-permute-start(bf16[2,64,512]{2,1,0:T(8,128)(2,1)S(1)} %slice.32), channel_id=1, source_target_pairs={{0,130},{1,131},{2,128},{3,129},{4,134},{5,135},{6,132},{7,133},{8... | collective-permute-start | bytes 393224 | tf_op jit(solution)/shard_map/ppermute | solution.py:21
  11.8 5.6 %collective-permute-start = (bf16[2,64,512]{2,1,0:T(8,128)(2,1)S(1)}, bf16[2,64,512]{2,1,0:T(8,128)(2,1)S(1)}, u32[]{:S(2)}, u32[]{:S(2)}) collective-permute-start(bf16[2,64,512]{2,1,0:T(8,128)(2,1)S(1)} %slice.32), channel_id=1, source_target_pairs={{0,128},{1,129},{2,130},{3,131},{4,132},{5,133},{6,134},{7,135},{8... | collective-permute-start | bytes 393224 | tf_op jit(solution)/shard_map/ppermute | solution.py:21
  19.2 30.1 %all-to-all-start = ((bf16[4,2,2,64,1024]{4,3,2,1,0:T(8,128)(2,1)}), bf16[4,2,2,64,1024]{4,3,2,1,0:T(8,128)(2,1)S(1)}, u32[]{:S(2)}, u32[]{:S(2)}) async-start(bf16[4,2,2,64,1024]{4,3,2,1,0:T(8,128)(2,1)} %broadcast_in_dim.6), calls=%async_computation | async-start | bytes 4194304 | tf_op jit(solution)/shard_map/all_to_all | solution.py:162
  24.3 95.0 %reduce-scatter.5.cloned.1.call-start = ((), (), s32[]{:S(2)}) async-start(), calls=%async_computation.8 | async-start | bytes 4718592 | tf_op jit(solution)/shard_map/reduce_scatter | solution.py:260
  24.3 24.8 %collective-permute-start.3 = (bf16[1024,512]{1,0:T(8,128)(2,1)}, bf16[1024,512]{1,0:T(8,128)(2,1)S(1)}, u32[]{:S(2)}, u32[]{:S(2)}) collective-permute-start(bf16[1024,512]{1,0:T(8,128)(2,1)} %get-tuple-element.28), channel_id=1, source_target_pairs={{0,128},{1,129},{2,130},{3,131},{4,132},{5,133},{6,134},{7,135},{8... | collective-permute-start | bytes 3145736 | tf_op jit(solution)/shard_map/ppermute | solution.py:21
  25.5 23.5 %collective-permute-start.4 = (f32[64]{0:T(128)S(1)}, f32[64]{0:T(128)S(1)}, u32[]{:S(2)}, u32[]{:S(2)}) collective-permute-start(f32[64]{0:T(128)S(1)} %copy-done.13), channel_id=1, source_target_pairs={{0,128},{1,129},{2,130},{3,131},{4,132},{5,133},{6,134},{7,135},{8... | collective-permute-start | bytes 776 | tf_op jit(solution)/shard_map/ppermute | solution.py:21
  49.3 6.8 %collective-permute-start.9 = (bf16[4,2,2,64,1024]{4,3,2,1,0:T(8,128)(2,1)S(1)}, bf16[4,2,2,64,1024]{4,3,2,1,0:T(8,128)(2,1)}, u32[]{:S(2)}, u32[]{:S(2)}) collective-permute-start(bf16[4,2,2,64,1024]{4,3,2,1,0:T(8,128)(2,1)S(1)} %all-to-all-done), channel_id=1, source_target_pairs={{0,1},{1,0},{2,3},{3,2},{4,5},{5,4},{6,7},{7,6},{8,9},{9,8},{10,11... | collective-permute-start | bytes 6291464 | tf_op jit(solution)/shard_map/ppermute | solution.py:21
  61.6 101.0 %reduce-scatter.3.cloned.1.call-start = ((), (), s32[]{:S(2)}) async-start(), calls=%async_computation.7 | async-start | bytes 2359296 | tf_op jit(solution)/shard_map/reduce_scatter | solution.py:260
  62.4 6.5 %collective-permute-start.8 = (bf16[64,512]{1,0:T(8,128)(2,1)S(1)}, bf16[64,512]{1,0:T(8,128)(2,1)S(1)}, u32[]{:S(2)}, u32[]{:S(2)}) collective-permute-start(bf16[64,512]{1,0:T(8,128)(2,1)S(1)} %copy-done.12), channel_id=1, source_target_pairs={{0,2},{1,3},{2,0},{3,1},{4,6},{5,7},{6,4},{7,5},{8,10},{9,11},{10,... | collective-permute-start | bytes 196616 | tf_op jit(solution)/shard_map/ppermute | solution.py:21
  64.6 8.1 %collective-permute-start.6 = (bf16[64,512]{1,0:T(8,128)(2,1)S(1)}, bf16[64,512]{1,0:T(8,128)(2,1)S(1)}, u32[]{:S(2)}, u32[]{:S(2)}) collective-permute-start(bf16[64,512]{1,0:T(8,128)(2,1)S(1)} %slice_bitcast_fusion), channel_id=1, source_target_pairs={{0,2},{1,3},{2,0},{3,1},{4,6},{5,7},{6,4},{7,5},{8,10},{9,11},{10,... | collective-permute-start | bytes 196616 | tf_op jit(solution)/shard_map/ppermute | solution.py:21
  65.9 6.8 %collective-permute-start.7 = (bf16[64,512]{1,0:T(8,128)(2,1)S(1)}, bf16[64,512]{1,0:T(8,128)(2,1)S(1)}, u32[]{:S(2)}, u32[]{:S(2)}) collective-permute-start(bf16[64,512]{1,0:T(8,128)(2,1)S(1)} %slice_bitcast_fusion), channel_id=1, source_target_pairs={{0,130},{1,131},{2,128},{3,129},{4,134},{5,135},{6,132},{7,133},{8... | collective-permute-start | bytes 196616 | tf_op jit(solution)/shard_map/ppermute | solution.py:21
  94.4 5.2 %collective-permute-start.10 = (bf16[4,2,96,1024]{3,2,1,0:T(8,128)(2,1)S(1)}, bf16[4,2,96,1024]{3,2,1,0:T(8,128)(2,1)S(1)}, u32[]{:S(2)}, u32[]{:S(2)}) collective-permute-start(bf16[4,2,96,1024]{3,2,1,0:T(8,128)(2,1)S(1)} %all_to_all.25), channel_id=1, source_target_pairs={{0,1},{1,0},{2,3},{3,2},{4,5},{5,4},{6,7},{7,6},{8,9},{9,8},{10,11... | collective-permute-start | bytes 4718600 | tf_op jit(solution)/shard_map/ppermute | solution.py:21
  137.5 12.7 %all-to-all-start.4 = ((bf16[32,4,1024]{2,1,0:T(4,128)(2,1)}), bf16[32,4,1024]{2,1,0:T(4,128)(2,1)S(1)}, u32[]{:S(2)}, u32[]{:S(2)}) async-start(bf16[32,4,1024]{2,1,0:T(4,128)(2,1)} %copy.24), calls=%async_computation.6 | async-start | bytes 524288 | tf_op jit(solution)/shard_map/all_to_all | solution.py:325
  142.8 74.8 %all-gather.2.cloned.1.call-start = ((), (), s32[]{:S(2)}) async-start(), calls=%async_computation.9 | async-start | bytes 2359296 | tf_op jit(solution)/shard_map/all_gather | solution.py:350
  164.4 6.7 %collective-permute-start.11 = (bf16[128,1024]{1,0:T(8,128)(2,1)}, bf16[128,1024]{1,0:T(8,128)(2,1)S(1)}, u32[]{:S(2)}, u32[]{:S(2)}) collective-permute-start(bf16[128,1024]{1,0:T(8,128)(2,1)} %fusion.3), channel_id=1, source_target_pairs={{0,128},{1,129},{2,130},{3,131},{4,132},{5,133},{6,134},{7,135},{8... | collective-permute-start | bytes 786440 | tf_op jit(solution)/shard_map/ppermute | solution.py:21
  171.1 13.2 %collective-permute-start.12 = (bf16[128,1024]{1,0:T(8,128)(2,1)S(1)}, bf16[128,1024]{1,0:T(8,128)(2,1)S(1)}, u32[]{:S(2)}, u32[]{:S(2)}) collective-permute-start(bf16[128,1024]{1,0:T(8,128)(2,1)S(1)} %collective-permute-done.11), channel_id=1, source_target_pairs={{0,16},{1,17},{2,18},{3,19},{4,20},{5,21},{6,22},{7,23},{8,24},{9,... | collective-permute-start | bytes 786440 | tf_op jit(solution)/shard_map/ppermute | solution.py:35
  172.3 13.1 %collective-permute-start.13 = (bf16[128,1024]{1,0:T(8,128)(2,1)S(1)}, bf16[128,1024]{1,0:T(8,128)(2,1)S(1)}, u32[]{:S(2)}, u32[]{:S(2)}) collective-permute-start(bf16[128,1024]{1,0:T(8,128)(2,1)S(1)} %collective-permute-done.11), channel_id=1, source_target_pairs={{0,112},{1,113},{2,114},{3,115},{4,116},{5,117},{6,118},{7,119},{8... | collective-permute-start | bytes 786440 | tf_op jit(solution)/shard_map/ppermute | solution.py:35
  184.3 15.2 %collective-permute-start.14 = (bf16[128,1024]{1,0:T(8,128)(2,1)S(1)}, bf16[128,1024]{1,0:T(8,128)(2,1)S(1)}, u32[]{:S(2)}, u32[]{:S(2)}) collective-permute-start(bf16[128,1024]{1,0:T(8,128)(2,1)S(1)} %collective-permute-done.12), channel_id=1, source_target_pairs={{0,16},{1,17},{2,18},{3,19},{4,20},{5,21},{6,22},{7,23},{8,24},{9,... | collective-permute-start | bytes 786440 | tf_op jit(solution)/shard_map/ppermute | solution.py:35
  185.5 14.8 %collective-permute-start.15 = (bf16[128,1024]{1,0:T(8,128)(2,1)S(1)}, bf16[128,1024]{1,0:T(8,128)(2,1)S(1)}, u32[]{:S(2)}, u32[]{:S(2)}) collective-permute-start(bf16[128,1024]{1,0:T(8,128)(2,1)S(1)} %collective-permute-done.13), channel_id=1, source_target_pairs={{0,112},{1,113},{2,114},{3,115},{4,116},{5,117},{6,118},{7,119},{8... | collective-permute-start | bytes 786440 | tf_op jit(solution)/shard_map/ppermute | solution.py:35
  199.5 11.8 %collective-permute-start.16 = (bf16[128,1024]{1,0:T(8,128)(2,1)S(1)}, bf16[128,1024]{1,0:T(8,128)(2,1)S(1)}, u32[]{:S(2)}, u32[]{:S(2)}) collective-permute-start(bf16[128,1024]{1,0:T(8,128)(2,1)S(1)} %collective-permute-done.14), channel_id=1, source_target_pairs={{0,16},{1,17},{2,18},{3,19},{4,20},{5,21},{6,22},{7,23},{8,24},{9,... | collective-permute-start | bytes 786440 | tf_op jit(solution)/shard_map/ppermute | solution.py:35
  200.3 11.8 %collective-permute-start.17 = (bf16[128,1024]{1,0:T(8,128)(2,1)S(1)}, bf16[128,1024]{1,0:T(8,128)(2,1)S(1)}, u32[]{:S(2)}, u32[]{:S(2)}) collective-permute-start(bf16[128,1024]{1,0:T(8,128)(2,1)S(1)} %collective-permute-done.15), channel_id=1, source_target_pairs={{0,112},{1,113},{2,114},{3,115},{4,116},{5,117},{6,118},{7,119},{8... | collective-permute-start | bytes 786440 | tf_op jit(solution)/shard_map/ppermute | solution.py:35
  211.3 6.3 %collective-permute-start.18 = (bf16[64,1024]{1,0:T(8,128)(2,1)S(1)}, bf16[64,1024]{1,0:T(8,128)(2,1)S(1)}, u32[]{:S(2)}, u32[]{:S(2)}) collective-permute-start(bf16[64,1024]{1,0:T(8,128)(2,1)S(1)} %slice.36), channel_id=1, source_target_pairs={{0,16},{1,17},{2,18},{3,19},{4,20},{5,21},{6,22},{7,23},{8,24},{9,... | collective-permute-start | bytes 393224 | tf_op jit(solution)/shard_map/ppermute | solution.py:35
  212.1 5.5 %collective-permute-start.19 = (bf16[64,1024]{1,0:T(8,128)(2,1)S(1)}, bf16[64,1024]{1,0:T(8,128)(2,1)S(1)}, u32[]{:S(2)}, u32[]{:S(2)}) collective-permute-start(bf16[64,1024]{1,0:T(8,128)(2,1)S(1)} %slice.37), channel_id=1, source_target_pairs={{0,112},{1,113},{2,114},{3,115},{4,116},{5,117},{6,118},{7,119},{8... | collective-permute-start | bytes 393224 | tf_op jit(solution)/shard_map/ppermute | solution.py:35
  (15 other events, 102.3 us)
Sparse Core Ops, SparseCore 0:
  61.7 57.5 reduce-scatter.4
  121.8 40.6 reduce-scatter.2
  164.5 48.3 all-gather.1

commit v2 on v1

--- a/solution.py
+++ b/solution.py
@@ -202,7 +202,7 @@
         ),
         out_shape=pltpu.HBM(shape, BF16),
         input_output_aliases={4: 0} if started else {},
-        compiler_params=pltpu.CompilerParams(vmem_limit_bytes=56 * 1024 * 1024),
+        compiler_params=pltpu.CompilerParams(vmem_limit_bytes=32 * 1024 * 1024),
         cost_estimate=pl.CostEstimate(
             flops=16 * rows * count * 1024, bytes_accessed=8 * 2**20, transcendentals=0
         ),
@@ -249,7 +249,7 @@
             ),
         ),
         out_shape=jax.ShapeDtypeStruct((2 * count, features), BF16),
-        compiler_params=pltpu.CompilerParams(vmem_limit_bytes=56 * 1024 * 1024),
+        compiler_params=pltpu.CompilerParams(vmem_limit_bytes=32 * 1024 * 1024),
         cost_estimate=pl.CostEstimate(
             flops=4 * channels * count * features, bytes_accessed=7 * 2**20, transcendentals=0
         ),

time: 233 us -> 229 us (0.983)
  Pallas kernels: 27.1 us -> 20.3 us
  local copies, waits for them, and re-layouts: 19.3 us -> 15.1 us
  starting transfers between devices: 37.8 us -> 40.7 us
    pallas_call x4, Pallas kernels: 18.9 us -> 14.3 us  [product(): pl.pallas_call(product_kernel, grid_spec=pltpu.PrefetchScalarGridSpec(num...]
    ppermute x8, waiting for transfers between devices: 28.7 us -> 25.6 us  [along_z(): return lax.ppermute(array, AXES, pairs)]
    unnamed x28, local copies, waits for them, and re-layouts: 6.82 us -> 4 us
    reduce_scatter x2, waiting for transfers between devices: 13 us -> 15.5 us  [reduce_over_z(): lax.psum_scatter(parts, 'fsdp', scatter_dimension=0, tiled=True, axis_ind...]
  transfers between devices with their start and end apart: 25 -> 25, of which waited for: 15 -> 16; matrix products, arithmetic and copies ran while one was open for 5% -> 4% of each run, Pallas kernels for 7% -> 5%
where the time goes in v2:
time: 229 us; the launch traced here: 227 us
  waiting for transfers between devices  84.6 us (37%)
  blocking collectives  49 us (21%)
  starting transfers between devices  40.7 us (18%)
  Pallas kernels  20.3 us (9%)
  local copies, waits for them, and re-layouts  15.1 us (7%)
  between operations  13.6 us (6%)
  other arithmetic  3.55 us (2%)
    ppermute x12, waiting for transfers between devices, flip(): return lax.ppermute(array, AXES, [(i, i ^ mask) for i in range(256)])  35.6 us
    ppermute x8, waiting for transfers between devices, along_z(): return lax.ppermute(array, AXES, pairs)  25.6 us
    all_to_all x1, blocking collectives, gather_x(): lax.all_to_all(copies, AXES, split_axis=0, concat_axis=0, tiled=True, axi...  22.4 us
    ppermute x8, starting transfers between devices, along_z(): return lax.ppermute(array, AXES, pairs)  15.6 us
    reduce_scatter x2, waiting for transfers between devices, reduce_over_z(): lax.psum_scatter(parts, 'fsdp', scatter_dimension=0, tiled=True, axis_ind...  15.5 us
    all_to_all x1, blocking collectives, to_plane(): lax.all_to_all(array, AXES, split_axis=0, concat_axis=0, tiled=True, axis...  14.5 us
    pallas_call x4, Pallas kernels, product(): pl.pallas_call(product_kernel, grid_spec=pltpu.PrefetchScalarGridSpec(num...  14.3 us
    ppermute x12, starting transfers between devices, flip(): return lax.ppermute(array, AXES, [(i, i ^ mask) for i in range(256)])  13.8 us
  transfers between devices with their start and end apart: 25, of which 16 were waited for; matrix products, arithmetic and copies ran while one was open for 4% of the time, Pallas kernels for 5%

profile of v2, /device:TPU:2, one launch (start us, length us, event | category | flops | bytes accessed | tf_op | source)
XLA Modules:
  0.0 226.8 jit_solution(9379510519162026212)
XLA Ops:
  7.5 3.3 %collective-permute-start.1 = (bf16[2,64,512]{2,1,0:T(8,128)(2,1)S(1)}, bf16[2,64,512]{2,1,0:T(8,128)(2,1)S(1)}, u32[]{:S(2)}, u32[]{:S(2)}) collective-permute-start(bf16[2,64,512]{2,1,0:T(8,128)(2,1)S(1)} %slice.32), channel_id=1, source_target_pairs={{0,2},{1,3},{2,0},{3,1},{4,6},{5,7},{6,4},{7,5},{8,10},{9,11},{10,... | collective-permute-start | bytes 393224 | tf_op jit(solution)/shard_map/ppermute | solution.py:21
  13.5 3.9 %collective-permute-done = bf16[2,64,512]{2,1,0:T(8,128)(2,1)S(1)} collective-permute-done((bf16[2,64,512]{2,1,0:T(8,128)(2,1)S(1)}, bf16[2,64,512]{2,1,0:T(8,128)(2,1)S(1)}, u32[]{:S(2)}, u32[]{:S(2)}) %collective-permute-start) | collective-permute-done | bytes 131104 | tf_op jit(solution)/shard_map/ppermute | solution.py:21
  19.2 5.9 %all-to-all-start = ((bf16[4,2,2,64,1024]{4,3,2,1,0:T(8,128)(2,1)}), bf16[4,2,2,64,1024]{4,3,2,1,0:T(8,128)(2,1)}, u32[]{:S(2)}, u32[]{:S(2)}) async-start(bf16[4,2,2,64,1024]{4,3,2,1,0:T(8,128)(2,1)} %broadcast_in_dim.6), calls=%async_computation | async-start | bytes 4194304 | tf_op jit(solution)/shard_map/all_to_all | solution.py:162
  28.0 21.7 %collective-permute-done.4 = f32[64]{0:T(128)S(1)} collective-permute-done((f32[64]{0:T(128)S(1)}, f32[64]{0:T(128)S(1)}, u32[]{:S(2)}, u32[]{:S(2)}) %collective-permute-start.4) | collective-permute-done | bytes 288 | tf_op jit(solution)/shard_map/ppermute | solution.py:21
  50.2 4.8 %shard_map.118.rest_0_ = bf16[2,2,2,2,128,1024]{5,4,3,2,1,0:T(8,128)(2,1)} custom-call(s32[1]{0:T(128)} %bitcast.9.core_ref, bf16[2,2,2,128,1024]{4,3,2,1,0:T(8,128)(2,1)} %bitcast.10.weights_ref, bf16[1024,512]{1,0:T(8,128)(2,1)S(1)} %get-tuple-element.27.kept_ref, bf16[1024,512]{1,0:T(8,128)(2,1)S(1)} %collective-permute-done.3.got_ref), custom_call_target="tpu_custom_call" | custom-call | flops 2147483648 | bytes 8388608 | tf_op jit(solution)/shard_map/pallas_call | solution.py:188
  55.0 4.8 %shard_map.119 = bf16[2,2,2,2,128,1024]{5,4,3,2,1,0:T(8,128)(2,1)} custom-call(s32[1]{0:T(128)} %bitcast.1.core_ref, bf16[2,2,2,128,1024]{4,3,2,1,0:T(8,128)(2,1)} %bitcast.8.weights_ref, bf16[1024,512]{1,0:T(8,128)(2,1)S(1)} %get-tuple-element.27.kept_ref, bf16[1024,512]{1,0:T(8,128)(2,1)S(1)} %collective-permute-done.3.got_ref, ...), custom_call_target="tpu_custom_call", output_to_operand_aliasing={{}: (4, {})} | custom-call | flops 2147483648 | bytes 8388608 | tf_op jit(solution)/shard_map/pallas_call | solution.py:188
  67.1 3.4 %collective-permute-done.5 = bf16[64,512]{1,0:T(8,128)(2,1)S(1)} collective-permute-done((bf16[64,512]{1,0:T(8,128)(2,1)S(1)}, bf16[64,512]{1,0:T(8,128)(2,1)S(1)}, u32[]{:S(2)}, u32[]{:S(2)}) %collective-permute-start.5) | collective-permute-done | bytes 65568 | tf_op jit(solution)/shard_map/ppermute | solution.py:21
  70.8 22.4 %all_to_all.25 = bf16[4,2,96,1024]{3,2,1,0:T(8,128)(2,1)S(1)} all-to-all(bf16[4,2,96,1024]{3,2,1,0:T(8,128)(2,1)S(1)} %broadcast_in_dim.7), channel_id=1, replica_groups={{0,4,8,12},{1,5,9,13},{2,6,10,14},{3,7,11,15},{16,20,24,28},{17,21,25,2..., dimensions={0} | all-to-all | bytes 3145728 | tf_op jit(solution)/shard_map/all_to_all | solution.py:162
  93.3 2.4 %shard_map.120.rest_0_ = bf16[2,2,2,2,64,1024]{5,4,3,2,1,0:T(8,128)(2,1)} custom-call(s32[1]{0:T(128)} %bitcast.9.core_ref, bf16[2,2,2,96,1024]{4,3,2,1,0:T(8,128)(2,1)S(1)} %bitcast.54, bf16[1024,512]{1,0:T(8,128)(2,1)S(1)} %get-tuple-element.27.kept_ref, bf16[1024,512]{1,0:T(8,128)(2,1)S(1)} %collective-permute-done.3.got_ref), custom_call_target="tpu_custom_call" | custom-call | flops 1073741824 | bytes 8388608 | tf_op jit(solution)/shard_map/pallas_call | solution.py:188
  100.2 12.0 %all_to_all.26 = bf16[16,4,2048]{2,1,0:T(4,128)(2,1)S(1)} all-to-all(bf16[16,4,2048]{2,1,0:T(4,128)(2,1)S(1)} %reshape.118), channel_id=1, replica_groups=mesh['fsdp'=16,'ctx'=16] {'ctx'}, dimensions={0} | all-to-all | bytes 524288 | tf_op jit(solution)/shard_map/all_to_all | solution.py:309
  113.1 3.5 %reduce-scatter.5.cloned.1.call-done = bf16[256,1024]{1,0:T(8,128)(2,1)} async-done(((bf16[2048,1024]{1,0:T(8,128)(2,1)}), bf16[256,1024]{1,0:T(8,128)(2,1)}) %reduce-scatter.5.cloned.1.call-update) | async-done | bytes 524304 | tf_op jit(solution)/shard_map/reduce_scatter | solution.py:260
  118.2 14.5 %all_to_all.27 = bf16[32,4,1024]{2,1,0:T(4,128)(2,1)S(1)} all-to-all(bf16[32,4,1024]{2,1,0:T(4,128)(2,1)S(1)} %bitcast.64), channel_id=1, replica_groups={{0,128,1,129,2,130,3,131,4,132,5,133,6,134,7,135,8,136,9,137,10,138,11,..., dimensions={0} | all-to-all | bytes 524288 | tf_op jit(solution)/shard_map/all_to_all | solution.py:325
  134.8 5.3 %all-to-all-start.4 = ((bf16[32,4,1024]{2,1,0:T(4,128)(2,1)}), bf16[32,4,1024]{2,1,0:T(4,128)(2,1)S(1)}, u32[]{:S(2)}, u32[]{:S(2)}) async-start(bf16[32,4,1024]{2,1,0:T(4,128)(2,1)} %copy.24), calls=%async_computation.6 | async-start | bytes 524288 | tf_op jit(solution)/shard_map/all_to_all | solution.py:325
  140.4 7.2 %all-to-all-done.4 = bf16[32,4,1024]{2,1,0:T(4,128)(2,1)S(1)} async-done(((bf16[32,4,1024]{2,1,0:T(4,128)(2,1)}), bf16[32,4,1024]{2,1,0:T(4,128)(2,1)S(1)}, u32[]{:S(2)}, u32[]{:S(2)}) %all-to-all-start.4) | async-done | bytes 262176 | tf_op jit(solution)/shard_map/all_to_all | solution.py:325
  147.8 12.0 %reduce-scatter.3.cloned.1.call-done = bf16[128,1024]{1,0:T(8,128)(2,1)} async-done(((bf16[1024,1024]{1,0:T(8,128)(2,1)}), bf16[128,1024]{1,0:T(8,128)(2,1)}) %reduce-scatter.3.cloned.1.call-update) | async-done | bytes 262160 | tf_op jit(solution)/shard_map/reduce_scatter | solution.py:260
  163.5 4.8 %collective-permute-done.11 = bf16[128,1024]{1,0:T(8,128)(2,1)S(1)} collective-permute-done((bf16[128,1024]{1,0:T(8,128)(2,1)}, bf16[128,1024]{1,0:T(8,128)(2,1)S(1)}, u32[]{:S(2)}, u32[]{:S(2)}) %collective-permute-start.11) | collective-permute-done | bytes 262176 | tf_op jit(solution)/shard_map/ppermute | solution.py:21
  174.2 6.5 %collective-permute-done.12 = bf16[128,1024]{1,0:T(8,128)(2,1)} collective-permute-done((bf16[128,1024]{1,0:T(8,128)(2,1)S(1)}, bf16[128,1024]{1,0:T(8,128)(2,1)}, u32[]{:S(2)}, u32[]{:S(2)}) %collective-permute-start.12) | collective-permute-done | bytes 262176 | tf_op jit(solution)/shard_map/ppermute | solution.py:35
  182.8 3.4 %collective-permute-start.15 = (bf16[128,1024]{1,0:T(8,128)(2,1)S(1)}, bf16[128,1024]{1,0:T(8,128)(2,1)S(1)}, u32[]{:S(2)}, u32[]{:S(2)}) collective-permute-start(bf16[128,1024]{1,0:T(8,128)(2,1)S(1)} %collective-permute-done.13), channel_id=1, source_target_pairs={{0,112},{1,113},{2,114},{3,115},{4,116},{5,117},{6,118},{7,119},{8... | collective-permute-start | bytes 786440 | tf_op jit(solution)/shard_map/ppermute | solution.py:35
  188.3 7.4 %collective-permute-done.14 = bf16[128,1024]{1,0:T(8,128)(2,1)S(1)} collective-permute-done((bf16[128,1024]{1,0:T(8,128)(2,1)}, bf16[128,1024]{1,0:T(8,128)(2,1)S(1)}, u32[]{:S(2)}, u32[]{:S(2)}) %collective-permute-start.14) | collective-permute-done | bytes 262176 | tf_op jit(solution)/shard_map/ppermute | solution.py:35
  197.5 3.7 %collective-permute-start.17 = (bf16[128,1024]{1,0:T(8,128)(2,1)S(1)}, bf16[128,1024]{1,0:T(8,128)(2,1)S(1)}, u32[]{:S(2)}, u32[]{:S(2)}) collective-permute-start(bf16[128,1024]{1,0:T(8,128)(2,1)S(1)} %collective-permute-done.15), channel_id=1, source_target_pairs={{0,112},{1,113},{2,114},{3,115},{4,116},{5,117},{6,118},{7,119},{8... | collective-permute-start | bytes 786440 | tf_op jit(solution)/shard_map/ppermute | solution.py:35
  201.3 6.8 %collective-permute-done.16 = bf16[128,1024]{1,0:T(8,128)(2,1)S(1)} collective-permute-done((bf16[128,1024]{1,0:T(8,128)(2,1)S(1)}, bf16[128,1024]{1,0:T(8,128)(2,1)S(1)}, u32[]{:S(2)}, u32[]{:S(2)}) %collective-permute-start.16) | collective-permute-done | bytes 262176 | tf_op jit(solution)/shard_map/ppermute | solution.py:35
  209.1 2.5 %collective-permute-start.19 = (bf16[64,1024]{1,0:T(8,128)(2,1)S(1)}, bf16[64,1024]{1,0:T(8,128)(2,1)S(1)}, u32[]{:S(2)}, u32[]{:S(2)}) collective-permute-start(bf16[64,1024]{1,0:T(8,128)(2,1)S(1)} %slice.37), channel_id=1, source_target_pairs={{0,112},{1,113},{2,114},{3,115},{4,116},{5,117},{6,118},{7,119},{8... | collective-permute-start | bytes 393224 | tf_op jit(solution)/shard_map/ppermute | solution.py:35
  211.6 2.8 %collective-permute-done.18 = bf16[64,1024]{1,0:T(8,128)(2,1)S(1)} collective-permute-done((bf16[64,1024]{1,0:T(8,128)(2,1)S(1)}, bf16[64,1024]{1,0:T(8,128)(2,1)S(1)}, u32[]{:S(2)}, u32[]{:S(2)}) %collective-permute-start.18) | collective-permute-done | bytes 131104 | tf_op jit(solution)/shard_map/ppermute | solution.py:35
  216.1 4.2 %shard_map.124 = bf16[2048,512]{1,0:T(8,128)(2,1)} custom-call(s32[1]{0:T(128)} %bitcast.y_lo_ref, bf16[1024,1024]{1,0:T(8,128)(2,1)S(1)} %copy-done.8, bf16[1024,1024]{1,0:T(8,128)(2,1)S(1)} %constant_dynamic-update-slice_fusion.other_ref, bf16[1024,512]{1,0:T(8,128)(2,1)S(1)} %bitcast.59), custom_call_target="tpu_custom_call" | custom-call | flops 2147483648 | bytes 7340032 | tf_op jit(solution)/shard_map/pallas_call | solution.py:237
  (114 shorter events, 43.9 us)
Async XLA Ops:
  7.5 10.0 %collective-permute-start.1 = (bf16[2,64,512]{2,1,0:T(8,128)(2,1)S(1)}, bf16[2,64,512]{2,1,0:T(8,128)(2,1)S(1)}, u32[]{:S(2)}, u32[]{:S(2)}) collective-permute-start(bf16[2,64,512]{2,1,0:T(8,128)(2,1)S(1)} %slice.32), channel_id=1, source_target_pairs={{0,2},{1,3},{2,0},{3,1},{4,6},{5,7},{6,4},{7,5},{8,10},{9,11},{10,... | collective-permute-start | bytes 393224 | tf_op jit(solution)/shard_map/ppermute | solution.py:21
  10.7 6.7 %collective-permute-start.2 = (bf16[2,64,512]{2,1,0:T(8,128)(2,1)S(1)}, bf16[2,64,512]{2,1,0:T(8,128)(2,1)S(1)}, u32[]{:S(2)}, u32[]{:S(2)}) collective-permute-start(bf16[2,64,512]{2,1,0:T(8,128)(2,1)S(1)} %slice.32), channel_id=1, source_target_pairs={{0,130},{1,131},{2,128},{3,129},{4,134},{5,135},{6,132},{7,133},{8... | collective-permute-start | bytes 393224 | tf_op jit(solution)/shard_map/ppermute | solution.py:21
  11.8 5.6 %collective-permute-start = (bf16[2,64,512]{2,1,0:T(8,128)(2,1)S(1)}, bf16[2,64,512]{2,1,0:T(8,128)(2,1)S(1)}, u32[]{:S(2)}, u32[]{:S(2)}) collective-permute-start(bf16[2,64,512]{2,1,0:T(8,128)(2,1)S(1)} %slice.32), channel_id=1, source_target_pairs={{0,128},{1,129},{2,130},{3,131},{4,132},{5,133},{6,134},{7,135},{8... | collective-permute-start | bytes 393224 | tf_op jit(solution)/shard_map/ppermute | solution.py:21
  19.2 31.0 %all-to-all-start = ((bf16[4,2,2,64,1024]{4,3,2,1,0:T(8,128)(2,1)}), bf16[4,2,2,64,1024]{4,3,2,1,0:T(8,128)(2,1)}, u32[]{:S(2)}, u32[]{:S(2)}) async-start(bf16[4,2,2,64,1024]{4,3,2,1,0:T(8,128)(2,1)} %broadcast_in_dim.6), calls=%async_computation | async-start | bytes 4194304 | tf_op jit(solution)/shard_map/all_to_all | solution.py:162
  25.1 91.6 %reduce-scatter.5.cloned.1.call-start = ((), (), s32[]{:S(2)}) async-start(), calls=%async_computation.8 | async-start | bytes 4718592 | tf_op jit(solution)/shard_map/reduce_scatter | solution.py:260
  25.1 24.5 %collective-permute-start.3 = (bf16[1024,512]{1,0:T(8,128)(2,1)S(1)}, bf16[1024,512]{1,0:T(8,128)(2,1)S(1)}, u32[]{:S(2)}, u32[]{:S(2)}) collective-permute-start(bf16[1024,512]{1,0:T(8,128)(2,1)S(1)} %get-tuple-element.28), channel_id=1, source_target_pairs={{0,128},{1,129},{2,130},{3,131},{4,132},{5,133},{6,134},{7,135},{8... | collective-permute-start | bytes 3145736 | tf_op jit(solution)/shard_map/ppermute | solution.py:21
  25.7 24.0 %collective-permute-start.4 = (f32[64]{0:T(128)S(1)}, f32[64]{0:T(128)S(1)}, u32[]{:S(2)}, u32[]{:S(2)}) collective-permute-start(f32[64]{0:T(128)S(1)} %copy-done.13), channel_id=1, source_target_pairs={{0,128},{1,129},{2,130},{3,131},{4,132},{5,133},{6,134},{7,135},{8... | collective-permute-start | bytes 776 | tf_op jit(solution)/shard_map/ppermute | solution.py:21
  50.2 4.8 %collective-permute-start.9 = (bf16[4,2,2,64,1024]{4,3,2,1,0:T(8,128)(2,1)}, bf16[4,2,2,64,1024]{4,3,2,1,0:T(8,128)(2,1)}, u32[]{:S(2)}, u32[]{:S(2)}) collective-permute-start(bf16[4,2,2,64,1024]{4,3,2,1,0:T(8,128)(2,1)} %all-to-all-done), channel_id=1, source_target_pairs={{0,1},{1,0},{2,3},{3,2},{4,5},{5,4},{6,7},{7,6},{8,9},{9,8},{10,11... | collective-permute-start | bytes 6291464 | tf_op jit(solution)/shard_map/ppermute | solution.py:21
  59.8 100.0 %reduce-scatter.3.cloned.1.call-start = ((), (), s32[]{:S(2)}) async-start(), calls=%async_computation.7 | async-start | bytes 2359296 | tf_op jit(solution)/shard_map/reduce_scatter | solution.py:260
  60.6 6.4 %collective-permute-start.8 = (bf16[64,512]{1,0:T(8,128)(2,1)S(1)}, bf16[64,512]{1,0:T(8,128)(2,1)S(1)}, u32[]{:S(2)}, u32[]{:S(2)}) collective-permute-start(bf16[64,512]{1,0:T(8,128)(2,1)S(1)} %copy-done.12), channel_id=1, source_target_pairs={{0,2},{1,3},{2,0},{3,1},{4,6},{5,7},{6,4},{7,5},{8,10},{9,11},{10,... | collective-permute-start | bytes 196616 | tf_op jit(solution)/shard_map/ppermute | solution.py:21
  61.9 8.6 %collective-permute-start.6 = (bf16[64,512]{1,0:T(8,128)(2,1)S(1)}, bf16[64,512]{1,0:T(8,128)(2,1)S(1)}, u32[]{:S(2)}, u32[]{:S(2)}) collective-permute-start(bf16[64,512]{1,0:T(8,128)(2,1)S(1)} %slice_bitcast_fusion), channel_id=1, source_target_pairs={{0,2},{1,3},{2,0},{3,1},{4,6},{5,7},{6,4},{7,5},{8,10},{9,11},{10,... | collective-permute-start | bytes 196616 | tf_op jit(solution)/shard_map/ppermute | solution.py:21
  64.2 6.4 %collective-permute-start.7 = (bf16[64,512]{1,0:T(8,128)(2,1)S(1)}, bf16[64,512]{1,0:T(8,128)(2,1)S(1)}, u32[]{:S(2)}, u32[]{:S(2)}) collective-permute-start(bf16[64,512]{1,0:T(8,128)(2,1)S(1)} %slice_bitcast_fusion), channel_id=1, source_target_pairs={{0,130},{1,131},{2,128},{3,129},{4,134},{5,135},{6,132},{7,133},{8... | collective-permute-start | bytes 196616 | tf_op jit(solution)/shard_map/ppermute | solution.py:21
  66.2 4.3 %collective-permute-start.5 = (bf16[64,512]{1,0:T(8,128)(2,1)S(1)}, bf16[64,512]{1,0:T(8,128)(2,1)S(1)}, u32[]{:S(2)}, u32[]{:S(2)}) collective-permute-start(bf16[64,512]{1,0:T(8,128)(2,1)S(1)} %slice_bitcast_fusion), channel_id=1, source_target_pairs={{0,128},{1,129},{2,130},{3,131},{4,132},{5,133},{6,134},{7,135},{8... | collective-permute-start | bytes 196616 | tf_op jit(solution)/shard_map/ppermute | solution.py:21
  134.8 12.7 %all-to-all-start.4 = ((bf16[32,4,1024]{2,1,0:T(4,128)(2,1)}), bf16[32,4,1024]{2,1,0:T(4,128)(2,1)S(1)}, u32[]{:S(2)}, u32[]{:S(2)}) async-start(bf16[32,4,1024]{2,1,0:T(4,128)(2,1)} %copy.24), calls=%async_computation.6 | async-start | bytes 524288 | tf_op jit(solution)/shard_map/all_to_all | solution.py:325
  140.2 74.3 %all-gather.2.cloned.1.call-start = ((), (), s32[]{:S(2)}) async-start(), calls=%async_computation.9 | async-start | bytes 2359296 | tf_op jit(solution)/shard_map/all_gather | solution.py:350
  161.7 6.7 %collective-permute-start.11 = (bf16[128,1024]{1,0:T(8,128)(2,1)}, bf16[128,1024]{1,0:T(8,128)(2,1)S(1)}, u32[]{:S(2)}, u32[]{:S(2)}) collective-permute-start(bf16[128,1024]{1,0:T(8,128)(2,1)} %fusion.3), channel_id=1, source_target_pairs={{0,128},{1,129},{2,130},{3,131},{4,132},{5,133},{6,134},{7,135},{8... | collective-permute-start | bytes 786440 | tf_op jit(solution)/shard_map/ppermute | solution.py:21
  168.3 12.4 %collective-permute-start.12 = (bf16[128,1024]{1,0:T(8,128)(2,1)S(1)}, bf16[128,1024]{1,0:T(8,128)(2,1)}, u32[]{:S(2)}, u32[]{:S(2)}) collective-permute-start(bf16[128,1024]{1,0:T(8,128)(2,1)S(1)} %collective-permute-done.11), channel_id=1, source_target_pairs={{0,16},{1,17},{2,18},{3,19},{4,20},{5,21},{6,22},{7,23},{8,24},{9,... | collective-permute-start | bytes 786440 | tf_op jit(solution)/shard_map/ppermute | solution.py:35
  169.7 13.0 %collective-permute-start.13 = (bf16[128,1024]{1,0:T(8,128)(2,1)S(1)}, bf16[128,1024]{1,0:T(8,128)(2,1)S(1)}, u32[]{:S(2)}, u32[]{:S(2)}) collective-permute-start(bf16[128,1024]{1,0:T(8,128)(2,1)S(1)} %collective-permute-done.11), channel_id=1, source_target_pairs={{0,112},{1,113},{2,114},{3,115},{4,116},{5,117},{6,118},{7,119},{8... | collective-permute-start | bytes 786440 | tf_op jit(solution)/shard_map/ppermute | solution.py:35
  180.7 14.9 %collective-permute-start.14 = (bf16[128,1024]{1,0:T(8,128)(2,1)}, bf16[128,1024]{1,0:T(8,128)(2,1)S(1)}, u32[]{:S(2)}, u32[]{:S(2)}) collective-permute-start(bf16[128,1024]{1,0:T(8,128)(2,1)} %collective-permute-done.12), channel_id=1, source_target_pairs={{0,16},{1,17},{2,18},{3,19},{4,20},{5,21},{6,22},{7,23},{8,24},{9,... | collective-permute-start | bytes 786440 | tf_op jit(solution)/shard_map/ppermute | solution.py:35
  182.8 14.8 %collective-permute-start.15 = (bf16[128,1024]{1,0:T(8,128)(2,1)S(1)}, bf16[128,1024]{1,0:T(8,128)(2,1)S(1)}, u32[]{:S(2)}, u32[]{:S(2)}) collective-permute-start(bf16[128,1024]{1,0:T(8,128)(2,1)S(1)} %collective-permute-done.13), channel_id=1, source_target_pairs={{0,112},{1,113},{2,114},{3,115},{4,116},{5,117},{6,118},{7,119},{8... | collective-permute-start | bytes 786440 | tf_op jit(solution)/shard_map/ppermute | solution.py:35
  195.7 12.5 %collective-permute-start.16 = (bf16[128,1024]{1,0:T(8,128)(2,1)S(1)}, bf16[128,1024]{1,0:T(8,128)(2,1)S(1)}, u32[]{:S(2)}, u32[]{:S(2)}) collective-permute-start(bf16[128,1024]{1,0:T(8,128)(2,1)S(1)} %collective-permute-done.14), channel_id=1, source_target_pairs={{0,16},{1,17},{2,18},{3,19},{4,20},{5,21},{6,22},{7,23},{8,24},{9,... | collective-permute-start | bytes 786440 | tf_op jit(solution)/shard_map/ppermute | solution.py:35
  197.5 11.6 %collective-permute-start.17 = (bf16[128,1024]{1,0:T(8,128)(2,1)S(1)}, bf16[128,1024]{1,0:T(8,128)(2,1)S(1)}, u32[]{:S(2)}, u32[]{:S(2)}) collective-permute-start(bf16[128,1024]{1,0:T(8,128)(2,1)S(1)} %collective-permute-done.15), channel_id=1, source_target_pairs={{0,112},{1,113},{2,114},{3,115},{4,116},{5,117},{6,118},{7,119},{8... | collective-permute-start | bytes 786440 | tf_op jit(solution)/shard_map/ppermute | solution.py:35
  208.2 6.3 %collective-permute-start.18 = (bf16[64,1024]{1,0:T(8,128)(2,1)S(1)}, bf16[64,1024]{1,0:T(8,128)(2,1)S(1)}, u32[]{:S(2)}, u32[]{:S(2)}) collective-permute-start(bf16[64,1024]{1,0:T(8,128)(2,1)S(1)} %slice.36), channel_id=1, source_target_pairs={{0,16},{1,17},{2,18},{3,19},{4,20},{5,21},{6,22},{7,23},{8,24},{9,... | collective-permute-start | bytes 393224 | tf_op jit(solution)/shard_map/ppermute | solution.py:35
  209.1 5.3 %collective-permute-start.19 = (bf16[64,1024]{1,0:T(8,128)(2,1)S(1)}, bf16[64,1024]{1,0:T(8,128)(2,1)S(1)}, u32[]{:S(2)}, u32[]{:S(2)}) collective-permute-start(bf16[64,1024]{1,0:T(8,128)(2,1)S(1)} %slice.37), channel_id=1, source_target_pairs={{0,112},{1,113},{2,114},{3,115},{4,116},{5,117},{6,118},{7,119},{8... | collective-permute-start | bytes 393224 | tf_op jit(solution)/shard_map/ppermute | solution.py:35
  (15 other events, 110.0 us)
Sparse Core Ops, SparseCore 0:
  59.9 56.6 reduce-scatter.4
  119.2 40.5 reduce-scatter.2
  161.8 48.7 all-gather.1

commit v3 on v2

--- a/solution.py
+++ b/solution.py
@@ -225,7 +225,7 @@
             values_ref[...], weights_ref[...], over, preferred_element_type=F32
         ).astype(BF16)
 
-    first = pl.program_id(0) == 0
+    first = pl.program_id(0) < 2
     pl.when(first)(lambda: write(own_ref))
     pl.when(jnp.logical_not(first))(lambda: write(other_ref))
 
@@ -238,20 +238,20 @@
         project_kernel,
         grid_spec=pltpu.PrefetchScalarGridSpec(
             num_scalar_prefetch=1,
-            grid=(2, 2),
+            grid=(3,),
             in_specs=[
-                pl.BlockSpec((channels, block), lambda i, j, y: (0, jnp.where(i == 0, j, 1))),
-                pl.BlockSpec((channels, block), lambda i, j, y: (0, jnp.where(i == 0, 0, j))),
-                pl.BlockSpec((channels, features), lambda i, j, y: (0, 0)),
+                pl.BlockSpec((channels, block), lambda i, y: (0, jnp.minimum(i, 1))),
+                pl.BlockSpec((channels, block), lambda i, y: (0, 0)),
+                pl.BlockSpec((channels, features), lambda i, y: (0, 0)),
             ],
             out_specs=pl.BlockSpec(
-                (block, features), lambda i, j, y: (jnp.where(i == 0, y[0], 1 - y[0]) * 2 + j, 0)
+                (block, features), lambda i, y: (jnp.where(i < 2, y[0] * 2 + i, (1 - y[0]) * 2), 0)
             ),
         ),
-        out_shape=jax.ShapeDtypeStruct((2 * count, features), BF16),
+        out_shape=pltpu.HBM((2 * count, features), BF16),
         compiler_params=pltpu.CompilerParams(vmem_limit_bytes=32 * 1024 * 1024),
         cost_estimate=pl.CostEstimate(
-            flops=4 * channels * count * features, bytes_accessed=7 * 2**20, transcendentals=0
+            flops=3 * channels * count * features, bytes_accessed=6 * 2**20, transcendentals=0
         ),
     )(jnp.reshape(y_lo, (1,)).astype(jnp.int32), own, other, weights)
 
@@ -286,11 +286,7 @@
         y_lo == 0, jnp.stack([skip_gain, other_gain]), jnp.stack([other_gain, skip_gain])
     )
     query_column = gather_y(query_shard, y_hi)
-    out_other = flip(out_proj, FLIP_Y_HI)
-    out_column = jnp.where(
-        y_hi == 0, jnp.stack([out_proj, out_other]), jnp.stack([out_other, out_proj])
-    )
-    late = jnp.concatenate([query_column, out_column.reshape(2, 32, 1024)], axis=1)
+    late = jnp.concatenate([query_column, gather_y(out_proj, y_hi)], axis=1)
 
     kept = lax.dynamic_slice_in_dim(tokens, y_lo * half, half, 0)
     parts, _ = products(plane, 128, kept, got, core)
@@ -303,7 +299,7 @@
     out_rows = jnp.where(
         core == 0, jnp.stack([out_own, out_other], 2), jnp.stack([out_other, out_own], 2)
     )
-    out_rows = out_rows.reshape(2, 2, 2, 2, 64, 512).transpose(1, 2, 3, 0, 4, 5).reshape(1024, 512)
+    out_rows = out_rows.reshape(2, 2, 2, 2, 64, 1024).transpose(1, 2, 3, 0, 4, 5).reshape(1024, 1024)
 
     taps = after(filter_taps.astype(BF16), parts)
     taps = lax.all_to_all(
@@ -346,25 +342,36 @@
     gated = (query * (convolved.astype(F32) + gain[:, :, None] * mixed)).astype(BF16)
 
     gated = gated.reshape(128, half)
-
-    gathered = lax.all_gather(
-        gated, "fsdp", axis=0, tiled=True, axis_index_groups=z_groups()
-    )
-    up = down = flip(gated, FLIP_Y_LO)
-    other_rows = jnp.zeros((1024, half), BF16)
+    quarter = half // 2
 
     def put(array, piece, offset, row=0):
         return lax.dynamic_update_slice_in_dim(
             array, piece, (z + offset) % RINGS * 128 + row, 0
         )
 
-    other_rows = put(other_rows, up, 0)
+    other_rows = lax.all_gather(
+        flip(gated[:, :quarter], FLIP_Y_LO),
+        "fsdp",
+        axis=0,
+        tiled=True,
+        axis_index_groups=z_groups(),
+    )
+    up = down = gated
+    own_rows = put(query_parts, gated, 0)
     for distance in (1, 2, 3):
         up, down = along_z(up, 1), along_z(down, -1)
-        other_rows = put(put(other_rows, up, -distance), down, distance)
+        own_rows = put(put(own_rows, up, -distance), down, distance)
     up, down = along_z(up[:64], 1), along_z(down[64:], -1)
-    other_rows = put(put(other_rows, up, -4), down, 4, 64)
-    return project(gathered, other_rows, out_rows, y_lo)
+    own_rows = put(put(own_rows, up, -4), down, 4, 64)
+    given = lax.dot_general(
+        own_rows[:, quarter:],
+        out_rows[:, 512:],
+        (((0,), (0,)), ((), ())),
+        preferred_element_type=F32,
+    ).astype(BF16)
+    got = flip(given, FLIP_Y_LO)
+    result = project(own_rows, other_rows, out_rows[:, :512], y_lo)
+    return lax.dynamic_update_slice_in_dim(result, got, (1 - y_lo) * half + quarter, 0)
 
 
 def solution(mesh):

time: 229 us -> 223 us (0.974)
  waiting for transfers between devices: 84.6 us -> 72.2 us
  blocking collectives: 49 us -> 52.6 us
  local copies, waits for them, and re-layouts: 15.1 us -> 18.2 us
    reduce_scatter x2, waiting for transfers between devices: 15.5 us -> 6.27 us  [reduce_over_z(): lax.psum_scatter(parts, 'fsdp', scatter_dimension=0, tiled=True, axis_ind...]
    ppermute x8, starting transfers between devices: 15.6 us -> 9 us  [along_z(): return lax.ppermute(array, AXES, pairs)]
    ppermute x12 -> x15, starting transfers between devices: 13.8 us -> 19.7 us  [flip(): return lax.ppermute(array, AXES, [(i, i ^ mask) for i in range(256)])]
    all_to_all x1, blocking collectives: 22.4 us -> 27.5 us  [gather_x(): lax.all_to_all(copies, AXES, split_axis=0, concat_axis=0, tiled=True, axi...]
    ppermute x8, waiting for transfers between devices: 25.6 us -> 22 us  [along_z(): return lax.ppermute(array, AXES, pairs)]
    ppermute x12 -> x15, waiting for transfers between devices: 35.6 us -> 34.5 us  [flip(): return lax.ppermute(array, AXES, [(i, i ^ mask) for i in range(256)])]
  transfers between devices with their start and end apart: 25 -> 28, of which waited for: 16 -> 16; matrix products, arithmetic and copies ran while one was open for 4% -> 7% of each run, Pallas kernels for 5% -> 7%
where the time goes in v3:
time: 223 us; the launch traced here: 221 us
  waiting for transfers between devices  72.2 us (32%)
  blocking collectives  52.6 us (24%)
  starting transfers between devices  39.3 us (18%)
  Pallas kernels  19.4 us (9%)
  local copies, waits for them, and re-layouts  18.2 us (8%)
  between operations  13.8 us (6%)
  other arithmetic  3.86 us (2%)
    ppermute x15, waiting for transfers between devices, flip(): return lax.ppermute(array, AXES, [(i, i ^ mask) for i in range(256)])  34.5 us
    all_to_all x1, blocking collectives, gather_x(): lax.all_to_all(copies, AXES, split_axis=0, concat_axis=0, tiled=True, axi...  27.5 us
    ppermute x8, waiting for transfers between devices, along_z(): return lax.ppermute(array, AXES, pairs)  22 us
    ppermute x15, starting transfers between devices, flip(): return lax.ppermute(array, AXES, [(i, i ^ mask) for i in range(256)])  19.7 us
    pallas_call x4, Pallas kernels, product(): pl.pallas_call(product_kernel, grid_spec=pltpu.PrefetchScalarGridSpec(num...  14.4 us
    all_to_all x1, blocking collectives, local(): lax.all_to_all(taps.reshape(16, 4, 2048), 'ctx', split_axis=0, concat_axi...  12.8 us
    all_to_all x1, blocking collectives, to_plane(): lax.all_to_all(array, AXES, split_axis=0, concat_axis=0, tiled=True, axis...  12.3 us
    ppermute x8, starting transfers between devices, along_z(): return lax.ppermute(array, AXES, pairs)  9 us
  transfers between devices with their start and end apart: 28, of which 16 were waited for; matrix products, arithmetic and copies ran while one was open for 7% of the time, Pallas kernels for 7%

profile of v3, /device:TPU:2, one launch (start us, length us, event | category | flops | bytes accessed | tf_op | source)
XLA Modules:
  0.0 220.8 jit_solution(11309217023138175479)
XLA Ops:
  7.5 3.1 %collective-permute-start.2 = (bf16[2,64,512]{2,1,0:T(8,128)(2,1)S(1)}, bf16[2,64,512]{2,1,0:T(8,128)(2,1)S(1)}, u32[]{:S(2)}, u32[]{:S(2)}) collective-permute-start(bf16[2,64,512]{2,1,0:T(8,128)(2,1)S(1)} %slice.48), channel_id=1, source_target_pairs={{0,130},{1,131},{2,128},{3,129},{4,134},{5,135},{6,132},{7,133},{8... | collective-permute-start | bytes 393224 | tf_op jit(solution)/shard_map/ppermute | solution.py:21
  13.3 4.2 %collective-permute-done = bf16[2,64,512]{2,1,0:T(8,128)(2,1)S(1)} collective-permute-done((bf16[2,64,512]{2,1,0:T(8,128)(2,1)S(1)}, bf16[2,64,512]{2,1,0:T(8,128)(2,1)S(1)}, u32[]{:S(2)}, u32[]{:S(2)}) %collective-permute-start) | collective-permute-done | bytes 131104 | tf_op jit(solution)/shard_map/ppermute | solution.py:21
  20.1 5.1 %all-to-all-start = ((bf16[4,2,2,64,1024]{4,3,2,1,0:T(8,128)(2,1)}), bf16[4,2,2,64,1024]{4,3,2,1,0:T(8,128)(2,1)}, u32[]{:S(2)}, u32[]{:S(2)}) async-start(bf16[4,2,2,64,1024]{4,3,2,1,0:T(8,128)(2,1)} %broadcast_in_dim.4), calls=%async_computation | async-start | bytes 4194304 | tf_op jit(solution)/shard_map/all_to_all | solution.py:162
  28.1 19.9 %collective-permute-done.4 = f32[64]{0:T(128)S(1)} collective-permute-done((f32[64]{0:T(128)S(1)}, f32[64]{0:T(128)S(1)}, u32[]{:S(2)}, u32[]{:S(2)}) %collective-permute-start.4) | collective-permute-done | bytes 288 | tf_op jit(solution)/shard_map/ppermute | solution.py:21
  48.5 4.8 %shard_map.118.rest_0_ = bf16[2,2,2,2,128,1024]{5,4,3,2,1,0:T(8,128)(2,1)} custom-call(s32[1]{0:T(128)} %bitcast.7.core_ref, bf16[2,2,2,128,1024]{4,3,2,1,0:T(8,128)(2,1)} %bitcast.8.weights_ref, bf16[1024,512]{1,0:T(8,128)(2,1)S(1)} %get-tuple-element.29.kept_ref, bf16[1024,512]{1,0:T(8,128)(2,1)S(1)} %collective-permute-done.3.got_ref), custom_call_target="tpu_custom_call" | custom-call | flops 2147483648 | bytes 8388608 | tf_op jit(solution)/shard_map/pallas_call | solution.py:188
  53.4 4.8 %shard_map.119 = bf16[2,2,2,2,128,1024]{5,4,3,2,1,0:T(8,128)(2,1)} custom-call(s32[1]{0:T(128)} %bitcast.1.core_ref, bf16[2,2,2,128,1024]{4,3,2,1,0:T(8,128)(2,1)} %bitcast.6.weights_ref, bf16[1024,512]{1,0:T(8,128)(2,1)S(1)} %get-tuple-element.29.kept_ref, bf16[1024,512]{1,0:T(8,128)(2,1)S(1)} %collective-permute-done.3.got_ref, ...), custom_call_target="tpu_custom_call", output_to_operand_aliasing={{}: (4, {})} | custom-call | flops 2147483648 | bytes 8388608 | tf_op jit(solution)/shard_map/pallas_call | solution.py:188
  62.9 2.6 %collective-permute-start.11 = (bf16[64,512]{1,0:T(8,128)(2,1)S(1)}, bf16[64,512]{1,0:T(8,128)(2,1)S(1)}, u32[]{:S(2)}, u32[]{:S(2)}) collective-permute-start(bf16[64,512]{1,0:T(8,128)(2,1)S(1)} %copy-done.14), channel_id=1, source_target_pairs={{0,130},{1,131},{2,128},{3,129},{4,134},{5,135},{6,132},{7,133},{8... | collective-permute-start | bytes 196616 | tf_op jit(solution)/shard_map/ppermute | solution.py:21
  67.0 3.2 %collective-permute-done.9 = bf16[64,512]{1,0:T(8,128)(2,1)S(1)} collective-permute-done((bf16[64,512]{1,0:T(8,128)(2,1)S(1)}, bf16[64,512]{1,0:T(8,128)(2,1)S(1)}, u32[]{:S(2)}, u32[]{:S(2)}) %collective-permute-start.9) | collective-permute-done | bytes 65568 | tf_op jit(solution)/shard_map/ppermute | solution.py:21
  71.7 27.5 %all_to_all.25 = bf16[4,2,128,1024]{3,2,1,0:T(8,128)(2,1)S(1)} all-to-all(bf16[4,2,128,1024]{3,2,1,0:T(8,128)(2,1)S(1)} %broadcast_in_dim.5), channel_id=1, replica_groups={{0,4,8,12},{1,5,9,13},{2,6,10,14},{3,7,11,15},{16,20,24,28},{17,21,25,2..., dimensions={0} | all-to-all | bytes 4194304 | tf_op jit(solution)/shard_map/all_to_all | solution.py:162
  99.1 2.4 %shard_map.120.rest_0_ = bf16[2,2,2,2,64,1024]{5,4,3,2,1,0:T(8,128)(2,1)} custom-call(s32[1]{0:T(128)} %bitcast.7.core_ref, bf16[2,2,2,128,1024]{4,3,2,1,0:T(8,128)(2,1)S(1)} %bitcast.58, bf16[1024,512]{1,0:T(8,128)(2,1)S(1)} %get-tuple-element.29.kept_ref, bf16[1024,512]{1,0:T(8,128)(2,1)S(1)} %collective-permute-done.3.got_ref), custom_call_target="tpu_custom_call" | custom-call | flops 1073741824 | bytes 8388608 | tf_op jit(solution)/shard_map/pallas_call | solution.py:188
  103.3 2.4 %shard_map.121 = bf16[2,2,2,2,64,1024]{5,4,3,2,1,0:T(8,128)(2,1)} custom-call(s32[1]{0:T(128)} %bitcast.1.core_ref, bf16[2,2,2,128,1024]{4,3,2,1,0:T(8,128)(2,1)S(1)} %bitcast.59, bf16[1024,512]{1,0:T(8,128)(2,1)S(1)} %get-tuple-element.29.kept_ref, bf16[1024,512]{1,0:T(8,128)(2,1)S(1)} %collective-permute-done.3.got_ref, ...), custom_call_target="tpu_custom_call", output_to_operand_aliasing={{}: (4, {})} | custom-call | flops 1073741824 | bytes 8388608 | tf_op jit(solution)/shard_map/pallas_call | solution.py:188
  106.9 12.8 %all_to_all.26 = bf16[16,4,2048]{2,1,0:T(4,128)(2,1)S(1)} all-to-all(bf16[16,4,2048]{2,1,0:T(4,128)(2,1)S(1)} %reshape.109), channel_id=1, replica_groups=mesh['fsdp'=16,'ctx'=16] {'ctx'}, dimensions={0} | all-to-all | bytes 524288 | tf_op jit(solution)/shard_map/all_to_all | solution.py:305
  123.7 12.3 %all_to_all.27 = bf16[32,4,1024]{2,1,0:T(4,128)(2,1)S(1)} all-to-all(bf16[32,4,1024]{2,1,0:T(4,128)(2,1)S(1)} %bitcast.70), channel_id=1, replica_groups={{0,128,1,129,2,130,3,131,4,132,5,133,6,134,7,135,8,136,9,137,10,138,11,..., dimensions={0} | all-to-all | bytes 524288 | tf_op jit(solution)/shard_map/all_to_all | solution.py:321
  138.2 5.3 %all-to-all-start.4 = ((bf16[32,4,1024]{2,1,0:T(4,128)(2,1)}), bf16[32,4,1024]{2,1,0:T(4,128)(2,1)S(1)}, u32[]{:S(2)}, u32[]{:S(2)}) async-start(bf16[32,4,1024]{2,1,0:T(4,128)(2,1)} %copy.24), calls=%async_computation.6 | async-start | bytes 524288 | tf_op jit(solution)/shard_map/all_to_all | solution.py:321
  143.8 7.1 %all-to-all-done.4 = bf16[32,4,1024]{2,1,0:T(4,128)(2,1)S(1)} async-done(((bf16[32,4,1024]{2,1,0:T(4,128)(2,1)}), bf16[32,4,1024]{2,1,0:T(4,128)(2,1)S(1)}, u32[]{:S(2)}, u32[]{:S(2)}) %all-to-all-start.4) | async-done | bytes 262176 | tf_op jit(solution)/shard_map/all_to_all | solution.py:321
  153.0 6.2 %reduce-scatter.5.cloned.1.call-done = bf16[128,1024]{1,0:T(8,128)(2,1)} async-done(((bf16[1024,1024]{1,0:T(8,128)(2,1)}), bf16[128,1024]{1,0:T(8,128)(2,1)}) %reduce-scatter.5.cloned.1.call-update) | async-done | bytes 262160 | tf_op jit(solution)/shard_map/reduce_scatter | solution.py:260
  164.0 3.5 %collective-permute-done.21 = bf16[128,512]{1,0:T(8,128)(2,1)S(1)} collective-permute-done((bf16[128,512]{1,0:T(8,128)(2,1)S(1)}, bf16[128,512]{1,0:T(8,128)(2,1)S(1)}, u32[]{:S(2)}, u32[]{:S(2)}) %collective-permute-start.21) | collective-permute-done | bytes 131104 | tf_op jit(solution)/shard_map/ppermute | solution.py:21
  170.4 2.6 %collective-permute-start.16 = (bf16[128,1024]{1,0:T(8,128)(2,1)S(1)}, bf16[128,1024]{1,0:T(8,128)(2,1)S(1)}, u32[]{:S(2)}, u32[]{:S(2)}) collective-permute-start(bf16[128,1024]{1,0:T(8,128)(2,1)S(1)} %collective-permute-done.14), channel_id=1, source_target_pairs={{0,112},{1,113},{2,114},{3,115},{4,116},{5,117},{6,118},{7,119},{8... | collective-permute-start | bytes 786440 | tf_op jit(solution)/shard_map/ppermute | solution.py:35
  173.6 4.1 %collective-permute-done.16 = bf16[128,1024]{1,0:T(8,128)(2,1)S(1)} collective-permute-done((bf16[128,1024]{1,0:T(8,128)(2,1)S(1)}, bf16[128,1024]{1,0:T(8,128)(2,1)S(1)}, u32[]{:S(2)}, u32[]{:S(2)}) %collective-permute-start.16) | collective-permute-done | bytes 262176 | tf_op jit(solution)/shard_map/ppermute | solution.py:35
  177.7 2.9 %collective-permute-start.18 = (bf16[128,1024]{1,0:T(8,128)(2,1)S(1)}, bf16[128,1024]{1,0:T(8,128)(2,1)S(1)}, u32[]{:S(2)}, u32[]{:S(2)}) collective-permute-start(bf16[128,1024]{1,0:T(8,128)(2,1)S(1)} %collective-permute-done.16), channel_id=1, source_target_pairs={{0,112},{1,113},{2,114},{3,115},{4,116},{5,117},{6,118},{7,119},{8... | collective-permute-start | bytes 786440 | tf_op jit(solution)/shard_map/ppermute | solution.py:35
  180.9 7.9 %collective-permute-done.18 = bf16[128,1024]{1,0:T(8,128)(2,1)S(1)} collective-permute-done((bf16[128,1024]{1,0:T(8,128)(2,1)S(1)}, bf16[128,1024]{1,0:T(8,128)(2,1)S(1)}, u32[]{:S(2)}, u32[]{:S(2)}) %collective-permute-start.18) | collective-permute-done | bytes 262176 | tf_op jit(solution)/shard_map/ppermute | solution.py:35
  192.4 7.6 %collective-permute-done.19 = bf16[64,1024]{1,0:T(8,128)(2,1)S(1)} collective-permute-done((bf16[64,1024]{1,0:T(8,128)(2,1)S(1)}, bf16[64,1024]{1,0:T(8,128)(2,1)S(1)}, u32[]{:S(2)}, u32[]{:S(2)}) %collective-permute-start.19) | collective-permute-done | bytes 131104 | tf_op jit(solution)/shard_map/ppermute | solution.py:35
  201.6 3.2 %collective-permute-start.22 = (bf16[512,512]{1,0:T(8,128)(2,1)}, bf16[512,512]{1,0:T(8,128)(2,1)}, u32[]{:S(2)}, u32[]{:S(2)}) collective-permute-start(bf16[512,512]{1,0:T(8,128)(2,1)} %convolution_convert_fusion), channel_id=1, source_target_pairs={{0,128},{1,129},{2,130},{3,131},{4,132},{5,133},{6,134},{7,135},{8... | collective-permute-start | bytes 1572872 | tf_op jit(solution)/shard_map/ppermute | solution.py:21
  209.2 3.2 %shard_map.124 = bf16[2048,512]{1,0:T(8,128)(2,1)} custom-call(s32[1]{0:T(128)} %bitcast.y_lo_ref, bf16[1024,1024]{1,0:T(8,128)(2,1)S(1)} %constant_dynamic-update-slice_fusion.1.own_ref, bf16[1024,512]{1,0:T(8,128)(2,1)S(1)} %copy-done.5, bf16[1024,512]{1,0:T(8,128)(2,1)S(1)} %slice.57.weights_ref), custom_call_target="tpu_custom_call" | custom-call | flops 1610612736 | bytes 6291456 | tf_op jit(solution)/shard_map/pallas_call | solution.py:237
  (124 shorter events, 48.1 us)
Async XLA Ops:
  7.5 10.2 %collective-permute-start.2 = (bf16[2,64,512]{2,1,0:T(8,128)(2,1)S(1)}, bf16[2,64,512]{2,1,0:T(8,128)(2,1)S(1)}, u32[]{:S(2)}, u32[]{:S(2)}) collective-permute-start(bf16[2,64,512]{2,1,0:T(8,128)(2,1)S(1)} %slice.48), channel_id=1, source_target_pairs={{0,130},{1,131},{2,128},{3,129},{4,134},{5,135},{6,132},{7,133},{8... | collective-permute-start | bytes 393224 | tf_op jit(solution)/shard_map/ppermute | solution.py:21
  10.6 7.9 %collective-permute-start.1 = (bf16[2,64,512]{2,1,0:T(8,128)(2,1)S(1)}, bf16[2,64,512]{2,1,0:T(8,128)(2,1)S(1)}, u32[]{:S(2)}, u32[]{:S(2)}) collective-permute-start(bf16[2,64,512]{2,1,0:T(8,128)(2,1)S(1)} %slice.48), channel_id=1, source_target_pairs={{0,2},{1,3},{2,0},{3,1},{4,6},{5,7},{6,4},{7,5},{8,10},{9,11},{10,... | collective-permute-start | bytes 393224 | tf_op jit(solution)/shard_map/ppermute | solution.py:21
  11.2 6.4 %collective-permute-start = (bf16[2,64,512]{2,1,0:T(8,128)(2,1)S(1)}, bf16[2,64,512]{2,1,0:T(8,128)(2,1)S(1)}, u32[]{:S(2)}, u32[]{:S(2)}) collective-permute-start(bf16[2,64,512]{2,1,0:T(8,128)(2,1)S(1)} %slice.48), channel_id=1, source_target_pairs={{0,128},{1,129},{2,130},{3,131},{4,132},{5,133},{6,134},{7,135},{8... | collective-permute-start | bytes 393224 | tf_op jit(solution)/shard_map/ppermute | solution.py:21
  20.1 28.4 %all-to-all-start = ((bf16[4,2,2,64,1024]{4,3,2,1,0:T(8,128)(2,1)}), bf16[4,2,2,64,1024]{4,3,2,1,0:T(8,128)(2,1)}, u32[]{:S(2)}, u32[]{:S(2)}) async-start(bf16[4,2,2,64,1024]{4,3,2,1,0:T(8,128)(2,1)} %broadcast_in_dim.4), calls=%async_computation | async-start | bytes 4194304 | tf_op jit(solution)/shard_map/all_to_all | solution.py:162
  25.2 95.3 %reduce-scatter.3.cloned.1.call-start = ((), (), s32[]{:S(2)}) async-start(), calls=%async_computation.7 | async-start | bytes 4718592 | tf_op jit(solution)/shard_map/reduce_scatter | solution.py:260
  25.2 22.8 %collective-permute-start.3 = (bf16[1024,512]{1,0:T(8,128)(2,1)S(1)}, bf16[1024,512]{1,0:T(8,128)(2,1)S(1)}, u32[]{:S(2)}, u32[]{:S(2)}) collective-permute-start(bf16[1024,512]{1,0:T(8,128)(2,1)S(1)} %get-tuple-element.30), channel_id=1, source_target_pairs={{0,128},{1,129},{2,130},{3,131},{4,132},{5,133},{6,134},{7,135},{8... | collective-permute-start | bytes 3145736 | tf_op jit(solution)/shard_map/ppermute | solution.py:21
  25.8 22.2 %collective-permute-start.4 = (f32[64]{0:T(128)S(1)}, f32[64]{0:T(128)S(1)}, u32[]{:S(2)}, u32[]{:S(2)}) collective-permute-start(f32[64]{0:T(128)S(1)} %copy-done.15), channel_id=1, source_target_pairs={{0,128},{1,129},{2,130},{3,131},{4,132},{5,133},{6,134},{7,135},{8... | collective-permute-start | bytes 776 | tf_op jit(solution)/shard_map/ppermute | solution.py:21
  58.2 101.1 %reduce-scatter.5.cloned.1.call-start = ((), (), s32[]{:S(2)}) async-start(), calls=%async_computation.8 | async-start | bytes 2359296 | tf_op jit(solution)/shard_map/reduce_scatter | solution.py:260
  58.2 7.7 %collective-permute-start.6 = (bf16[64,512]{1,0:T(8,128)(2,1)S(1)}, bf16[64,512]{1,0:T(8,128)(2,1)S(1)}, u32[]{:S(2)}, u32[]{:S(2)}) collective-permute-start(bf16[64,512]{1,0:T(8,128)(2,1)S(1)} %slice_bitcast_fusion), channel_id=1, source_target_pairs={{0,128},{1,129},{2,130},{3,131},{4,132},{5,133},{6,134},{7,135},{8... | collective-permute-start | bytes 196616 | tf_op jit(solution)/shard_map/ppermute | solution.py:21
  59.7 10.5 %collective-permute-start.8 = (bf16[64,512]{1,0:T(8,128)(2,1)S(1)}, bf16[64,512]{1,0:T(8,128)(2,1)S(1)}, u32[]{:S(2)}, u32[]{:S(2)}) collective-permute-start(bf16[64,512]{1,0:T(8,128)(2,1)S(1)} %slice_bitcast_fusion), channel_id=1, source_target_pairs={{0,130},{1,131},{2,128},{3,129},{4,134},{5,135},{6,132},{7,133},{8... | collective-permute-start | bytes 196616 | tf_op jit(solution)/shard_map/ppermute | solution.py:21
  61.8 8.4 %collective-permute-start.7 = (bf16[64,512]{1,0:T(8,128)(2,1)S(1)}, bf16[64,512]{1,0:T(8,128)(2,1)S(1)}, u32[]{:S(2)}, u32[]{:S(2)}) collective-permute-start(bf16[64,512]{1,0:T(8,128)(2,1)S(1)} %slice_bitcast_fusion), channel_id=1, source_target_pairs={{0,2},{1,3},{2,0},{3,1},{4,6},{5,7},{6,4},{7,5},{8,10},{9,11},{10,... | collective-permute-start | bytes 196616 | tf_op jit(solution)/shard_map/ppermute | solution.py:21
  62.9 7.3 %collective-permute-start.11 = (bf16[64,512]{1,0:T(8,128)(2,1)S(1)}, bf16[64,512]{1,0:T(8,128)(2,1)S(1)}, u32[]{:S(2)}, u32[]{:S(2)}) collective-permute-start(bf16[64,512]{1,0:T(8,128)(2,1)S(1)} %copy-done.14), channel_id=1, source_target_pairs={{0,130},{1,131},{2,128},{3,129},{4,134},{5,135},{6,132},{7,133},{8... | collective-permute-start | bytes 196616 | tf_op jit(solution)/shard_map/ppermute | solution.py:21
  65.5 5.8 %collective-permute-start.10 = (bf16[64,512]{1,0:T(8,128)(2,1)S(1)}, bf16[64,512]{1,0:T(8,128)(2,1)S(1)}, u32[]{:S(2)}, u32[]{:S(2)}) collective-permute-start(bf16[64,512]{1,0:T(8,128)(2,1)S(1)} %copy-done.14), channel_id=1, source_target_pairs={{0,2},{1,3},{2,0},{3,1},{4,6},{5,7},{6,4},{7,5},{8,10},{9,11},{10,... | collective-permute-start | bytes 196616 | tf_op jit(solution)/shard_map/ppermute | solution.py:21
  138.2 12.7 %all-to-all-start.4 = ((bf16[32,4,1024]{2,1,0:T(4,128)(2,1)}), bf16[32,4,1024]{2,1,0:T(4,128)(2,1)S(1)}, u32[]{:S(2)}, u32[]{:S(2)}) async-start(bf16[32,4,1024]{2,1,0:T(4,128)(2,1)} %copy.24), calls=%async_computation.6 | async-start | bytes 524288 | tf_op jit(solution)/shard_map/all_to_all | solution.py:321
  143.6 64.4 %all-gather.2.cloned.1.call-start = ((), (), s32[]{:S(2)}) async-start(), calls=%async_computation.9 | async-start | bytes 1179648 | tf_op jit(solution)/shard_map/all_gather | solution.py:352
  160.4 10.0 %collective-permute-start.14 = (bf16[128,1024]{1,0:T(8,128)(2,1)S(1)}, bf16[128,1024]{1,0:T(8,128)(2,1)S(1)}, u32[]{:S(2)}, u32[]{:S(2)}) collective-permute-start(bf16[128,1024]{1,0:T(8,128)(2,1)S(1)} %get-tuple-element.32), channel_id=1, source_target_pairs={{0,112},{1,113},{2,114},{3,115},{4,116},{5,117},{6,118},{7,119},{8... | collective-permute-start | bytes 786440 | tf_op jit(solution)/shard_map/ppermute | solution.py:35
  161.8 11.2 %collective-permute-start.13 = (bf16[128,1024]{1,0:T(8,128)(2,1)S(1)}, bf16[128,1024]{1,0:T(8,128)(2,1)S(1)}, u32[]{:S(2)}, u32[]{:S(2)}) collective-permute-start(bf16[128,1024]{1,0:T(8,128)(2,1)S(1)} %get-tuple-element.32), channel_id=1, source_target_pairs={{0,16},{1,17},{2,18},{3,19},{4,20},{5,21},{6,22},{7,23},{8,24},{9,... | collective-permute-start | bytes 786440 | tf_op jit(solution)/shard_map/ppermute | solution.py:35
  170.4 7.3 %collective-permute-start.16 = (bf16[128,1024]{1,0:T(8,128)(2,1)S(1)}, bf16[128,1024]{1,0:T(8,128)(2,1)S(1)}, u32[]{:S(2)}, u32[]{:S(2)}) collective-permute-start(bf16[128,1024]{1,0:T(8,128)(2,1)S(1)} %collective-permute-done.14), channel_id=1, source_target_pairs={{0,112},{1,113},{2,114},{3,115},{4,116},{5,117},{6,118},{7,119},{8... | collective-permute-start | bytes 786440 | tf_op jit(solution)/shard_map/ppermute | solution.py:35
  173.0 7.8 %collective-permute-start.15 = (bf16[128,1024]{1,0:T(8,128)(2,1)S(1)}, bf16[128,1024]{1,0:T(8,128)(2,1)S(1)}, u32[]{:S(2)}, u32[]{:S(2)}) collective-permute-start(bf16[128,1024]{1,0:T(8,128)(2,1)S(1)} %collective-permute-done.13), channel_id=1, source_target_pairs={{0,16},{1,17},{2,18},{3,19},{4,20},{5,21},{6,22},{7,23},{8,24},{9,... | collective-permute-start | bytes 786440 | tf_op jit(solution)/shard_map/ppermute | solution.py:35
  177.7 11.1 %collective-permute-start.18 = (bf16[128,1024]{1,0:T(8,128)(2,1)S(1)}, bf16[128,1024]{1,0:T(8,128)(2,1)S(1)}, u32[]{:S(2)}, u32[]{:S(2)}) collective-permute-start(bf16[128,1024]{1,0:T(8,128)(2,1)S(1)} %collective-permute-done.16), channel_id=1, source_target_pairs={{0,112},{1,113},{2,114},{3,115},{4,116},{5,117},{6,118},{7,119},{8... | collective-permute-start | bytes 786440 | tf_op jit(solution)/shard_map/ppermute | solution.py:35
  180.8 11.4 %collective-permute-start.17 = (bf16[128,1024]{1,0:T(8,128)(2,1)S(1)}, bf16[128,1024]{1,0:T(8,128)(2,1)S(1)}, u32[]{:S(2)}, u32[]{:S(2)}) collective-permute-start(bf16[128,1024]{1,0:T(8,128)(2,1)S(1)} %collective-permute-done.15), channel_id=1, source_target_pairs={{0,16},{1,17},{2,18},{3,19},{4,20},{5,21},{6,22},{7,23},{8,24},{9,... | collective-permute-start | bytes 786440 | tf_op jit(solution)/shard_map/ppermute | solution.py:35
  188.8 11.2 %collective-permute-start.20 = (bf16[64,1024]{1,0:T(8,128)(2,1)S(1)}, bf16[64,1024]{1,0:T(8,128)(2,1)S(1)}, u32[]{:S(2)}, u32[]{:S(2)}) collective-permute-start(bf16[64,1024]{1,0:T(8,128)(2,1)S(1)} %slice.53), channel_id=1, source_target_pairs={{0,112},{1,113},{2,114},{3,115},{4,116},{5,117},{6,118},{7,119},{8... | collective-permute-start | bytes 393224 | tf_op jit(solution)/shard_map/ppermute | solution.py:35
  192.3 7.7 %collective-permute-start.19 = (bf16[64,1024]{1,0:T(8,128)(2,1)S(1)}, bf16[64,1024]{1,0:T(8,128)(2,1)S(1)}, u32[]{:S(2)}, u32[]{:S(2)}) collective-permute-start(bf16[64,1024]{1,0:T(8,128)(2,1)S(1)} %slice.52), channel_id=1, source_target_pairs={{0,16},{1,17},{2,18},{3,19},{4,20},{5,21},{6,22},{7,23},{8,24},{9,... | collective-permute-start | bytes 393224 | tf_op jit(solution)/shard_map/ppermute | solution.py:35
  201.6 10.8 %collective-permute-start.22 = (bf16[512,512]{1,0:T(8,128)(2,1)}, bf16[512,512]{1,0:T(8,128)(2,1)}, u32[]{:S(2)}, u32[]{:S(2)}) collective-permute-start(bf16[512,512]{1,0:T(8,128)(2,1)} %convolution_convert_fusion), channel_id=1, source_target_pairs={{0,128},{1,129},{2,130},{3,131},{4,132},{5,133},{6,134},{7,135},{8... | collective-permute-start | bytes 1572872 | tf_op jit(solution)/shard_map/ppermute | solution.py:21
  (20 other events, 172.5 us)
Sparse Core Ops, SparseCore 0:
  58.3 57.6 reduce-scatter.2
  118.6 40.6 reduce-scatter.4
  168.4 39.5 all-gather.1

commit v4 on v3

--- a/solution.py
+++ b/solution.py
@@ -216,44 +216,61 @@
     return both.reshape(-1, kept.shape[0]), other
 
 
-def project_kernel(y_lo_ref, own_ref, other_ref, weights_ref, out_ref):
+def project_kernel(y_lo_ref, values_ref, weights_ref, *rest):
     del y_lo_ref
-    over = (((0,), (0,)), ((), ()))
-
-    def write(values_ref):
+    out_ref = rest[-1]
+
+    def multiply():
         out_ref[...] = lax.dot_general(
-            values_ref[...], weights_ref[...], over, preferred_element_type=F32
+            values_ref[...],
+            weights_ref[...],
+            (((0,), (0,)), ((), ())),
+            preferred_element_type=F32,
         ).astype(BF16)
 
-    first = pl.program_id(0) < 2
-    pl.when(first)(lambda: write(own_ref))
-    pl.when(jnp.logical_not(first))(lambda: write(other_ref))
-
-
-def project(own, other, weights, y_lo):
-    channels, count = own.shape
-    features = weights.shape[1]
-    block = count // 2
+    def copy():
+        out_ref[...] = rest[0][...]
+
+    if len(rest) == 1:
+        multiply()
+    else:
+        first = pl.program_id(0) == 0
+        pl.when(first)(multiply)
+        pl.when(jnp.logical_not(first))(copy)
+
+
+def project(values, weights, y_lo, rows, *more):
+    channels, block = values.shape[0], rows // 4
+    if more:
+        place = lambda i, y: ((1 - y[0]) * 2 + i, 0)
+        chosen = lambda i, y: (0, 0)
+        extra = [
+            pl.BlockSpec((block, 512), lambda i, y: (0, 0)),
+            pl.BlockSpec(memory_space=pl.ANY),
+        ]
+    else:
+        place = lambda i, y: (y[0] * 2 + i, 0)
+        chosen = lambda i, y: (0, i)
+        extra = []
     return pl.pallas_call(
         project_kernel,
         grid_spec=pltpu.PrefetchScalarGridSpec(
             num_scalar_prefetch=1,
-            grid=(3,),
+            grid=(2,),
             in_specs=[
-                pl.BlockSpec((channels, block), lambda i, y: (0, jnp.minimum(i, 1))),
-                pl.BlockSpec((channels, block), lambda i, y: (0, 0)),
-                pl.BlockSpec((channels, features), lambda i, y: (0, 0)),
-            ],
-            out_specs=pl.BlockSpec(
-                (block, features), lambda i, y: (jnp.where(i < 2, y[0] * 2 + i, (1 - y[0]) * 2), 0)
-            ),
+                pl.BlockSpec((channels, block), chosen),
+                pl.BlockSpec((channels, 512), lambda i, y: (0, 0)),
+            ]
+            + extra,
+            out_specs=pl.BlockSpec((block, 512), place),
         ),
-        out_shape=pltpu.HBM((2 * count, features), BF16),
+        out_shape=pltpu.HBM((rows, 512), BF16),
+        input_output_aliases={4: 0} if more else {},
         compiler_params=pltpu.CompilerParams(vmem_limit_bytes=32 * 1024 * 1024),
         cost_estimate=pl.CostEstimate(
-            flops=3 * channels * count * features, bytes_accessed=6 * 2**20, transcendentals=0
+            flops=2 * channels * block * 512, bytes_accessed=3 * 2**20, transcendentals=0
         ),
-    )(jnp.reshape(y_lo, (1,)).astype(jnp.int32), own, other, weights)
+    )(jnp.reshape(y_lo, (1,)).astype(jnp.int32), values, weights, *more)
 
 
 def reduce_over_z(parts):
@@ -370,8 +387,8 @@
         preferred_element_type=F32,
     ).astype(BF16)
     got = flip(given, FLIP_Y_LO)
-    result = project(own_rows, other_rows, out_rows[:, :512], y_lo)
-    return lax.dynamic_update_slice_in_dim(result, got, (1 - y_lo) * half + quarter, 0)
+    result = project(own_rows, out_rows, y_lo, 2 * half)
+    return project(other_rows, out_rows, y_lo, 2 * half, got, result)
 
 
 def solution(mesh):

time: 223 us -> 221 us (level)
  waiting for transfers between devices: 72.2 us -> 65.3 us
  starting transfers between devices: 39.3 us -> 42 us
  local copies, waits for them, and re-layouts: 18.2 us -> 20.5 us
    ppermute x8, waiting for transfers between devices: 22 us -> 14.5 us  [along_z(): return lax.ppermute(array, AXES, pairs)]
    ppermute x8, starting transfers between devices: 9 us -> 13.5 us  [along_z(): return lax.ppermute(array, AXES, pairs)]
    ppermute x15, waiting for transfers between devices: 34.5 us -> 36.9 us  [flip(): return lax.ppermute(array, AXES, [(i, i ^ mask) for i in range(256)])]
    unnamed x32 -> x34, local copies, waits for them, and re-layouts: 3.35 us -> 4.95 us
  transfers between devices with their start and end apart: 28 -> 28, of which waited for: 16 -> 14; matrix products, arithmetic and copies ran while one was open for 7% -> 8% of each run, Pallas kernels for 7% -> 6%
where the time goes in v4:
time: 221 us; the launch traced here: 220 us
  waiting for transfers between devices  65.3 us (30%)
  blocking collectives  52.6 us (24%)
  starting transfers between devices  42 us (19%)
  local copies, waits for them, and re-layouts  20.5 us (9%)
  Pallas kernels  20.4 us (9%)
  between operations  13.6 us (6%)
  other arithmetic  5.39 us (2%)
    ppermute x15, waiting for transfers between devices, flip(): return lax.ppermute(array, AXES, [(i, i ^ mask) for i in range(256)])  36.9 us
    all_to_all x1, blocking collectives, gather_x(): lax.all_to_all(copies, AXES, split_axis=0, concat_axis=0, tiled=True, axi...  27.5 us
    ppermute x15, starting transfers between devices, flip(): return lax.ppermute(array, AXES, [(i, i ^ mask) for i in range(256)])  17.9 us
    ppermute x8, waiting for transfers between devices, along_z(): return lax.ppermute(array, AXES, pairs)  14.5 us
    pallas_call x4, Pallas kernels, product(): pl.pallas_call(product_kernel, grid_spec=pltpu.PrefetchScalarGridSpec(num...  14.4 us
    ppermute x8, starting transfers between devices, along_z(): return lax.ppermute(array, AXES, pairs)  13.5 us
    all_to_all x1, blocking collectives, local(): lax.all_to_all(taps.reshape(16, 4, 2048), 'ctx', split_axis=0, concat_axi...  12.8 us
    all_to_all x1, blocking collectives, to_plane(): lax.all_to_all(array, AXES, split_axis=0, concat_axis=0, tiled=True, axis...  12.3 us
  transfers between devices with their start and end apart: 28, of which 14 were waited for; matrix products, arithmetic and copies ran while one was open for 8% of the time, Pallas kernels for 6%

profile of v4, /device:TPU:2, one launch (start us, length us, event | category | flops | bytes accessed | tf_op | source)
XLA Modules:
  0.0 220.5 jit_solution(7254751139913290871)
XLA Ops:
  7.5 3.1 %collective-permute-start.2 = (bf16[2,64,512]{2,1,0:T(8,128)(2,1)S(1)}, bf16[2,64,512]{2,1,0:T(8,128)(2,1)S(1)}, u32[]{:S(2)}, u32[]{:S(2)}) collective-permute-start(bf16[2,64,512]{2,1,0:T(8,128)(2,1)S(1)} %slice.44), channel_id=1, source_target_pairs={{0,130},{1,131},{2,128},{3,129},{4,134},{5,135},{6,132},{7,133},{8... | collective-permute-start | bytes 393224 | tf_op jit(solution)/shard_map/ppermute | solution.py:21
  13.3 4.2 %collective-permute-done = bf16[2,64,512]{2,1,0:T(8,128)(2,1)S(1)} collective-permute-done((bf16[2,64,512]{2,1,0:T(8,128)(2,1)S(1)}, bf16[2,64,512]{2,1,0:T(8,128)(2,1)S(1)}, u32[]{:S(2)}, u32[]{:S(2)}) %collective-permute-start) | collective-permute-done | bytes 131104 | tf_op jit(solution)/shard_map/ppermute | solution.py:21
  20.1 5.1 %all-to-all-start = ((bf16[4,2,2,64,1024]{4,3,2,1,0:T(8,128)(2,1)}), bf16[4,2,2,64,1024]{4,3,2,1,0:T(8,128)(2,1)}, u32[]{:S(2)}, u32[]{:S(2)}) async-start(bf16[4,2,2,64,1024]{4,3,2,1,0:T(8,128)(2,1)} %broadcast_in_dim.4), calls=%async_computation | async-start | bytes 4194304 | tf_op jit(solution)/shard_map/all_to_all | solution.py:162
  28.1 19.9 %collective-permute-done.4 = f32[64]{0:T(128)S(1)} collective-permute-done((f32[64]{0:T(128)S(1)}, f32[64]{0:T(128)S(1)}, u32[]{:S(2)}, u32[]{:S(2)}) %collective-permute-start.4) | collective-permute-done | bytes 288 | tf_op jit(solution)/shard_map/ppermute | solution.py:21
  48.5 4.8 %shard_map.118.rest_0_ = bf16[2,2,2,2,128,1024]{5,4,3,2,1,0:T(8,128)(2,1)} custom-call(s32[1]{0:T(128)} %bitcast.11.core_ref, bf16[2,2,2,128,1024]{4,3,2,1,0:T(8,128)(2,1)} %bitcast.12.weights_ref, bf16[1024,512]{1,0:T(8,128)(2,1)S(1)} %get-tuple-element.29.kept_ref, bf16[1024,512]{1,0:T(8,128)(2,1)S(1)} %collective-permute-done.3.got_ref), custom_call_target="tpu_custom_call" | custom-call | flops 2147483648 | bytes 8388608 | tf_op jit(solution)/shard_map/pallas_call | solution.py:188
  53.4 4.8 %shard_map.119 = bf16[2,2,2,2,128,1024]{5,4,3,2,1,0:T(8,128)(2,1)} custom-call(s32[1]{0:T(128)} %bitcast.1.core_ref, bf16[2,2,2,128,1024]{4,3,2,1,0:T(8,128)(2,1)} %bitcast.10.weights_ref, bf16[1024,512]{1,0:T(8,128)(2,1)S(1)} %get-tuple-element.29.kept_ref, bf16[1024,512]{1,0:T(8,128)(2,1)S(1)} %collective-permute-done.3.got_ref, ...), custom_call_target="tpu_custom_call", output_to_operand_aliasing={{}: (4, {})} | custom-call | flops 2147483648 | bytes 8388608 | tf_op jit(solution)/shard_map/pallas_call | solution.py:188
  62.9 2.6 %collective-permute-start.10 = (bf16[64,512]{1,0:T(8,128)(2,1)S(1)}, bf16[64,512]{1,0:T(8,128)(2,1)S(1)}, u32[]{:S(2)}, u32[]{:S(2)}) collective-permute-start(bf16[64,512]{1,0:T(8,128)(2,1)S(1)} %copy-done.15), channel_id=1, source_target_pairs={{0,130},{1,131},{2,128},{3,129},{4,134},{5,135},{6,132},{7,133},{8... | collective-permute-start | bytes 196616 | tf_op jit(solution)/shard_map/ppermute | solution.py:21
  67.0 3.2 %collective-permute-done.8 = bf16[64,512]{1,0:T(8,128)(2,1)S(1)} collective-permute-done((bf16[64,512]{1,0:T(8,128)(2,1)S(1)}, bf16[64,512]{1,0:T(8,128)(2,1)S(1)}, u32[]{:S(2)}, u32[]{:S(2)}) %collective-permute-start.8) | collective-permute-done | bytes 65568 | tf_op jit(solution)/shard_map/ppermute | solution.py:21
  71.6 27.5 %all_to_all.25 = bf16[4,2,128,1024]{3,2,1,0:T(8,128)(2,1)S(1)} all-to-all(bf16[4,2,128,1024]{3,2,1,0:T(8,128)(2,1)S(1)} %broadcast_in_dim.5), channel_id=1, replica_groups={{0,4,8,12},{1,5,9,13},{2,6,10,14},{3,7,11,15},{16,20,24,28},{17,21,25,2..., dimensions={0} | all-to-all | bytes 4194304 | tf_op jit(solution)/shard_map/all_to_all | solution.py:162
  99.1 2.4 %shard_map.120.rest_0_ = bf16[2,2,2,2,64,1024]{5,4,3,2,1,0:T(8,128)(2,1)} custom-call(s32[1]{0:T(128)} %bitcast.11.core_ref, bf16[2,2,2,128,1024]{4,3,2,1,0:T(8,128)(2,1)S(1)} %bitcast.61, bf16[1024,512]{1,0:T(8,128)(2,1)S(1)} %get-tuple-element.29.kept_ref, bf16[1024,512]{1,0:T(8,128)(2,1)S(1)} %collective-permute-done.3.got_ref), custom_call_target="tpu_custom_call" | custom-call | flops 1073741824 | bytes 8388608 | tf_op jit(solution)/shard_map/pallas_call | solution.py:188
  103.3 2.4 %shard_map.121 = bf16[2,2,2,2,64,1024]{5,4,3,2,1,0:T(8,128)(2,1)} custom-call(s32[1]{0:T(128)} %bitcast.1.core_ref, bf16[2,2,2,128,1024]{4,3,2,1,0:T(8,128)(2,1)S(1)} %bitcast.62, bf16[1024,512]{1,0:T(8,128)(2,1)S(1)} %get-tuple-element.29.kept_ref, bf16[1024,512]{1,0:T(8,128)(2,1)S(1)} %collective-permute-done.3.got_ref, ...), custom_call_target="tpu_custom_call", output_to_operand_aliasing={{}: (4, {})} | custom-call | flops 1073741824 | bytes 8388608 | tf_op jit(solution)/shard_map/pallas_call | solution.py:188
  106.9 12.8 %all_to_all.26 = bf16[16,4,2048]{2,1,0:T(4,128)(2,1)S(1)} all-to-all(bf16[16,4,2048]{2,1,0:T(4,128)(2,1)S(1)} %reshape.110), channel_id=1, replica_groups=mesh['fsdp'=16,'ctx'=16] {'ctx'}, dimensions={0} | all-to-all | bytes 524288 | tf_op jit(solution)/shard_map/all_to_all | solution.py:322
  123.7 12.3 %all_to_all.27 = bf16[32,4,1024]{2,1,0:T(4,128)(2,1)S(1)} all-to-all(bf16[32,4,1024]{2,1,0:T(4,128)(2,1)S(1)} %bitcast.71), channel_id=1, replica_groups={{0,128,1,129,2,130,3,131,4,132,5,133,6,134,7,135,8,136,9,137,10,138,11,..., dimensions={0} | all-to-all | bytes 524288 | tf_op jit(solution)/shard_map/all_to_all | solution.py:338
  138.2 5.3 %all-to-all-start.4 = ((bf16[32,4,1024]{2,1,0:T(4,128)(2,1)}), bf16[32,4,1024]{2,1,0:T(4,128)(2,1)S(1)}, u32[]{:S(2)}, u32[]{:S(2)}) async-start(bf16[32,4,1024]{2,1,0:T(4,128)(2,1)} %copy.25), calls=%async_computation.6 | async-start | bytes 524288 | tf_op jit(solution)/shard_map/all_to_all | solution.py:338
  143.7 7.1 %all-to-all-done.4 = bf16[32,4,1024]{2,1,0:T(4,128)(2,1)S(1)} async-done(((bf16[32,4,1024]{2,1,0:T(4,128)(2,1)}), bf16[32,4,1024]{2,1,0:T(4,128)(2,1)S(1)}, u32[]{:S(2)}, u32[]{:S(2)}) %all-to-all-start.4) | async-done | bytes 262176 | tf_op jit(solution)/shard_map/all_to_all | solution.py:338
  153.0 6.2 %reduce-scatter.3.cloned.1.call-done = bf16[128,1024]{1,0:T(8,128)(2,1)} async-done(((bf16[1024,1024]{1,0:T(8,128)(2,1)}), bf16[128,1024]{1,0:T(8,128)(2,1)}) %reduce-scatter.3.cloned.1.call-update) | async-done | bytes 262160 | tf_op jit(solution)/shard_map/reduce_scatter | solution.py:277
  170.2 3.2 %collective-permute-start.17 = (bf16[128,1024]{1,0:T(8,128)(2,1)}, bf16[128,1024]{1,0:T(8,128)(2,1)S(1)}, u32[]{:S(2)}, u32[]{:S(2)}) collective-permute-start(bf16[128,1024]{1,0:T(8,128)(2,1)} %collective-permute-done.15), channel_id=1, source_target_pairs={{0,112},{1,113},{2,114},{3,115},{4,116},{5,117},{6,118},{7,119},{8... | collective-permute-start | bytes 786440 | tf_op jit(solution)/shard_map/ppermute | solution.py:35
  176.8 2.6 %collective-permute-done.16 = bf16[128,1024]{1,0:T(8,128)(2,1)S(1)} collective-permute-done((bf16[128,1024]{1,0:T(8,128)(2,1)}, bf16[128,1024]{1,0:T(8,128)(2,1)S(1)}, u32[]{:S(2)}, u32[]{:S(2)}) %collective-permute-start.16) | collective-permute-done | bytes 262176 | tf_op jit(solution)/shard_map/ppermute | solution.py:35
  179.4 3.6 %collective-permute-start.19 = (bf16[128,1024]{1,0:T(8,128)(2,1)S(1)}, bf16[128,1024]{1,0:T(8,128)(2,1)S(1)}, u32[]{:S(2)}, u32[]{:S(2)}) collective-permute-start(bf16[128,1024]{1,0:T(8,128)(2,1)S(1)} %collective-permute-done.17), channel_id=1, source_target_pairs={{0,112},{1,113},{2,114},{3,115},{4,116},{5,117},{6,118},{7,119},{8... | collective-permute-start | bytes 786440 | tf_op jit(solution)/shard_map/ppermute | solution.py:35
  184.0 7.5 %collective-permute-done.18 = bf16[128,1024]{1,0:T(8,128)(2,1)S(1)} collective-permute-done((bf16[128,1024]{1,0:T(8,128)(2,1)S(1)}, bf16[128,1024]{1,0:T(8,128)(2,1)S(1)}, u32[]{:S(2)}, u32[]{:S(2)}) %collective-permute-start.18) | collective-permute-done | bytes 262176 | tf_op jit(solution)/shard_map/ppermute | solution.py:35
  191.6 3.3 %collective-permute-start.21 = (bf16[64,1024]{1,0:T(8,128)(2,1)S(1)}, bf16[64,1024]{1,0:T(8,128)(2,1)S(1)}, u32[]{:S(2)}, u32[]{:S(2)}) collective-permute-start(bf16[64,1024]{1,0:T(8,128)(2,1)S(1)} %slice.52), channel_id=1, source_target_pairs={{0,112},{1,113},{2,114},{3,115},{4,116},{5,117},{6,118},{7,119},{8... | collective-permute-start | bytes 393224 | tf_op jit(solution)/shard_map/ppermute | solution.py:35
  194.9 4.4 %collective-permute-done.20 = bf16[64,1024]{1,0:T(8,128)(2,1)S(1)} collective-permute-done((bf16[64,1024]{1,0:T(8,128)(2,1)S(1)}, bf16[64,1024]{1,0:T(8,128)(2,1)S(1)}, u32[]{:S(2)}, u32[]{:S(2)}) %collective-permute-start.20) | collective-permute-done | bytes 131104 | tf_op jit(solution)/shard_map/ppermute | solution.py:35
  201.5 2.5 %shard_map.124.rest_1_ = bf16[2048,512]{1,0:T(8,128)(2,1)} custom-call(s32[1]{0:T(128)} %bitcast.y_lo_ref, bf16[1024,1024]{1,0:T(8,128)(2,1)S(1)} %constant_dynamic-update-slice_fusion.values_ref, bf16[1024,1024]{1,0:T(8,128)(2,1)S(1)} %bitcast.59), custom_call_target="tpu_custom_call" | custom-call | flops 536870912 | bytes 3145728 | tf_op jit(solution)/shard_map/pallas_call | solution.py:255
  204.0 5.4 %collective-permute-done.22.rest_0_ = bf16[512,512]{1,0:T(8,128)(2,1)S(1)} collective-permute-done((bf16[512,512]{1,0:T(8,128)(2,1)S(1)}, bf16[512,512]{1,0:T(8,128)(2,1)S(1)}, u32[]{:S(2)}, u32[]{:S(2)}) %collective-permute-start.22) | collective-permute-done | bytes 524320 | tf_op jit(solution)/shard_map/ppermute | solution.py:21
  (125 shorter events, 50.7 us)
Async XLA Ops:
  7.5 10.2 %collective-permute-start.2 = (bf16[2,64,512]{2,1,0:T(8,128)(2,1)S(1)}, bf16[2,64,512]{2,1,0:T(8,128)(2,1)S(1)}, u32[]{:S(2)}, u32[]{:S(2)}) collective-permute-start(bf16[2,64,512]{2,1,0:T(8,128)(2,1)S(1)} %slice.44), channel_id=1, source_target_pairs={{0,130},{1,131},{2,128},{3,129},{4,134},{5,135},{6,132},{7,133},{8... | collective-permute-start | bytes 393224 | tf_op jit(solution)/shard_map/ppermute | solution.py:21
  10.6 7.9 %collective-permute-start.1 = (bf16[2,64,512]{2,1,0:T(8,128)(2,1)S(1)}, bf16[2,64,512]{2,1,0:T(8,128)(2,1)S(1)}, u32[]{:S(2)}, u32[]{:S(2)}) collective-permute-start(bf16[2,64,512]{2,1,0:T(8,128)(2,1)S(1)} %slice.44), channel_id=1, source_target_pairs={{0,2},{1,3},{2,0},{3,1},{4,6},{5,7},{6,4},{7,5},{8,10},{9,11},{10,... | collective-permute-start | bytes 393224 | tf_op jit(solution)/shard_map/ppermute | solution.py:21
  11.2 6.4 %collective-permute-start = (bf16[2,64,512]{2,1,0:T(8,128)(2,1)S(1)}, bf16[2,64,512]{2,1,0:T(8,128)(2,1)S(1)}, u32[]{:S(2)}, u32[]{:S(2)}) collective-permute-start(bf16[2,64,512]{2,1,0:T(8,128)(2,1)S(1)} %slice.44), channel_id=1, source_target_pairs={{0,128},{1,129},{2,130},{3,131},{4,132},{5,133},{6,134},{7,135},{8... | collective-permute-start | bytes 393224 | tf_op jit(solution)/shard_map/ppermute | solution.py:21
  20.1 28.4 %all-to-all-start = ((bf16[4,2,2,64,1024]{4,3,2,1,0:T(8,128)(2,1)}), bf16[4,2,2,64,1024]{4,3,2,1,0:T(8,128)(2,1)}, u32[]{:S(2)}, u32[]{:S(2)}) async-start(bf16[4,2,2,64,1024]{4,3,2,1,0:T(8,128)(2,1)} %broadcast_in_dim.4), calls=%async_computation | async-start | bytes 4194304 | tf_op jit(solution)/shard_map/all_to_all | solution.py:162
  25.2 95.3 %reduce-scatter.5.cloned.1.call-start = ((), (), s32[]{:S(2)}) async-start(), calls=%async_computation.8 | async-start | bytes 4718592 | tf_op jit(solution)/shard_map/reduce_scatter | solution.py:277
  25.2 22.8 %collective-permute-start.3 = (bf16[1024,512]{1,0:T(8,128)(2,1)S(1)}, bf16[1024,512]{1,0:T(8,128)(2,1)S(1)}, u32[]{:S(2)}, u32[]{:S(2)}) collective-permute-start(bf16[1024,512]{1,0:T(8,128)(2,1)S(1)} %get-tuple-element.30), channel_id=1, source_target_pairs={{0,128},{1,129},{2,130},{3,131},{4,132},{5,133},{6,134},{7,135},{8... | collective-permute-start | bytes 3145736 | tf_op jit(solution)/shard_map/ppermute | solution.py:21
  25.8 22.2 %collective-permute-start.4 = (f32[64]{0:T(128)S(1)}, f32[64]{0:T(128)S(1)}, u32[]{:S(2)}, u32[]{:S(2)}) collective-permute-start(f32[64]{0:T(128)S(1)} %copy-done.16), channel_id=1, source_target_pairs={{0,128},{1,129},{2,130},{3,131},{4,132},{5,133},{6,134},{7,135},{8... | collective-permute-start | bytes 776 | tf_op jit(solution)/shard_map/ppermute | solution.py:21
  58.2 101.0 %reduce-scatter.3.cloned.1.call-start = ((), (), s32[]{:S(2)}) async-start(), calls=%async_computation.7 | async-start | bytes 2359296 | tf_op jit(solution)/shard_map/reduce_scatter | solution.py:277
  58.2 7.6 %collective-permute-start.5 = (bf16[64,512]{1,0:T(8,128)(2,1)S(1)}, bf16[64,512]{1,0:T(8,128)(2,1)S(1)}, u32[]{:S(2)}, u32[]{:S(2)}) collective-permute-start(bf16[64,512]{1,0:T(8,128)(2,1)S(1)} %slice_bitcast_fusion), channel_id=1, source_target_pairs={{0,128},{1,129},{2,130},{3,131},{4,132},{5,133},{6,134},{7,135},{8... | collective-permute-start | bytes 196616 | tf_op jit(solution)/shard_map/ppermute | solution.py:21
  59.7 10.5 %collective-permute-start.7 = (bf16[64,512]{1,0:T(8,128)(2,1)S(1)}, bf16[64,512]{1,0:T(8,128)(2,1)S(1)}, u32[]{:S(2)}, u32[]{:S(2)}) collective-permute-start(bf16[64,512]{1,0:T(8,128)(2,1)S(1)} %slice_bitcast_fusion), channel_id=1, source_target_pairs={{0,130},{1,131},{2,128},{3,129},{4,134},{5,135},{6,132},{7,133},{8... | collective-permute-start | bytes 196616 | tf_op jit(solution)/shard_map/ppermute | solution.py:21
  61.8 8.4 %collective-permute-start.6 = (bf16[64,512]{1,0:T(8,128)(2,1)S(1)}, bf16[64,512]{1,0:T(8,128)(2,1)S(1)}, u32[]{:S(2)}, u32[]{:S(2)}) collective-permute-start(bf16[64,512]{1,0:T(8,128)(2,1)S(1)} %slice_bitcast_fusion), channel_id=1, source_target_pairs={{0,2},{1,3},{2,0},{3,1},{4,6},{5,7},{6,4},{7,5},{8,10},{9,11},{10,... | collective-permute-start | bytes 196616 | tf_op jit(solution)/shard_map/ppermute | solution.py:21
  62.9 7.3 %collective-permute-start.10 = (bf16[64,512]{1,0:T(8,128)(2,1)S(1)}, bf16[64,512]{1,0:T(8,128)(2,1)S(1)}, u32[]{:S(2)}, u32[]{:S(2)}) collective-permute-start(bf16[64,512]{1,0:T(8,128)(2,1)S(1)} %copy-done.15), channel_id=1, source_target_pairs={{0,130},{1,131},{2,128},{3,129},{4,134},{5,135},{6,132},{7,133},{8... | collective-permute-start | bytes 196616 | tf_op jit(solution)/shard_map/ppermute | solution.py:21
  65.5 5.8 %collective-permute-start.9 = (bf16[64,512]{1,0:T(8,128)(2,1)S(1)}, bf16[64,512]{1,0:T(8,128)(2,1)S(1)}, u32[]{:S(2)}, u32[]{:S(2)}) collective-permute-start(bf16[64,512]{1,0:T(8,128)(2,1)S(1)} %copy-done.15), channel_id=1, source_target_pairs={{0,2},{1,3},{2,0},{3,1},{4,6},{5,7},{6,4},{7,5},{8,10},{9,11},{10,... | collective-permute-start | bytes 196616 | tf_op jit(solution)/shard_map/ppermute | solution.py:21
  138.2 12.7 %all-to-all-start.4 = ((bf16[32,4,1024]{2,1,0:T(4,128)(2,1)}), bf16[32,4,1024]{2,1,0:T(4,128)(2,1)S(1)}, u32[]{:S(2)}, u32[]{:S(2)}) async-start(bf16[32,4,1024]{2,1,0:T(4,128)(2,1)} %copy.25), calls=%async_computation.6 | async-start | bytes 524288 | tf_op jit(solution)/shard_map/all_to_all | solution.py:338
  143.5 65.8 %all-gather.2.cloned.1.call-start = ((), (), s32[]{:S(2)}) async-start(), calls=%async_computation.9 | async-start | bytes 1179648 | tf_op jit(solution)/shard_map/all_gather | solution.py:369
  160.3 9.8 %collective-permute-start.14 = (bf16[128,1024]{1,0:T(8,128)(2,1)S(1)}, bf16[128,1024]{1,0:T(8,128)(2,1)}, u32[]{:S(2)}, u32[]{:S(2)}) collective-permute-start(bf16[128,1024]{1,0:T(8,128)(2,1)S(1)} %get-tuple-element.32), channel_id=1, source_target_pairs={{0,16},{1,17},{2,18},{3,19},{4,20},{5,21},{6,22},{7,23},{8,24},{9,... | collective-permute-start | bytes 786440 | tf_op jit(solution)/shard_map/ppermute | solution.py:35
  161.6 8.6 %collective-permute-start.15 = (bf16[128,1024]{1,0:T(8,128)(2,1)S(1)}, bf16[128,1024]{1,0:T(8,128)(2,1)}, u32[]{:S(2)}, u32[]{:S(2)}) collective-permute-start(bf16[128,1024]{1,0:T(8,128)(2,1)S(1)} %get-tuple-element.32), channel_id=1, source_target_pairs={{0,112},{1,113},{2,114},{3,115},{4,116},{5,117},{6,118},{7,119},{8... | collective-permute-start | bytes 786440 | tf_op jit(solution)/shard_map/ppermute | solution.py:35
  170.1 9.2 %collective-permute-start.16 = (bf16[128,1024]{1,0:T(8,128)(2,1)}, bf16[128,1024]{1,0:T(8,128)(2,1)S(1)}, u32[]{:S(2)}, u32[]{:S(2)}) collective-permute-start(bf16[128,1024]{1,0:T(8,128)(2,1)} %collective-permute-done.14), channel_id=1, source_target_pairs={{0,16},{1,17},{2,18},{3,19},{4,20},{5,21},{6,22},{7,23},{8,24},{9,... | collective-permute-start | bytes 786440 | tf_op jit(solution)/shard_map/ppermute | solution.py:35
  170.2 9.1 %collective-permute-start.17 = (bf16[128,1024]{1,0:T(8,128)(2,1)}, bf16[128,1024]{1,0:T(8,128)(2,1)S(1)}, u32[]{:S(2)}, u32[]{:S(2)}) collective-permute-start(bf16[128,1024]{1,0:T(8,128)(2,1)} %collective-permute-done.15), channel_id=1, source_target_pairs={{0,112},{1,113},{2,114},{3,115},{4,116},{5,117},{6,118},{7,119},{8... | collective-permute-start | bytes 786440 | tf_op jit(solution)/shard_map/ppermute | solution.py:35
  179.4 12.1 %collective-permute-start.18 = (bf16[128,1024]{1,0:T(8,128)(2,1)S(1)}, bf16[128,1024]{1,0:T(8,128)(2,1)S(1)}, u32[]{:S(2)}, u32[]{:S(2)}) collective-permute-start(bf16[128,1024]{1,0:T(8,128)(2,1)S(1)} %collective-permute-done.16), channel_id=1, source_target_pairs={{0,16},{1,17},{2,18},{3,19},{4,20},{5,21},{6,22},{7,23},{8,24},{9,... | collective-permute-start | bytes 786440 | tf_op jit(solution)/shard_map/ppermute | solution.py:35
  179.4 12.2 %collective-permute-start.19 = (bf16[128,1024]{1,0:T(8,128)(2,1)S(1)}, bf16[128,1024]{1,0:T(8,128)(2,1)S(1)}, u32[]{:S(2)}, u32[]{:S(2)}) collective-permute-start(bf16[128,1024]{1,0:T(8,128)(2,1)S(1)} %collective-permute-done.17), channel_id=1, source_target_pairs={{0,112},{1,113},{2,114},{3,115},{4,116},{5,117},{6,118},{7,119},{8... | collective-permute-start | bytes 786440 | tf_op jit(solution)/shard_map/ppermute | solution.py:35
  191.5 7.8 %collective-permute-start.20 = (bf16[64,1024]{1,0:T(8,128)(2,1)S(1)}, bf16[64,1024]{1,0:T(8,128)(2,1)S(1)}, u32[]{:S(2)}, u32[]{:S(2)}) collective-permute-start(bf16[64,1024]{1,0:T(8,128)(2,1)S(1)} %slice.51), channel_id=1, source_target_pairs={{0,16},{1,17},{2,18},{3,19},{4,20},{5,21},{6,22},{7,23},{8,24},{9,... | collective-permute-start | bytes 393224 | tf_op jit(solution)/shard_map/ppermute | solution.py:35
  191.6 7.7 %collective-permute-start.21 = (bf16[64,1024]{1,0:T(8,128)(2,1)S(1)}, bf16[64,1024]{1,0:T(8,128)(2,1)S(1)}, u32[]{:S(2)}, u32[]{:S(2)}) collective-permute-start(bf16[64,1024]{1,0:T(8,128)(2,1)S(1)} %slice.52), channel_id=1, source_target_pairs={{0,112},{1,113},{2,114},{3,115},{4,116},{5,117},{6,118},{7,119},{8... | collective-permute-start | bytes 393224 | tf_op jit(solution)/shard_map/ppermute | solution.py:35
  200.1 9.3 %collective-permute-start.22 = (bf16[512,512]{1,0:T(8,128)(2,1)S(1)}, bf16[512,512]{1,0:T(8,128)(2,1)S(1)}, u32[]{:S(2)}, u32[]{:S(2)}) collective-permute-start(bf16[512,512]{1,0:T(8,128)(2,1)S(1)} %convolution_convert_fusion), channel_id=1, source_target_pairs={{0,128},{1,129},{2,130},{3,131},{4,132},{5,133},{6,134},{7,135},{8... | collective-permute-start | bytes 1572872 | tf_op jit(solution)/shard_map/ppermute | solution.py:21
  (21 other events, 173.5 us)
Sparse Core Ops, SparseCore 0:
  58.3 57.6 reduce-scatter.4
  118.6 40.5 reduce-scatter.2
  170.2 37.9 all-gather.1

commit v5 on v4

--- a/solution.py
+++ b/solution.py
@@ -291,7 +291,7 @@
 
     shards = in_proj.transpose(0, 2, 1)
     given = lax.dynamic_slice_in_dim(tokens, (1 - y_lo) * half, half, 0)
-    column = after(gather_y(shards[1:3], y_hi), given)
+    column = gather_y(shards[1:3], y_hi)
 
     plane = gather_x(column)
     got = flip(given, FLIP_Y_LO)

time: 221 us -> 223 us (level)
  no operation moved by 1% of the time
where the time goes in v5:
time: 223 us; the launch traced here: 222 us
  waiting for transfers between devices  65.5 us (29%)
  blocking collectives  53.1 us (24%)
  starting transfers between devices  42.5 us (19%)
  local copies, waits for them, and re-layouts  20.5 us (9%)
  Pallas kernels  20.5 us (9%)
  between operations  13.6 us (6%)
  other arithmetic  5.39 us (2%)
    ppermute x15, waiting for transfers between devices, flip(): return lax.ppermute(array, AXES, [(i, i ^ mask) for i in range(256)])  37.7 us
    all_to_all x1, blocking collectives, gather_x(): lax.all_to_all(copies, AXES, split_axis=0, concat_axis=0, tiled=True, axi...  27.8 us
    ppermute x15, starting transfers between devices, flip(): return lax.ppermute(array, AXES, [(i, i ^ mask) for i in range(256)])  18.3 us
    pallas_call x4, Pallas kernels, product(): pl.pallas_call(product_kernel, grid_spec=pltpu.PrefetchScalarGridSpec(num...  14.4 us
    ppermute x8, waiting for transfers between devices, along_z(): return lax.ppermute(array, AXES, pairs)  14.1 us
    ppermute x8, starting transfers between devices, along_z(): return lax.ppermute(array, AXES, pairs)  13.6 us
    all_to_all x1, blocking collectives, local(): lax.all_to_all(taps.reshape(16, 4, 2048), 'ctx', split_axis=0, concat_axi...  12.9 us
    all_to_all x1, blocking collectives, to_plane(): lax.all_to_all(array, AXES, split_axis=0, concat_axis=0, tiled=True, axis...  12.3 us
  transfers between devices with their start and end apart: 28, of which 14 were waited for; matrix products, arithmetic and copies ran while one was open for 8% of the time, Pallas kernels for 6%

profile of v5, /device:TPU:2, one launch (start us, length us, event | category | flops | bytes accessed | tf_op | source)
XLA Modules:
  0.0 221.7 jit_solution(9518577431097074975)
XLA Ops:
  9.1 2.2 collective-permute-start.2
  12.8 3.8 %collective-permute-done.2 = bf16[2,64,512]{2,1,0:T(8,128)(2,1)S(1)} collective-permute-done((bf16[2,64,512]{2,1,0:T(8,128)(2,1)S(1)}, bf16[2,64,512]{2,1,0:T(8,128)(2,1)S(1)}, u32[]{:S(2)}, u32[]{:S(2)}) %collective-permute-start.2) | collective-permute-done | bytes 131104 | tf_op jit(solution)/shard_map/ppermute | solution.py:21
  19.8 5.2 %all-to-all-start = ((bf16[4,2,2,64,1024]{4,3,2,1,0:T(8,128)(2,1)}), bf16[4,2,2,64,1024]{4,3,2,1,0:T(8,128)(2,1)}, u32[]{:S(2)}, u32[]{:S(2)}) async-start(bf16[4,2,2,64,1024]{4,3,2,1,0:T(8,128)(2,1)} %broadcast_in_dim.4), calls=%async_computation | async-start | bytes 4194304 | tf_op jit(solution)/shard_map/all_to_all | solution.py:162
  29.7 20.6 %collective-permute-done.4 = f32[64]{0:T(128)S(1)} collective-permute-done((f32[64]{0:T(128)S(1)}, f32[64]{0:T(128)S(1)}, u32[]{:S(2)}, u32[]{:S(2)}) %collective-permute-start.4) | collective-permute-done | bytes 288 | tf_op jit(solution)/shard_map/ppermute | solution.py:21
  50.3 4.9 %shard_map.118.rest_0_ = bf16[2,2,2,2,128,1024]{5,4,3,2,1,0:T(8,128)(2,1)} custom-call(s32[1]{0:T(128)} %bitcast.11.core_ref, bf16[2,2,2,128,1024]{4,3,2,1,0:T(8,128)(2,1)} %bitcast.12.weights_ref, bf16[1024,512]{1,0:T(8,128)(2,1)S(1)} %get-tuple-element.27.kept_ref, bf16[1024,512]{1,0:T(8,128)(2,1)S(1)} %collective-permute-done.3.got_ref), custom_call_target="tpu_custom_call" | custom-call | flops 2147483648 | bytes 8388608 | tf_op jit(solution)/shard_map/pallas_call | solution.py:188
  55.2 4.8 %shard_map.119 = bf16[2,2,2,2,128,1024]{5,4,3,2,1,0:T(8,128)(2,1)} custom-call(s32[1]{0:T(128)} %bitcast.1.core_ref, bf16[2,2,2,128,1024]{4,3,2,1,0:T(8,128)(2,1)} %bitcast.10.weights_ref, bf16[1024,512]{1,0:T(8,128)(2,1)S(1)} %get-tuple-element.27.kept_ref, bf16[1024,512]{1,0:T(8,128)(2,1)S(1)} %collective-permute-done.3.got_ref, ...), custom_call_target="tpu_custom_call", output_to_operand_aliasing={{}: (4, {})} | custom-call | flops 2147483648 | bytes 8388608 | tf_op jit(solution)/shard_map/pallas_call | solution.py:188
  60.4 2.1 collective-permute-start.7
  68.3 2.9 %collective-permute-done.8 = bf16[64,512]{1,0:T(8,128)(2,1)S(1)} collective-permute-done((bf16[64,512]{1,0:T(8,128)(2,1)S(1)}, bf16[64,512]{1,0:T(8,128)(2,1)S(1)}, u32[]{:S(2)}, u32[]{:S(2)}) %collective-permute-start.8) | collective-permute-done | bytes 65568 | tf_op jit(solution)/shard_map/ppermute | solution.py:21
  72.4 27.8 %all_to_all.25 = bf16[4,2,128,1024]{3,2,1,0:T(8,128)(2,1)S(1)} all-to-all(bf16[4,2,128,1024]{3,2,1,0:T(8,128)(2,1)S(1)} %broadcast_in_dim.5), channel_id=1, replica_groups={{0,4,8,12},{1,5,9,13},{2,6,10,14},{3,7,11,15},{16,20,24,28},{17,21,25,2..., dimensions={0} | all-to-all | bytes 4194304 | tf_op jit(solution)/shard_map/all_to_all | solution.py:162
  100.3 2.4 %shard_map.120.rest_0_ = bf16[2,2,2,2,64,1024]{5,4,3,2,1,0:T(8,128)(2,1)} custom-call(s32[1]{0:T(128)} %bitcast.11.core_ref, bf16[2,2,2,128,1024]{4,3,2,1,0:T(8,128)(2,1)S(1)} %bitcast.61, bf16[1024,512]{1,0:T(8,128)(2,1)S(1)} %get-tuple-element.27.kept_ref, bf16[1024,512]{1,0:T(8,128)(2,1)S(1)} %collective-permute-done.3.got_ref), custom_call_target="tpu_custom_call" | custom-call | flops 1073741824 | bytes 8388608 | tf_op jit(solution)/shard_map/pallas_call | solution.py:188
  104.4 2.4 %shard_map.121 = bf16[2,2,2,2,64,1024]{5,4,3,2,1,0:T(8,128)(2,1)} custom-call(s32[1]{0:T(128)} %bitcast.1.core_ref, bf16[2,2,2,128,1024]{4,3,2,1,0:T(8,128)(2,1)S(1)} %bitcast.62, bf16[1024,512]{1,0:T(8,128)(2,1)S(1)} %get-tuple-element.27.kept_ref, bf16[1024,512]{1,0:T(8,128)(2,1)S(1)} %collective-permute-done.3.got_ref, ...), custom_call_target="tpu_custom_call", output_to_operand_aliasing={{}: (4, {})} | custom-call | flops 1073741824 | bytes 8388608 | tf_op jit(solution)/shard_map/pallas_call | solution.py:188
  108.0 12.9 %all_to_all.26 = bf16[16,4,2048]{2,1,0:T(4,128)(2,1)S(1)} all-to-all(bf16[16,4,2048]{2,1,0:T(4,128)(2,1)S(1)} %reshape.142), channel_id=1, replica_groups=mesh['fsdp'=16,'ctx'=16] {'ctx'}, dimensions={0} | all-to-all | bytes 524288 | tf_op jit(solution)/shard_map/all_to_all | solution.py:322
  125.0 12.3 %all_to_all.27 = bf16[32,4,1024]{2,1,0:T(4,128)(2,1)S(1)} all-to-all(bf16[32,4,1024]{2,1,0:T(4,128)(2,1)S(1)} %bitcast.71), channel_id=1, replica_groups={{0,128,1,129,2,130,3,131,4,132,5,133,6,134,7,135,8,136,9,137,10,138,11,..., dimensions={0} | all-to-all | bytes 524288 | tf_op jit(solution)/shard_map/all_to_all | solution.py:338
  139.4 5.3 %all-to-all-start.4 = ((bf16[32,4,1024]{2,1,0:T(4,128)(2,1)}), bf16[32,4,1024]{2,1,0:T(4,128)(2,1)S(1)}, u32[]{:S(2)}, u32[]{:S(2)}) async-start(bf16[32,4,1024]{2,1,0:T(4,128)(2,1)} %copy.25), calls=%async_computation.6 | async-start | bytes 524288 | tf_op jit(solution)/shard_map/all_to_all | solution.py:338
  145.0 7.1 %all-to-all-done.4 = bf16[32,4,1024]{2,1,0:T(4,128)(2,1)S(1)} async-done(((bf16[32,4,1024]{2,1,0:T(4,128)(2,1)}), bf16[32,4,1024]{2,1,0:T(4,128)(2,1)S(1)}, u32[]{:S(2)}, u32[]{:S(2)}) %all-to-all-start.4) | async-done | bytes 262176 | tf_op jit(solution)/shard_map/all_to_all | solution.py:338
  154.2 6.4 %reduce-scatter.3.cloned.1.call-done = bf16[128,1024]{1,0:T(8,128)(2,1)} async-done(((bf16[1024,1024]{1,0:T(8,128)(2,1)}), bf16[128,1024]{1,0:T(8,128)(2,1)}) %reduce-scatter.3.cloned.1.call-update) | async-done | bytes 262160 | tf_op jit(solution)/shard_map/reduce_scatter | solution.py:277
  171.9 3.0 %collective-permute-start.17 = (bf16[128,1024]{1,0:T(8,128)(2,1)}, bf16[128,1024]{1,0:T(8,128)(2,1)S(1)}, u32[]{:S(2)}, u32[]{:S(2)}) collective-permute-start(bf16[128,1024]{1,0:T(8,128)(2,1)} %collective-permute-done.15), channel_id=1, source_target_pairs={{0,112},{1,113},{2,114},{3,115},{4,116},{5,117},{6,118},{7,119},{8... | collective-permute-start | bytes 786440 | tf_op jit(solution)/shard_map/ppermute | solution.py:35
  178.3 3.2 %collective-permute-done.16 = bf16[128,1024]{1,0:T(8,128)(2,1)S(1)} collective-permute-done((bf16[128,1024]{1,0:T(8,128)(2,1)}, bf16[128,1024]{1,0:T(8,128)(2,1)S(1)}, u32[]{:S(2)}, u32[]{:S(2)}) %collective-permute-start.16) | collective-permute-done | bytes 262176 | tf_op jit(solution)/shard_map/ppermute | solution.py:35
  181.5 3.6 %collective-permute-start.19 = (bf16[128,1024]{1,0:T(8,128)(2,1)S(1)}, bf16[128,1024]{1,0:T(8,128)(2,1)S(1)}, u32[]{:S(2)}, u32[]{:S(2)}) collective-permute-start(bf16[128,1024]{1,0:T(8,128)(2,1)S(1)} %collective-permute-done.17), channel_id=1, source_target_pairs={{0,112},{1,113},{2,114},{3,115},{4,116},{5,117},{6,118},{7,119},{8... | collective-permute-start | bytes 786440 | tf_op jit(solution)/shard_map/ppermute | solution.py:35
  186.1 6.9 %collective-permute-done.18 = bf16[128,1024]{1,0:T(8,128)(2,1)S(1)} collective-permute-done((bf16[128,1024]{1,0:T(8,128)(2,1)S(1)}, bf16[128,1024]{1,0:T(8,128)(2,1)S(1)}, u32[]{:S(2)}, u32[]{:S(2)}) %collective-permute-start.18) | collective-permute-done | bytes 262176 | tf_op jit(solution)/shard_map/ppermute | solution.py:35
  193.1 3.3 %collective-permute-start.21 = (bf16[64,1024]{1,0:T(8,128)(2,1)S(1)}, bf16[64,1024]{1,0:T(8,128)(2,1)S(1)}, u32[]{:S(2)}, u32[]{:S(2)}) collective-permute-start(bf16[64,1024]{1,0:T(8,128)(2,1)S(1)} %slice.52), channel_id=1, source_target_pairs={{0,112},{1,113},{2,114},{3,115},{4,116},{5,117},{6,118},{7,119},{8... | collective-permute-start | bytes 393224 | tf_op jit(solution)/shard_map/ppermute | solution.py:35
  196.4 4.0 %collective-permute-done.20 = bf16[64,1024]{1,0:T(8,128)(2,1)S(1)} collective-permute-done((bf16[64,1024]{1,0:T(8,128)(2,1)S(1)}, bf16[64,1024]{1,0:T(8,128)(2,1)S(1)}, u32[]{:S(2)}, u32[]{:S(2)}) %collective-permute-start.20) | collective-permute-done | bytes 131104 | tf_op jit(solution)/shard_map/ppermute | solution.py:35
  203.0 2.5 %shard_map.124.rest_1_ = bf16[2048,512]{1,0:T(8,128)(2,1)} custom-call(s32[1]{0:T(128)} %bitcast.y_lo_ref, bf16[1024,1024]{1,0:T(8,128)(2,1)S(1)} %constant_dynamic-update-slice_fusion.values_ref, bf16[1024,1024]{1,0:T(8,128)(2,1)S(1)} %bitcast.59), custom_call_target="tpu_custom_call" | custom-call | flops 536870912 | bytes 3145728 | tf_op jit(solution)/shard_map/pallas_call | solution.py:255
  205.5 5.0 %collective-permute-done.22.rest_0_ = bf16[512,512]{1,0:T(8,128)(2,1)S(1)} collective-permute-done((bf16[512,512]{1,0:T(8,128)(2,1)S(1)}, bf16[512,512]{1,0:T(8,128)(2,1)S(1)}, u32[]{:S(2)}, u32[]{:S(2)}) %collective-permute-start.22) | collective-permute-done | bytes 524320 | tf_op jit(solution)/shard_map/ppermute | solution.py:21
  (125 shorter events, 53.4 us)
Async XLA Ops:
  7.5 5.3 %collective-permute-start = (bf16[2,64,512]{2,1,0:T(8,128)(2,1)S(1)}, bf16[2,64,512]{2,1,0:T(8,128)(2,1)S(1)}, u32[]{:S(2)}, u32[]{:S(2)}) collective-permute-start(bf16[2,64,512]{2,1,0:T(8,128)(2,1)S(1)} %slice.44), channel_id=1, source_target_pairs={{0,128},{1,129},{2,130},{3,131},{4,132},{5,133},{6,134},{7,135},{8... | collective-permute-start | bytes 393224 | tf_op jit(solution)/shard_map/ppermute | solution.py:21
  9.1 7.5 %collective-permute-start.2 = (bf16[2,64,512]{2,1,0:T(8,128)(2,1)S(1)}, bf16[2,64,512]{2,1,0:T(8,128)(2,1)S(1)}, u32[]{:S(2)}, u32[]{:S(2)}) collective-permute-start(bf16[2,64,512]{2,1,0:T(8,128)(2,1)S(1)} %slice.44), channel_id=1, source_target_pairs={{0,130},{1,131},{2,128},{3,129},{4,134},{5,135},{6,132},{7,133},{8... | collective-permute-start | bytes 393224 | tf_op jit(solution)/shard_map/ppermute | solution.py:21
  11.3 6.8 %collective-permute-start.1 = (bf16[2,64,512]{2,1,0:T(8,128)(2,1)S(1)}, bf16[2,64,512]{2,1,0:T(8,128)(2,1)S(1)}, u32[]{:S(2)}, u32[]{:S(2)}) collective-permute-start(bf16[2,64,512]{2,1,0:T(8,128)(2,1)S(1)} %slice.44), channel_id=1, source_target_pairs={{0,2},{1,3},{2,0},{3,1},{4,6},{5,7},{6,4},{7,5},{8,10},{9,11},{10,... | collective-permute-start | bytes 393224 | tf_op jit(solution)/shard_map/ppermute | solution.py:21
  19.8 30.5 %all-to-all-start = ((bf16[4,2,2,64,1024]{4,3,2,1,0:T(8,128)(2,1)}), bf16[4,2,2,64,1024]{4,3,2,1,0:T(8,128)(2,1)}, u32[]{:S(2)}, u32[]{:S(2)}) async-start(bf16[4,2,2,64,1024]{4,3,2,1,0:T(8,128)(2,1)} %broadcast_in_dim.4), calls=%async_computation | async-start | bytes 4194304 | tf_op jit(solution)/shard_map/all_to_all | solution.py:162
  25.0 96.8 %reduce-scatter.5.cloned.1.call-start = ((), (), s32[]{:S(2)}) async-start(), calls=%async_computation.8 | async-start | bytes 4718592 | tf_op jit(solution)/shard_map/reduce_scatter | solution.py:277
  26.7 23.6 %collective-permute-start.3 = (bf16[1024,512]{1,0:T(8,128)(2,1)S(1)}, bf16[1024,512]{1,0:T(8,128)(2,1)S(1)}, u32[]{:S(2)}, u32[]{:S(2)}) collective-permute-start(bf16[1024,512]{1,0:T(8,128)(2,1)S(1)} %get-tuple-element.28), channel_id=1, source_target_pairs={{0,128},{1,129},{2,130},{3,131},{4,132},{5,133},{6,134},{7,135},{8... | collective-permute-start | bytes 3145736 | tf_op jit(solution)/shard_map/ppermute | solution.py:21
  27.5 22.8 %collective-permute-start.4 = (f32[64]{0:T(128)S(1)}, f32[64]{0:T(128)S(1)}, u32[]{:S(2)}, u32[]{:S(2)}) collective-permute-start(f32[64]{0:T(128)S(1)} %copy-done.16), channel_id=1, source_target_pairs={{0,128},{1,129},{2,130},{3,131},{4,132},{5,133},{6,134},{7,135},{8... | collective-permute-start | bytes 776 | tf_op jit(solution)/shard_map/ppermute | solution.py:21
  60.0 100.7 %reduce-scatter.3.cloned.1.call-start = ((), (), s32[]{:S(2)}) async-start(), calls=%async_computation.7 | async-start | bytes 2359296 | tf_op jit(solution)/shard_map/reduce_scatter | solution.py:277
  60.0 6.5 %collective-permute-start.5 = (bf16[64,512]{1,0:T(8,128)(2,1)S(1)}, bf16[64,512]{1,0:T(8,128)(2,1)S(1)}, u32[]{:S(2)}, u32[]{:S(2)}) collective-permute-start(bf16[64,512]{1,0:T(8,128)(2,1)S(1)} %slice_bitcast_fusion), channel_id=1, source_target_pairs={{0,128},{1,129},{2,130},{3,131},{4,132},{5,133},{6,134},{7,135},{8... | collective-permute-start | bytes 196616 | tf_op jit(solution)/shard_map/ppermute | solution.py:21
  60.4 10.9 %collective-permute-start.7 = (bf16[64,512]{1,0:T(8,128)(2,1)S(1)}, bf16[64,512]{1,0:T(8,128)(2,1)S(1)}, u32[]{:S(2)}, u32[]{:S(2)}) collective-permute-start(bf16[64,512]{1,0:T(8,128)(2,1)S(1)} %slice_bitcast_fusion), channel_id=1, source_target_pairs={{0,130},{1,131},{2,128},{3,129},{4,134},{5,135},{6,132},{7,133},{8... | collective-permute-start | bytes 196616 | tf_op jit(solution)/shard_map/ppermute | solution.py:21
  62.4 8.8 %collective-permute-start.6 = (bf16[64,512]{1,0:T(8,128)(2,1)S(1)}, bf16[64,512]{1,0:T(8,128)(2,1)S(1)}, u32[]{:S(2)}, u32[]{:S(2)}) collective-permute-start(bf16[64,512]{1,0:T(8,128)(2,1)S(1)} %slice_bitcast_fusion), channel_id=1, source_target_pairs={{0,2},{1,3},{2,0},{3,1},{4,6},{5,7},{6,4},{7,5},{8,10},{9,11},{10,... | collective-permute-start | bytes 196616 | tf_op jit(solution)/shard_map/ppermute | solution.py:21
  64.2 7.1 %collective-permute-start.10 = (bf16[64,512]{1,0:T(8,128)(2,1)S(1)}, bf16[64,512]{1,0:T(8,128)(2,1)S(1)}, u32[]{:S(2)}, u32[]{:S(2)}) collective-permute-start(bf16[64,512]{1,0:T(8,128)(2,1)S(1)} %copy-done.15), channel_id=1, source_target_pairs={{0,130},{1,131},{2,128},{3,129},{4,134},{5,135},{6,132},{7,133},{8... | collective-permute-start | bytes 196616 | tf_op jit(solution)/shard_map/ppermute | solution.py:21
  66.3 5.8 %collective-permute-start.9 = (bf16[64,512]{1,0:T(8,128)(2,1)S(1)}, bf16[64,512]{1,0:T(8,128)(2,1)S(1)}, u32[]{:S(2)}, u32[]{:S(2)}) collective-permute-start(bf16[64,512]{1,0:T(8,128)(2,1)S(1)} %copy-done.15), channel_id=1, source_target_pairs={{0,2},{1,3},{2,0},{3,1},{4,6},{5,7},{6,4},{7,5},{8,10},{9,11},{10,... | collective-permute-start | bytes 196616 | tf_op jit(solution)/shard_map/ppermute | solution.py:21
  139.4 12.7 %all-to-all-start.4 = ((bf16[32,4,1024]{2,1,0:T(4,128)(2,1)}), bf16[32,4,1024]{2,1,0:T(4,128)(2,1)S(1)}, u32[]{:S(2)}, u32[]{:S(2)}) async-start(bf16[32,4,1024]{2,1,0:T(4,128)(2,1)} %copy.25), calls=%async_computation.6 | async-start | bytes 524288 | tf_op jit(solution)/shard_map/all_to_all | solution.py:338
  144.8 65.8 %all-gather.2.cloned.1.call-start = ((), (), s32[]{:S(2)}) async-start(), calls=%async_computation.9 | async-start | bytes 1179648 | tf_op jit(solution)/shard_map/all_gather | solution.py:369
  161.8 9.8 %collective-permute-start.14 = (bf16[128,1024]{1,0:T(8,128)(2,1)S(1)}, bf16[128,1024]{1,0:T(8,128)(2,1)}, u32[]{:S(2)}, u32[]{:S(2)}) collective-permute-start(bf16[128,1024]{1,0:T(8,128)(2,1)S(1)} %get-tuple-element.30), channel_id=1, source_target_pairs={{0,16},{1,17},{2,18},{3,19},{4,20},{5,21},{6,22},{7,23},{8,24},{9,... | collective-permute-start | bytes 786440 | tf_op jit(solution)/shard_map/ppermute | solution.py:35
  163.3 8.6 %collective-permute-start.15 = (bf16[128,1024]{1,0:T(8,128)(2,1)S(1)}, bf16[128,1024]{1,0:T(8,128)(2,1)}, u32[]{:S(2)}, u32[]{:S(2)}) collective-permute-start(bf16[128,1024]{1,0:T(8,128)(2,1)S(1)} %get-tuple-element.30), channel_id=1, source_target_pairs={{0,112},{1,113},{2,114},{3,115},{4,116},{5,117},{6,118},{7,119},{8... | collective-permute-start | bytes 786440 | tf_op jit(solution)/shard_map/ppermute | solution.py:35
  171.6 9.8 %collective-permute-start.16 = (bf16[128,1024]{1,0:T(8,128)(2,1)}, bf16[128,1024]{1,0:T(8,128)(2,1)S(1)}, u32[]{:S(2)}, u32[]{:S(2)}) collective-permute-start(bf16[128,1024]{1,0:T(8,128)(2,1)} %collective-permute-done.14), channel_id=1, source_target_pairs={{0,16},{1,17},{2,18},{3,19},{4,20},{5,21},{6,22},{7,23},{8,24},{9,... | collective-permute-start | bytes 786440 | tf_op jit(solution)/shard_map/ppermute | solution.py:35
  171.9 9.6 %collective-permute-start.17 = (bf16[128,1024]{1,0:T(8,128)(2,1)}, bf16[128,1024]{1,0:T(8,128)(2,1)S(1)}, u32[]{:S(2)}, u32[]{:S(2)}) collective-permute-start(bf16[128,1024]{1,0:T(8,128)(2,1)} %collective-permute-done.15), channel_id=1, source_target_pairs={{0,112},{1,113},{2,114},{3,115},{4,116},{5,117},{6,118},{7,119},{8... | collective-permute-start | bytes 786440 | tf_op jit(solution)/shard_map/ppermute | solution.py:35
  181.5 11.5 %collective-permute-start.18 = (bf16[128,1024]{1,0:T(8,128)(2,1)S(1)}, bf16[128,1024]{1,0:T(8,128)(2,1)S(1)}, u32[]{:S(2)}, u32[]{:S(2)}) collective-permute-start(bf16[128,1024]{1,0:T(8,128)(2,1)S(1)} %collective-permute-done.16), channel_id=1, source_target_pairs={{0,16},{1,17},{2,18},{3,19},{4,20},{5,21},{6,22},{7,23},{8,24},{9,... | collective-permute-start | bytes 786440 | tf_op jit(solution)/shard_map/ppermute | solution.py:35
  181.5 11.6 %collective-permute-start.19 = (bf16[128,1024]{1,0:T(8,128)(2,1)S(1)}, bf16[128,1024]{1,0:T(8,128)(2,1)S(1)}, u32[]{:S(2)}, u32[]{:S(2)}) collective-permute-start(bf16[128,1024]{1,0:T(8,128)(2,1)S(1)} %collective-permute-done.17), channel_id=1, source_target_pairs={{0,112},{1,113},{2,114},{3,115},{4,116},{5,117},{6,118},{7,119},{8... | collective-permute-start | bytes 786440 | tf_op jit(solution)/shard_map/ppermute | solution.py:35
  193.0 7.5 %collective-permute-start.20 = (bf16[64,1024]{1,0:T(8,128)(2,1)S(1)}, bf16[64,1024]{1,0:T(8,128)(2,1)S(1)}, u32[]{:S(2)}, u32[]{:S(2)}) collective-permute-start(bf16[64,1024]{1,0:T(8,128)(2,1)S(1)} %slice.51), channel_id=1, source_target_pairs={{0,16},{1,17},{2,18},{3,19},{4,20},{5,21},{6,22},{7,23},{8,24},{9,... | collective-permute-start | bytes 393224 | tf_op jit(solution)/shard_map/ppermute | solution.py:35
  193.1 7.4 %collective-permute-start.21 = (bf16[64,1024]{1,0:T(8,128)(2,1)S(1)}, bf16[64,1024]{1,0:T(8,128)(2,1)S(1)}, u32[]{:S(2)}, u32[]{:S(2)}) collective-permute-start(bf16[64,1024]{1,0:T(8,128)(2,1)S(1)} %slice.52), channel_id=1, source_target_pairs={{0,112},{1,113},{2,114},{3,115},{4,116},{5,117},{6,118},{7,119},{8... | collective-permute-start | bytes 393224 | tf_op jit(solution)/shard_map/ppermute | solution.py:35
  201.3 9.3 %collective-permute-start.22 = (bf16[512,512]{1,0:T(8,128)(2,1)S(1)}, bf16[512,512]{1,0:T(8,128)(2,1)S(1)}, u32[]{:S(2)}, u32[]{:S(2)}) collective-permute-start(bf16[512,512]{1,0:T(8,128)(2,1)S(1)} %convolution_convert_fusion), channel_id=1, source_target_pairs={{0,128},{1,129},{2,130},{3,131},{4,132},{5,133},{6,134},{7,135},{8... | collective-permute-start | bytes 1572872 | tf_op jit(solution)/shard_map/ppermute | solution.py:21
  (21 other events, 170.9 us)
Sparse Core Ops, SparseCore 0:
  60.1 57.3 reduce-scatter.4
  120.0 40.6 reduce-scatter.2
  171.7 38.4 all-gather.1
